TPU v7x, 32 devices: a whole 2x2x4 slice. The times are simulated.
32 devices in a mesh: dp: 8 (over y, x, core), tensor: 4 (over z).
Axes of the slice: x: 2, y: 2, z: 4, core: 2. Of those that a mesh axis runs over, the one named last changes fastest.
Arguments:
- tokens: bfloat16 [8192, 2048], P('dp'), may hold values from -6 to 6
- cotangent: bfloat16 [8192, 2048], P('dp'), may hold values from -6 to 6
- lengths: int32 [8, 4], P('dp'), may hold values from 1 to 512, 1024 in all within a row
- counts: int32 [8, 8], replicated, may hold values from 0 to 256, as said below
- query_weight: float32 [2048, 2048], P('dp', 'tensor'), may hold values from -0.125 to 0.125
- query_moment: float32 [2048, 2048], P('dp', 'tensor'), may hold values from -0.00010681152 to 0.00010681152
- query_square: float32 [2048, 2048], P('dp', 'tensor'), may hold values from 1.2473528e-09 to 4.942341e-09
- shared_weight: float32 [2048, 256], P(('dp', 'tensor')), may hold values from -0.125 to 0.125
- shared_moment: float32 [2048, 256], P(('dp', 'tensor')), may hold values from -0.00010681152 to 0.00010681152
- shared_square: float32 [2048, 256], P(('dp', 'tensor')), may hold values from 6.119089e-10 to 9.884682e-09
- project_weight: float32 [2048, 2048], P('tensor', 'dp'), may hold values from -0.5 to 0.5
- project_moment: float32 [2048, 2048], P('tensor', 'dp'), may hold values from -0.00010681152 to 0.00010681152
- project_square: float32 [2048, 2048], P('tensor', 'dp'), may hold values from 1.2473528e-09 to 4.942341e-09
- expand_weight: float32 [2048, 8192], P('dp', 'tensor'), may hold values from -0.125 to 0.125
- expand_moment: float32 [2048, 8192], P('dp', 'tensor'), may hold values from -0.00010681152 to 0.00010681152
- expand_square: float32 [2048, 8192], P('dp', 'tensor'), may hold values from 1.2473528e-09 to 4.942341e-09
- shrink_weight: float32 [8192, 2048], P('tensor', 'dp'), may hold values from -0.0625 to 0.0625
- shrink_moment: float32 [8192, 2048], P('tensor', 'dp'), may hold values from -0.00010681152 to 0.00010681152
- shrink_square: float32 [8192, 2048], P('tensor', 'dp'), may hold values from 1.2473528e-09 to 4.942341e-09
- vectors_value: float32 [22656], replicated
- vectors_moment: float32 [22656], replicated, may hold values from -0.00048828125 to 0.00048828125
- vectors_square: float32 [22656], replicated, may hold values from 3.0595444e-08 to 1.2473528e-07
Outputs:
- block_output: bfloat16 [8192, 2048], P('dp')
- input_grad: bfloat16 [8192, 2048], P('dp')
- grad_norm: float32 [], replicated
- updated_query: float32 [2048, 2048], P('dp', 'tensor')
- moment_query: float32 [2048, 2048], P('dp', 'tensor')
- square_query: float32 [2048, 2048], P('dp', 'tensor')
- updated_shared: float32 [2048, 256], P(('dp', 'tensor'))
- moment_shared: float32 [2048, 256], P(('dp', 'tensor'))
- square_shared: float32 [2048, 256], P(('dp', 'tensor'))
- updated_project: float32 [2048, 2048], P('tensor', 'dp')
- moment_project: float32 [2048, 2048], P('tensor', 'dp')
- square_project: float32 [2048, 2048], P('tensor', 'dp')
- updated_expand: float32 [2048, 8192], P('dp', 'tensor')
- moment_expand: float32 [2048, 8192], P('dp', 'tensor')
- square_expand: float32 [2048, 8192], P('dp', 'tensor')
- updated_shrink: float32 [8192, 2048], P('tensor', 'dp')
- moment_shrink: float32 [8192, 2048], P('tensor', 'dp')
- square_shrink: float32 [8192, 2048], P('tensor', 'dp')
- updated_vectors: float32 [22656], replicated
- moment_vectors: float32 [22656], replicated
- square_vectors: float32 [22656], replicated
- clipped_vectors: float32 [22656], replicated
- token_rms: float32 [8192], P('dp')
Inputs may be any that keep to these rules, and one draw needn't show every extreme that they name: counts[s, o] tokens of device s belong to owner o; every row and every column sums to 1024; a device's tokens for owners lie in order of owners, and an owner takes sources in order. `lengths`: each row lists the sequences of one owner in order and sums to 1024.
All inputs are finite; a program needn't handle non-finite values.
Results may differ from a plain program's by a relative error of at most 0.023.
Values may be sent and summed in bfloat16 or wider, within the bound.
A program may use at most 256 MiB of HBM per device.

v0:
```python
import jax
import jax.numpy as jnp
from jax import lax
from jax.sharding import PartitionSpec as P

STEP = 10


beta_one = 0.9
beta_two = 0.95
adam_epsilon = 1e-08
decay_rate = 0.1
clip_level = 1.0
norm_epsilon = 1e-05
rate_matrix = 0.6
rate_attention = 2.4
rate_vector = 0.3
masked_score = -1e30


def mul_plain(left, right):
    return jnp.dot(left, right, preferred_element_type=jnp.float32)


def mul_right_t(left, right):
    return lax.dot_general(
        left, right, (((1,), (1,)), ((), ())), preferred_element_type=jnp.float32
    )


def mul_left_t(left, right):
    return lax.dot_general(
        left, right, (((0,), (0,)), ((), ())), preferred_element_type=jnp.float32
    )


def layer_norm(values, scaling, offset):
    average = jnp.mean(values, axis=-1, keepdims=True)
    centered = values - average
    variance = jnp.mean(centered * centered, axis=-1, keepdims=True)
    return centered * lax.rsqrt(variance + norm_epsilon) * scaling + offset


def gelu_tanh(values):
    return jax.nn.gelu(values, approximate=True)


def exclusive_sum(table, axis_index):
    return jnp.cumsum(table, axis=axis_index) - table


def segment_ids(seq_lengths, row_count):
    position = jnp.arange(row_count, dtype=jnp.int32)
    starts = jnp.cumsum(seq_lengths) - seq_lengths
    segment = jnp.sum((starts[None, :] <= position[:, None]).astype(jnp.int32), axis=1)
    return (segment, position)


def pack_slots(rows_in, starts, amounts, slots):
    offsets = jnp.arange(slots, dtype=jnp.int32)
    picked = starts[:, None] + offsets[None, :]
    valid = offsets[None, :] < amounts[:, None]
    picked = jnp.clip(picked, 0, rows_in.shape[0] - 1)
    gathered = jnp.take(rows_in, picked.reshape(-1), axis=0).reshape(
        starts.shape[0], slots, rows_in.shape[1]
    )
    return jnp.where(valid[:, :, None], gathered, jnp.zeros((), rows_in.dtype))


def unpack_slots(buffers, starts, row_count):
    position = jnp.arange(row_count, dtype=jnp.int32)
    source = jnp.sum((starts[None, :] <= position[:, None]).astype(jnp.int32), axis=1) - 1
    chosen = (source[:, None] == jnp.arange(starts.shape[0], dtype=jnp.int32)[None, :]).astype(
        jnp.int32
    )
    first_row = jnp.sum(chosen * starts[None, :], axis=1)
    flat_index = source * buffers.shape[1] + position - first_row
    return jnp.take(buffers.reshape(-1, buffers.shape[2]), flat_index, axis=0)


def masked_scores(
    query_rows, key_rows, segment_rows, position_rows, segment, position, score_scale
):
    scores = (
        jnp.einsum("bhd,kd->hbk", query_rows, key_rows, preferred_element_type=jnp.float32)
        * score_scale
    )
    allowed = (segment_rows[:, None] == segment[None, :]) & (
        position_rows[:, None] >= position[None, :]
    )
    return jnp.where(allowed[None], scores, masked_score)


def adamw_step(weight, moment, square, gradient, rate):
    moment_new = beta_one * moment + (1.0 - beta_one) * gradient
    square_new = beta_two * square + (1.0 - beta_two) * gradient * gradient
    moment_hat = moment_new / (1.0 - beta_one**STEP)
    square_hat = square_new / (1.0 - beta_two**STEP)
    weight_new = weight - rate * (
        moment_hat / (jnp.sqrt(square_hat) + adam_epsilon) + decay_rate * weight
    )
    return (weight_new, moment_new, square_new)


def local(
    tokens,
    cotangent,
    lengths,
    counts,
    query_weight,
    query_moment,
    query_square,
    shared_weight,
    shared_moment,
    shared_square,
    project_weight,
    project_moment,
    project_square,
    expand_weight,
    expand_moment,
    expand_square,
    shrink_weight,
    shrink_moment,
    shrink_square,
    vectors_value,
    vectors_moment,
    vectors_square,
):
    device = lax.axis_index("dp")
    devices_dp = lax.axis_size("dp")
    tensor_part = lax.axis_index("tensor")
    tensor_count = lax.axis_size("tensor")
    row_count, width = tokens.shape
    slots = 2 * row_count // devices_dp
    send_start = lax.dynamic_index_in_dim(exclusive_sum(counts, 1), device, 0, keepdims=False)
    send_amount = lax.dynamic_index_in_dim(counts, device, 0, keepdims=False)
    recv_start = lax.dynamic_index_in_dim(exclusive_sum(counts, 0), device, 1, keepdims=False)
    recv_amount = lax.dynamic_index_in_dim(counts, device, 1, keepdims=False)
    arrived_rows, arrived_grad = (
        lax.all_to_all(
            pack_slots(tokens, send_start, send_amount, slots),
            "dp",
            split_axis=0,
            concat_axis=0,
            tiled=True,
        ),
        lax.all_to_all(
            pack_slots(cotangent, send_start, send_amount, slots),
            "dp",
            split_axis=0,
            concat_axis=0,
            tiled=True,
        ),
    )
    owned_rows = unpack_slots(arrived_rows, recv_start, row_count)
    owned_grad = unpack_slots(arrived_grad, recv_start, row_count)
    query_cols, expand_cols = (
        lax.all_gather(query_weight.astype(jnp.bfloat16), "dp", axis=0, tiled=True),
        lax.all_gather(expand_weight.astype(jnp.bfloat16), "dp", axis=0, tiled=True),
    )
    project_rows, shrink_rows = (
        lax.all_gather(project_weight.astype(jnp.bfloat16), "dp", axis=1, tiled=True),
        lax.all_gather(shrink_weight.astype(jnp.bfloat16), "dp", axis=1, tiled=True),
    )
    shared_cols = lax.all_gather(
        shared_weight.astype(jnp.bfloat16), ("dp", "tensor"), axis=0, tiled=True
    )
    head_width = query_cols.shape[1]
    hidden_width = expand_cols.shape[1]
    head_size = shared_cols.shape[1] // 2
    heads_here = head_width // head_size
    hidden_total = hidden_width * tensor_count
    gain_one = vectors_value[0:width]
    shift_one = vectors_value[width : 2 * width]
    gain_two = vectors_value[2 * width : 3 * width]
    shift_two = vectors_value[3 * width : 4 * width]
    query_bias = lax.dynamic_slice_in_dim(
        vectors_value, 4 * width + tensor_part * head_width, head_width, 0
    )
    project_bias = vectors_value[5 * width : 6 * width]
    shrink_bias = vectors_value[6 * width : 7 * width]
    expand_bias = lax.dynamic_slice_in_dim(
        vectors_value, 7 * width + tensor_part * hidden_width, hidden_width, 0
    )
    value_bias = vectors_value[7 * width + hidden_total : 7 * width + hidden_total + head_size]
    inputs_float = owned_rows.astype(jnp.float32)
    output_float = owned_grad.astype(jnp.float32)
    normed_one, norm_one_back = jax.vjp(layer_norm, inputs_float, gain_one, shift_one)
    normed_low = normed_one.astype(jnp.bfloat16)
    queries = (mul_plain(normed_low, query_cols) + query_bias).astype(jnp.bfloat16)
    shared_out = mul_plain(normed_low, shared_cols) + jnp.concatenate(
        [jnp.zeros((head_size,), jnp.float32), value_bias]
    )
    key_rows = shared_out[:, :head_size].astype(jnp.bfloat16)
    value_rows = shared_out[:, head_size:].astype(jnp.bfloat16)
    query_heads = queries.reshape(row_count, heads_here, head_size)
    segment, position = segment_ids(lengths[0], row_count)
    block_rows = min(512, row_count)
    block_count = row_count // block_rows
    score_scale = head_size ** (-0.5)
    attended = []
    log_totals = []
    for block_index in range(block_count):
        lower = block_index * block_rows
        upper = lower + block_rows
        scores = masked_scores(
            query_heads[lower:upper],
            key_rows,
            segment[lower:upper],
            position[lower:upper],
            segment,
            position,
            score_scale,
        )
        row_max = jnp.max(scores, axis=-1, keepdims=True)
        expo = jnp.exp(scores - row_max)
        row_total = jnp.sum(expo, axis=-1, keepdims=True)
        probs = expo / row_total
        attended.append(
            jnp.einsum(
                "hbk,kd->bhd",
                probs.astype(jnp.bfloat16),
                value_rows,
                preferred_element_type=jnp.float32,
            )
        )
        log_totals.append(row_max + jnp.log(row_total))
    heads_out = (
        jnp.concatenate(attended, axis=0).reshape(row_count, head_width).astype(jnp.bfloat16)
    )
    attn_branch = lax.psum(mul_plain(heads_out, project_rows), "tensor") + project_bias
    hidden_one = inputs_float + attn_branch
    normed_two, norm_two_back = jax.vjp(layer_norm, hidden_one, gain_two, shift_two)
    normed_two_low = normed_two.astype(jnp.bfloat16)
    expand_pre = mul_plain(normed_two_low, expand_cols) + expand_bias
    activated, gelu_back = jax.vjp(gelu_tanh, expand_pre)
    activated_low = activated.astype(jnp.bfloat16)
    ffn_partial = mul_plain(activated_low, shrink_rows)
    shrink_grad = mul_left_t(activated_low, owned_grad)
    shrink_bias_grad = jnp.sum(output_float, axis=0)
    activated_grad = mul_right_t(owned_grad, shrink_rows)
    expand_pre_grad = gelu_back(activated_grad)[0].astype(jnp.bfloat16)
    expand_grad = mul_left_t(normed_two_low, expand_pre_grad)
    expand_bias_grad = jnp.sum(expand_pre_grad.astype(jnp.float32), axis=0)
    normed_two_part = mul_right_t(expand_pre_grad, expand_cols)
    ffn_branch = (
        lax.psum(ffn_partial.astype(jnp.bfloat16), "tensor").astype(jnp.float32) + shrink_bias
    )
    layer_result = (hidden_one + ffn_branch).astype(jnp.bfloat16)
    normed_two_grad = lax.psum(normed_two_part, "tensor")
    hidden_from_norm, gain_two_grad, shift_two_grad = norm_two_back(normed_two_grad)
    hidden_grad = output_float + hidden_from_norm
    branch_grad = hidden_grad.astype(jnp.bfloat16)
    project_bias_grad = jnp.sum(branch_grad.astype(jnp.float32), axis=0)
    project_grad = mul_left_t(heads_out, branch_grad)
    heads_grad = (
        mul_right_t(branch_grad, project_rows)
        .astype(jnp.bfloat16)
        .reshape(row_count, heads_here, head_size)
    )
    key_grad = jnp.zeros((row_count, head_size), jnp.float32)
    value_grad = jnp.zeros((row_count, head_size), jnp.float32)
    query_grads = []
    for block_index in range(block_count):
        lower = block_index * block_rows
        upper = lower + block_rows
        query_block = query_heads[lower:upper]
        grad_block = heads_grad[lower:upper]
        scores = masked_scores(
            query_block,
            key_rows,
            segment[lower:upper],
            position[lower:upper],
            segment,
            position,
            score_scale,
        )
        probs = jnp.exp(scores - log_totals[block_index])
        prob_grad = jnp.einsum(
            "bhd,kd->hbk", grad_block, value_rows, preferred_element_type=jnp.float32
        )
        score_grad = (
            probs * (prob_grad - jnp.sum(probs * prob_grad, axis=-1, keepdims=True))
        ).astype(jnp.bfloat16)
        query_grads.append(
            jnp.einsum("hbk,kd->bhd", score_grad, key_rows, preferred_element_type=jnp.float32)
            * score_scale
        )
        key_grad = (
            key_grad
            + jnp.einsum("hbk,bhd->kd", score_grad, query_block, preferred_element_type=jnp.float32)
            * score_scale
        )
        value_grad = value_grad + jnp.einsum(
            "hbk,bhd->kd",
            probs.astype(jnp.bfloat16),
            grad_block,
            preferred_element_type=jnp.float32,
        )
    query_grad = (
        jnp.concatenate(query_grads, axis=0).reshape(row_count, head_width).astype(jnp.bfloat16)
    )
    query_bias_grad = jnp.sum(query_grad.astype(jnp.float32), axis=0)
    query_weight_grad = mul_left_t(normed_low, query_grad)
    normed_one_local = mul_right_t(query_grad, query_cols)
    kv_local = jnp.concatenate([key_grad, value_grad], axis=1)
    normed_one_part, shared_sum = lax.psum((normed_one_local, kv_local), "tensor")
    shared_grad = shared_sum.astype(jnp.bfloat16)
    normed_one_grad = normed_one_part + mul_right_t(shared_grad, shared_cols)
    inputs_from_norm, gain_one_grad, shift_one_grad = norm_one_back(normed_one_grad)
    input_result = (hidden_grad + inputs_from_norm).astype(jnp.bfloat16)
    norm_scale = (tensor_part == 0).astype(jnp.float32)
    shared_weight_grad = mul_left_t(normed_low, shared_grad)
    value_bias_grad = jnp.sum(shared_grad[:, head_size:].astype(jnp.float32), axis=0)
    back_rows, back_grad = (
        lax.all_to_all(
            pack_slots(layer_result, recv_start, recv_amount, slots),
            "dp",
            split_axis=0,
            concat_axis=0,
            tiled=True,
        ),
        lax.all_to_all(
            pack_slots(input_result, recv_start, recv_amount, slots),
            "dp",
            split_axis=0,
            concat_axis=0,
            tiled=True,
        ),
    )
    output_rows = unpack_slots(back_rows, send_start, row_count)
    grad_rows = unpack_slots(back_grad, send_start, row_count)
    output_back = output_rows.astype(jnp.float32)
    token_rms = jnp.sqrt(jnp.mean(output_back * output_back, axis=1))
    query_part, expand_part, shared_part = (
        lax.psum_scatter(
            query_weight_grad.astype(jnp.bfloat16), "dp", scatter_dimension=0, tiled=True
        ).astype(jnp.float32),
        lax.psum_scatter(
            expand_grad.astype(jnp.bfloat16), "dp", scatter_dimension=0, tiled=True
        ).astype(jnp.float32),
        lax.psum_scatter(
            shared_weight_grad.astype(jnp.bfloat16), "dp", scatter_dimension=0, tiled=True
        ).astype(jnp.float32),
    )
    project_part, shrink_part = (
        lax.psum_scatter(
            project_grad.astype(jnp.bfloat16), "dp", scatter_dimension=1, tiled=True
        ).astype(jnp.float32),
        lax.psum_scatter(
            shrink_grad.astype(jnp.bfloat16), "dp", scatter_dimension=1, tiled=True
        ).astype(jnp.float32),
    )
    piece_rows = shared_part.shape[0] // tensor_count
    shared_piece = lax.dynamic_slice_in_dim(shared_part, tensor_part * piece_rows, piece_rows, 0)
    leading = (tensor_part == 0).astype(jnp.float32)
    norm_part = (
        jnp.concatenate(
            [
                gain_one_grad,
                shift_one_grad,
                gain_two_grad,
                shift_two_grad,
                jnp.zeros((width,), jnp.float32),
                project_bias_grad,
            ]
        )
        * norm_scale
    )
    lead_part = (
        jnp.concatenate(
            [shrink_bias_grad, jnp.zeros((hidden_total,), jnp.float32), value_bias_grad]
        )
        * leading
    )
    split_part = jnp.zeros_like(vectors_value)
    split_part = lax.dynamic_update_slice_in_dim(
        split_part, query_bias_grad, 4 * width + tensor_part * head_width, 0
    )
    split_part = lax.dynamic_update_slice_in_dim(
        split_part, expand_bias_grad, 7 * width + tensor_part * hidden_width, 0
    )
    vector_part = jnp.concatenate([norm_part, lead_part]) + split_part
    local_squares = (
        jnp.sum(query_part * query_part)
        + jnp.sum(expand_part * expand_part)
        + jnp.sum(shared_piece * shared_piece)
        + jnp.sum(project_part * project_part)
        + jnp.sum(shrink_part * shrink_part)
    )
    vector_grad, weight_squares = lax.psum((vector_part, local_squares), ("dp", "tensor"))
    grad_size = jnp.sqrt(weight_squares + jnp.sum(vector_grad * vector_grad))
    clip_factor = jnp.minimum(1.0, clip_level / (grad_size + 1e-06))
    clipped_vectors = clip_factor * vector_grad
    query_new = adamw_step(
        query_weight,
        query_moment,
        query_square,
        clip_factor * query_part,
        rate_matrix * width ** (-0.5),
    )
    shared_new = adamw_step(
        shared_weight,
        shared_moment,
        shared_square,
        clip_factor * shared_piece,
        rate_attention * width ** (-0.5),
    )
    project_new = adamw_step(
        project_weight,
        project_moment,
        project_square,
        clip_factor * project_part,
        rate_attention * width ** (-0.5),
    )
    expand_new = adamw_step(
        expand_weight,
        expand_moment,
        expand_square,
        clip_factor * expand_part,
        rate_matrix * width ** (-0.5),
    )
    shrink_new = adamw_step(
        shrink_weight,
        shrink_moment,
        shrink_square,
        clip_factor * shrink_part,
        rate_matrix * hidden_total ** (-0.5),
    )
    vectors_new = adamw_step(
        vectors_value, vectors_moment, vectors_square, clipped_vectors, rate_vector
    )
    return (
        output_rows,
        grad_rows,
        grad_size,
        query_new[0],
        query_new[1],
        query_new[2],
        shared_new[0],
        shared_new[1],
        shared_new[2],
        project_new[0],
        project_new[1],
        project_new[2],
        expand_new[0],
        expand_new[1],
        expand_new[2],
        shrink_new[0],
        shrink_new[1],
        shrink_new[2],
        vectors_new[0],
        vectors_new[1],
        vectors_new[2],
        clipped_vectors,
        token_rms,
    )


def solution(mesh):
    placed = (
        P("dp", None),
        P("dp", None),
        P("dp", None),
        P(),
        P("dp", "tensor"),
        P("dp", "tensor"),
        P("dp", "tensor"),
        P(("dp", "tensor"), None),
        P(("dp", "tensor"), None),
        P(("dp", "tensor"), None),
        P("tensor", "dp"),
        P("tensor", "dp"),
        P("tensor", "dp"),
        P("dp", "tensor"),
        P("dp", "tensor"),
        P("dp", "tensor"),
        P("tensor", "dp"),
        P("tensor", "dp"),
        P("tensor", "dp"),
        P(),
        P(),
        P(),
    )
    return jax.shard_map(
        local,
        mesh=mesh,
        in_specs=placed,
        out_specs=(
            P("dp", None),
            P("dp", None),
            P(),
            P("dp", "tensor"),
            P("dp", "tensor"),
            P("dp", "tensor"),
            P(("dp", "tensor"), None),
            P(("dp", "tensor"), None),
            P(("dp", "tensor"), None),
            P("tensor", "dp"),
            P("tensor", "dp"),
            P("tensor", "dp"),
            P("dp", "tensor"),
            P("dp", "tensor"),
            P("dp", "tensor"),
            P("tensor", "dp"),
            P("tensor", "dp"),
            P("tensor", "dp"),
            P(),
            P(),
            P(),
            P(),
            P("dp"),
        ),
        check_vma=False,
    )
```

profile of v0, /device:TPU:0, one launch (start us, length us, event | category | flops | bytes accessed | tf_op | source)
XLA Modules:
  0.0 2030.7 jit_solution(15083424093176470792)
XLA Ops:
  12.7 19.1 gather_fusion.4
  31.7 19.0 gather_fusion
  50.8 7.1 broadcast_select_fusion.2
  57.9 6.2 broadcast_select_fusion.4
  64.1 5.3 all-to-all-start
  74.1 92.9 %all-to-all-done = bf16[8,256,2048]{2,1,0:T(8,128)(2,1)} async-done(((bf16[8,256,2048]{2,1,0:T(8,128)(2,1)}), bf16[8,256,2048]{2,1,0:T(8,128)(2,1)}, u32[]{:S(2)}, u32[]{:S(2)}) %all-to-all-start) | async-done | bytes 8388640 | tf_op jit(solution)/shard_map/all_to_all | solution.py:140
  167.0 13.3 gather_fusion.1
  191.1 5.2 add_convert_fusion.3
  211.0 7.6 fusion.111
  222.8 99.8 %all_to_all.20 = bf16[8,256,2048]{2,1,0:T(8,128)(2,1)} all-to-all(bf16[8,256,2048]{2,1,0:T(8,128)(2,1)} %get-tuple-element.84), channel_id=1, replica_groups=mesh['dp'=8,'tensor'=4] {'dp'}, dimensions={0} | all-to-all | bytes 16777216 | tf_op jit(solution)/shard_map/all_to_all | solution.py:147
  322.6 13.3 gather_fusion.5
  335.9 174.5 %all-reduce.8.cloned.1.call-done = f32[1024,2048]{1,0:T(8,128)} async-done(((f32[1024,2048]{1,0:T(8,128)}), f32[1024,2048]{1,0:T(8,128)}) %all-reduce.8.cloned.1.call-update) | async-done | bytes 8388624 | tf_op jit(solution)/shard_map/psum | solution.py:231
  510.3 5.7 fusion.103
  520.4 45.6 %all-gather.12.cloned.1.call-done = bf16[2048,2048]{1,0:T(8,128)(2,1)} async-done(((bf16[256,2048]{1,0:T(8,128)(2,1)}), bf16[2048,2048]{1,0:T(8,128)(2,1)}) %all-gather.12.cloned.1.call-update) | async-done | bytes 8388624 | tf_op jit(solution)/shard_map/all_gather | solution.py:159
  566.1 15.8 fusion.87
  581.8 42.5 %all-gather.14.cloned.1.call-done = bf16[2048,2048]{1,0:T(8,128)(2,1)} async-done(((bf16[2048,256]{1,0:T(8,128)(2,1)}), bf16[2048,2048]{1,0:T(8,128)(2,1)}) %all-gather.14.cloned.1.call-update) | async-done | bytes 8388624 | tf_op jit(solution)/shard_map/all_gather | solution.py:163
  624.4 20.8 %convert_reduce_fusion.2 = (f32[2048]{0:T(1024)}, bf16[1024,2048]{1,0:T(8,128)(2,1)S(1)}) fusion(f32[1024,2048]{1,0:T(8,128)} %fusion.87, f32[2048]{0:T(1024)S(1)} %get-tuple-element.68, bf16[2048,2048]{1,0:T(8,128)(2,1)} %all-gather.14.cloned.1.call-done, bf16[1024,2048]{1,0:T(8,128)(2,1)} %gather_fusion.5, pred[1024]{0:T(1024)(128)(4,1)S(1)} %compare_and_fusion.3), kind=kOutput, calls=%fused_computation.48 | convolution fusion | flops 8640264192 | bytes 25183232 | tf_op jit(solution)/shard_map/dot_general | solution.py:26
  647.1 13.2 fusion.112
  660.5 16.0 convolution_convert_fusion.2
  676.6 274.8 %all-reduce.12.cloned.1.call-done = f32[1024,2048]{1,0:T(8,128)} async-done(((f32[1024,2048]{1,0:T(8,128)}), f32[1024,2048]{1,0:T(8,128)}) %all-reduce.12.cloned.1.call-update) | async-done | bytes 8388624 | tf_op jit(solution)/shard_map/psum | solution.py:250
  951.4 8.3 multiply_reduce_fusion.1
  959.7 148.1 %all-reduce.10.cloned.1.call-done = bf16[1024,2048]{1,0:T(8,128)(2,1)} async-done(((bf16[1024,2048]{1,0:T(8,128)(2,1)}), bf16[1024,2048]{1,0:T(8,128)(2,1)}) %all-reduce.10.cloned.1.call-update) | async-done | bytes 4194320 | tf_op jit(solution)/shard_map/psum | solution.py:247
  1107.8 10.9 fusion.102
  1141.1 5.6 fusion.113
  1150.5 4.4 fusion.61
  1154.9 5.1 fusion.52
  1161.8 75.0 %all-reduce.17 = bf16[1024,256]{0,1:T(8,128)(2,1)S(1)} all-reduce(f32[1024,256]{0,1:T(8,128)S(1)} %pad_maximum_fusion.1), channel_id=1, replica_groups=mesh['dp'=8,'tensor'=4] {'tensor'}, use_global_device_ids=true, to_apply=%region_24.27 | all-reduce | flops 262144 | bytes 1572864 | tf_op jit(solution)/shard_map/psum | solution.py:307
  1236.8 4.5 convolution_convert_fusion.5
  1241.4 5.9 convolution_convert_fusion.3
  1247.6 5.9 convolution_convert_fusion.4
  1253.6 15.3 convolution_convert_fusion.1
  1269.7 16.4 convolution_convert_fusion
  1286.2 19.2 gather_fusion.2
  1305.4 164.8 %all-reduce.14.cloned.1.call-done = f32[1024,2048]{1,0:T(8,128)} async-done(((f32[1024,2048]{1,0:T(8,128)}), f32[1024,2048]{1,0:T(8,128)}) %all-reduce.14.cloned.1.call-update) | async-done | bytes 8388624 | tf_op jit(solution)/shard_map/psum | solution.py:307
  1470.2 8.2 fusion.89
  1478.4 4.4 fusion.8
  1482.8 8.7 add_convert_fusion
  1491.5 19.2 gather_fusion.6
  1510.7 7.1 broadcast_select_fusion
  1521.8 114.3 %all_to_all.21 = bf16[8,256,2048]{2,1,0:T(8,128)(2,1)} all-to-all(bf16[8,256,2048]{2,1,0:T(8,128)(2,1)S(1)} %get-tuple-element.80), channel_id=1, replica_groups=mesh['dp'=8,'tensor'=4] {'dp'}, dimensions={0} | all-to-all | bytes 16777216 | tf_op jit(solution)/shard_map/all_to_all | solution.py:323
  1636.2 5.2 all-to-all-start.1
  1647.6 118.6 %reduce-scatter.8.cloned.1.call-done = bf16[256,2048]{1,0:T(8,128)(2,1)} async-done(((bf16[2048,2048]{1,0:T(8,128)(2,1)}), bf16[256,2048]{1,0:T(8,128)(2,1)}) %reduce-scatter.8.cloned.1.call-update) | async-done | bytes 1048592 | tf_op jit(solution)/shard_map/reduce_scatter | solution.py:339
  1771.2 68.8 %reduce-scatter.14.cloned.1.call-done = bf16[2048,256]{1,0:T(8,128)(2,1)} async-done(((bf16[2048,2048]{1,0:T(8,128)(2,1)}), bf16[2048,256]{1,0:T(8,128)(2,1)}) %reduce-scatter.14.cloned.1.call-update) | async-done | bytes 1048592 | tf_op jit(solution)/shard_map/reduce_scatter | solution.py:350
  1844.6 39.4 %psum.54 = f32[]{:T(128)} all-reduce(f32[]{:T(128)S(6)} %add.403), channel_id=1, replica_groups=mesh['dp'=8,'tensor'=4] {'dp','tensor'}, use_global_device_ids=true, to_apply=%region_37.40 | all-reduce | flops 1 | bytes 8 | tf_op jit(solution)/shard_map/psum | solution.py:391
  1884.0 83.5 %all-reduce.16.cloned.1.call-done = f32[22656]{0:T(1024)} async-done(((f32[22656]{0:T(1024)}), f32[22656]{0:T(1024)}) %all-reduce.16.cloned.1.call-update) | async-done | bytes 90640 | tf_op jit(solution)/shard_map/psum | solution.py:391
  1987.8 13.3 gather_fusion.7
  2001.0 13.3 gather_fusion.3
  2014.3 4.8 broadcast_select_fusion.8
  (281 shorter events, 113.6 us)
Async XLA Ops:
  7.2 183.8 %all-gather.8.cloned.1.call-start = ((), (), s32[]{:S(2)}) async-start(), calls=%async_computation.10 | async-start | bytes 2359296 | tf_op jit(solution)/shard_map/all_gather | solution.py:158
  64.1 7.3 slice-start.6
  64.1 7.3 copy-start.39
  64.1 102.9 %all-to-all-start = ((bf16[8,256,2048]{2,1,0:T(8,128)(2,1)}), bf16[8,256,2048]{2,1,0:T(8,128)(2,1)}, u32[]{:S(2)}, u32[]{:S(2)}) async-start(bf16[8,256,2048]{2,1,0:T(8,128)(2,1)} %get-tuple-element.85), calls=%async_computation | async-start | bytes 16777216 | tf_op jit(solution)/shard_map/all_to_all | solution.py:140
  69.5 127.0 %all-gather.6.cloned.1.call-start = ((), (), s32[]{:S(2)}) async-start(), calls=%async_computation.9 | async-start | bytes 1081344 | tf_op jit(solution)/shard_map/all_gather | solution.py:165
  70.2 139.8 %all-gather.10.cloned.1.call-start = ((), (), s32[]{:S(2)}) async-start(), calls=%async_computation.11 | async-start | bytes 2359296 | tf_op jit(solution)/shard_map/all_gather | solution.py:162
  71.0 439.3 %all-reduce.8.cloned.1.call-start = ((), (), s32[]{:S(2)}) async-start(), calls=%async_computation.12 | async-start | bytes 16777216 | tf_op jit(solution)/shard_map/psum | solution.py:231
  73.2 114.0 %copy-start.34 = (f32[2048]{0:T(1024)}, f32[2048]{0:T(1024)S(1)}, u32[]{:S(2)}) copy-start(f32[2048]{0:T(1024)S(1)} %get-tuple-element.73) | copy-start | bytes 24580
  183.7 7.4 copy-start.36
  187.2 9.1 copy-start.42
  187.2 9.1 copy-start.40
  218.6 347.5 %all-gather.12.cloned.1.call-start = ((), (), s32[]{:S(2)}) async-start(), calls=%async_computation.13 | async-start | bytes 9437184 | tf_op jit(solution)/shard_map/all_gather | solution.py:159
  221.6 402.8 %all-gather.14.cloned.1.call-start = ((), (), s32[]{:S(2)}) async-start(), calls=%async_computation.14 | async-start | bytes 9437184 | tf_op jit(solution)/shard_map/all_gather | solution.py:163
  222.7 728.7 %all-reduce.12.cloned.1.call-start = ((), (), s32[]{:S(2)}) async-start(), calls=%async_computation.16 | async-start | bytes 16777216 | tf_op jit(solution)/shard_map/psum | solution.py:250
  660.4 447.4 %all-reduce.10.cloned.1.call-start = ((), (), s32[]{:S(2)}) async-start(), calls=%async_computation.15 | async-start | bytes 8388608 | tf_op jit(solution)/shard_map/psum | solution.py:247
  676.5 793.7 %all-reduce.14.cloned.1.call-start = ((), (), s32[]{:S(2)}) async-start(), calls=%async_computation.17 | async-start | bytes 16777216 | tf_op jit(solution)/shard_map/psum | solution.py:307
  676.6 431.2 %copy-start.44 = (f32[2048]{0:T(1024)S(1)}, f32[2048]{0:T(1024)}, u32[]{:S(2)}) copy-start(f32[2048]{0:T(1024)} %get-tuple-element.67) | copy-start | bytes 24580
  1107.8 10.9 copy-start.7
  1118.7 7.4 slice-start
  1146.7 496.1 %reduce-scatter.10.cloned.1.call-start = ((), (), s32[]{:S(2)}) async-start(), calls=%async_computation.20 | async-start | bytes 1179648 | tf_op jit(solution)/shard_map/reduce_scatter | solution.py:342
  1150.5 9.5 slice-start.2
  1161.7 79.7 %copy-start.29 = (bf16[1024,4,128]{0,2,1:T(8,128)(2,1)S(1)}, bf16[1024,4,128]{0,2,1:T(8,128)(2,1)}, u32[]{:S(2)}) copy-start(bf16[1024,4,128]{0,2,1:T(8,128)(2,1)} %copy-done.28) | copy-start | bytes 3145732
  1241.3 402.9 %reduce-scatter.12.cloned.1.call-start = ((), (), s32[]{:S(2)}) async-start(), calls=%async_computation.21 | async-start | bytes 2359296 | tf_op jit(solution)/shard_map/reduce_scatter | solution.py:347
  1247.3 398.6 %reduce-scatter.6.cloned.1.call-start = ((), (), s32[]{:S(2)}) async-start(), calls=%async_computation.18 | async-start | bytes 2359296 | tf_op jit(solution)/shard_map/reduce_scatter | solution.py:336
  1253.5 512.7 %reduce-scatter.8.cloned.1.call-start = ((), (), s32[]{:S(2)}) async-start(), calls=%async_computation.19 | async-start | bytes 9437184 | tf_op jit(solution)/shard_map/reduce_scatter | solution.py:339
  1268.9 571.1 %reduce-scatter.14.cloned.1.call-start = ((), (), s32[]{:S(2)}) async-start(), calls=%async_computation.22 | async-start | bytes 9437184 | tf_op jit(solution)/shard_map/reduce_scatter | solution.py:350
  1286.2 184.0 %copy-start.35 = (f32[2048]{0:T(1024)S(1)}, f32[2048]{0:T(1024)}, u32[]{:S(2)}) copy-start(f32[2048]{0:T(1024)} %copy-done.34) | copy-start | bytes 24580
  1286.2 184.0 %copy-start.37 = (f32[1024]{0:T(1024)S(1)}, f32[1024]{0:T(1024)}, u32[]{:S(2)}) copy-start(f32[1024]{0:T(1024)} %copy-done.36) | copy-start | bytes 12292
  1286.2 184.0 %copy-start.57 = (bf16[2048,256]{1,0:T(8,128)(2,1)S(1)}, bf16[2048,256]{1,0:T(8,128)(2,1)}, u32[]{:S(2)}) copy-start(bf16[2048,256]{1,0:T(8,128)(2,1)} %all-gather.6.cloned.1.call-done) | copy-start | bytes 3145732
  1305.4 173.0 %copy-start.43 = (f32[1024]{0:T(1024)S(1)}, f32[1024]{0:T(1024)}, u32[]{:S(2)}) copy-start(f32[1024]{0:T(1024)} %copy-done.42) | copy-start | bytes 12292
  1305.4 173.0 %copy-start.41 = (f32[1024]{0:T(1024)S(1)}, f32[1024]{0:T(1024)}, u32[]{:S(2)}) copy-start(f32[1024]{0:T(1024)} %copy-done.40) | copy-start | bytes 12292
  1470.2 8.2 copy-start.3
  1636.2 207.0 %copy-start.46 = (f32[2048]{0:T(1024)S(1)}, f32[2048]{0:T(1024)}, u32[]{:S(2)}) copy-start(f32[2048]{0:T(1024)} %get-tuple-element.25) | copy-start | bytes 24580
  1636.2 207.0 %copy-start.45 = (f32[2048]{0:T(1024)S(1)}, f32[2048]{0:T(1024)}, u32[]{:S(2)}) copy-start(f32[2048]{0:T(1024)} %get-tuple-element.29) | copy-start | bytes 24580
  1636.2 207.0 %copy-start.47 = (f32[2048]{0:T(1024)S(1)}, f32[2048]{0:T(1024)}, u32[]{:S(2)}) copy-start(f32[2048]{0:T(1024)} %get-tuple-element.54) | copy-start | bytes 24580
  1636.2 334.2 %copy-start.31 = (f32[64,256]{1,0:T(8,128)S(1)}, f32[64,256]{1,0:T(8,128)}, u32[]{:S(2)}) copy-start(f32[64,256]{1,0:T(8,128)} %param.33) | copy-start | bytes 196612
  1636.2 364.8 %all-to-all-start.1 = ((bf16[8,256,2048]{2,1,0:T(8,128)(2,1)}), bf16[8,256,2048]{2,1,0:T(8,128)(2,1)}, u32[]{:S(2)}, u32[]{:S(2)}) async-start(bf16[8,256,2048]{2,1,0:T(8,128)(2,1)} %get-tuple-element.81), calls=%async_computation.1 | async-start | bytes 16777216 | tf_op jit(solution)/shard_map/all_to_all | solution.py:316
  1641.4 336.7 %copy-start.33 = (f32[22656]{0:T(1024)S(1)}, f32[22656]{0:T(1024)}, u32[]{:S(2)}) copy-start(f32[22656]{0:T(1024)} %param.45) | copy-start | bytes 271876
  1641.4 336.7 %copy-start.38 = (f32[22656]{0:T(1024)S(1)}, f32[22656]{0:T(1024)}, u32[]{:S(2)}) copy-start(f32[22656]{0:T(1024)} %param.46) | copy-start | bytes 271876
  1641.5 338.6 %copy-start.12 = (f32[2048,256]{1,0:T(8,128)S(1)}, f32[2048,256]{1,0:T(8,128)}, u32[]{:S(2)}) copy-start(f32[2048,256]{1,0:T(8,128)} %param.42) | copy-start | bytes 6291460
  1641.5 326.1 %all-reduce.16.cloned.1.call-start = ((), (), s32[]{:S(2)}) async-start(), calls=%async_computation.23 | async-start | bytes 188416 | tf_op jit(solution)/shard_map/psum | solution.py:391
  1840.0 140.0 %copy-start.18 = (bf16[2048,256]{1,0:T(8,128)(2,1)S(1)}, bf16[2048,256]{1,0:T(8,128)(2,1)}, u32[]{:S(2)}) copy-start(bf16[2048,256]{1,0:T(8,128)(2,1)} %reduce-scatter.14.cloned.1.call-done) | copy-start | bytes 3145732
  1970.5 9.6 copy-start.22
  1970.5 9.6 copy-start.23
  1975.1 8.8 copy-start.13
  1975.1 8.8 copy-start.17
  1975.1 8.8 copy-start.24
  1975.1 8.8 copy-start.25
  (36 other events, 145.7 us)
Sparse Core Ops, SparseCore 0:
  10.5 30.5 all-gather.7
  73.8 73.8 all-gather.5
  150.2 34.9 all-gather.9
  218.7 291.5 all-reduce.7
  512.7 53.3 all-gather.11
  568.4 55.9 all-gather.13
  660.5 290.8 all-reduce.11
  953.7 153.9 all-reduce.9
  1146.9 323.2 all-reduce.13
  1474.1 35.0 reduce-scatter.9
  1513.4 58.4 reduce-scatter.11
  1575.6 58.4 reduce-scatter.5
  1638.0 128.1 reduce-scatter.7
  1769.6 70.4 reduce-scatter.13
  1847.0 120.5 all-reduce.15
where the time goes:
time: 2040 us; the launch traced here: 2030 us
  waiting for transfers between devices  1210 us (59%)
  blocking collectives  329 us (16%)
  matrix products  173 us (8%)
  local copies, waits for them, and re-layouts  147 us (7%)
  other arithmetic  135 us (7%)
  between operations  21 us (1%)
    psum x1, waiting for transfers between devices, local(): normed_two_grad = lax.psum(normed_two_part, 'tensor')  275 us
    psum x1, waiting for transfers between devices, local(): lax.psum(mul_plain(heads_out, project_rows), 'tensor') + project_bias  174 us
    psum x1, waiting for transfers between devices, local(): lax.psum((normed_one_local, kv_local), 'tensor')  165 us
    psum x1, waiting for transfers between devices, local(): lax.psum(ffn_partial.astype(jnp.bfloat16), 'tensor').astype(jnp.float32)  148 us
    reduce_scatter x1, waiting for transfers between devices, local(): lax.psum_scatter(expand_grad.astype(jnp.bfloat16), 'dp', scatter_dimensio...  119 us
    all_to_all x1, blocking collectives, local(): lax.all_to_all(pack_slots(input_result, recv_start, recv_amount, slots),...  114 us
    all_to_all x1, blocking collectives, local(): lax.all_to_all(pack_slots(cotangent, send_start, send_amount, slots), 'dp...  99.8 us
    all_to_all x1, waiting for transfers between devices, local(): lax.all_to_all(pack_slots(tokens, send_start, send_amount, slots), 'dp',...  92.9 us
  transfers between devices with their start and end apart: 17, of which 10 were waited for; matrix products, arithmetic and copies ran while one was open for 17% of the time, Pallas kernels for 0%

commit v1 on v0

v1 whole, which is shorter than its diff:
```python
import functools

import jax
import jax.numpy as jnp
from jax import lax
from jax.experimental import pallas as pl
from jax.experimental.pallas import tpu as pltpu
from jax.sharding import PartitionSpec as P

STEP = 10


beta_one = 0.9
beta_two = 0.95
adam_epsilon = 1e-08
decay_rate = 0.1
clip_level = 1.0
norm_epsilon = 1e-05
rate_matrix = 0.6
rate_attention = 2.4
rate_vector = 0.3
masked_score = -1e30

MESH = pl.DeviceIdType.MESH
IN_PLACE = pl.BlockSpec(memory_space=pl.ANY)
IN_VMEM = pl.BlockSpec(memory_space=pltpu.VMEM)
DMA = pltpu.SemaphoreType.DMA
MIB = 2**20


def mul_plain(left, right):
    return jnp.dot(left, right, preferred_element_type=jnp.float32)


def mul_right_t(left, right):
    return lax.dot_general(
        left, right, (((1,), (1,)), ((), ())), preferred_element_type=jnp.float32
    )


def mul_left_t(left, right):
    return lax.dot_general(
        left, right, (((0,), (0,)), ((), ())), preferred_element_type=jnp.float32
    )


def layer_norm(values, scaling, offset):
    average = jnp.mean(values, axis=-1, keepdims=True)
    centered = values - average
    variance = jnp.mean(centered * centered, axis=-1, keepdims=True)
    return centered * lax.rsqrt(variance + norm_epsilon) * scaling + offset


def gelu_tanh(values):
    return jax.nn.gelu(values, approximate=True)


def exclusive_sum(table, axis_index):
    return jnp.cumsum(table, axis=axis_index) - table


def segment_ids(seq_lengths, row_count):
    position = jnp.arange(row_count, dtype=jnp.int32)
    starts = jnp.cumsum(seq_lengths) - seq_lengths
    segment = jnp.sum((starts[None, :] <= position[:, None]).astype(jnp.int32), axis=1)
    return (segment, position)


def slot_matrix(starts, amounts, slots, row_count):
    offsets = jnp.arange(slots, dtype=jnp.int32)
    picked = jnp.where(offsets[None, :] < amounts[:, None], starts[:, None] + offsets[None, :], -1)
    position = jnp.arange(row_count, dtype=jnp.int32)
    return (picked.reshape(-1)[:, None] == position[None, :]).astype(jnp.bfloat16)


def adamw_step(weight, moment, square, gradient, rate):
    moment_new = beta_one * moment + (1.0 - beta_one) * gradient
    square_new = beta_two * square + (1.0 - beta_two) * gradient * gradient
    moment_hat = moment_new / (1.0 - beta_one**STEP)
    square_hat = square_new / (1.0 - beta_two**STEP)
    weight_new = weight - rate * (
        moment_hat / (jnp.sqrt(square_hat) + adam_epsilon) + decay_rate * weight
    )
    return (weight_new, moment_new, square_new)


def along(place):
    return (lax.axis_index("dp"), place)


def greet_line(t, n):
    barrier = pltpu.get_barrier_semaphore()

    @pl.when(t > 0)
    def _():
        pl.semaphore_signal(barrier, inc=1, device_id=along(t - 1), device_id_type=MESH)

    @pl.when(t < n - 1)
    def _():
        pl.semaphore_signal(barrier, inc=1, device_id=along(t + 1), device_id_type=MESH)

    pl.semaphore_wait(barrier, (t > 0).astype(jnp.int32) + (t < n - 1).astype(jnp.int32))


def greet_all(t, n):
    barrier = pltpu.get_barrier_semaphore()
    for k in range(1, n):
        pl.semaphore_signal(
            barrier, inc=1, device_id=along(lax.rem(t + k, n)), device_id_type=MESH
        )
    pl.semaphore_wait(barrier, n - 1)


class LineGather:
    def __init__(self, t, n, chunks, first, place, sems):
        self.t, self.n, self.chunks, self.first, self.place = t, n, chunks, first, place
        self.sems = sems

    def copy(self, h, c, right):
        b = self.t - h if right else self.t + h
        dst = self.place(b, c)
        src = self.first(c) if h == 0 else dst
        s, r = self.sems[:2] if right else self.sems[2:]
        return pltpu.make_async_remote_copy(
            src,
            dst,
            s.at[h, c],
            r.at[h, c],
            device_id=along(self.t + 1 if right else self.t - 1),
            device_id_type=MESH,
        )

    def sends(self, h, right):
        t, n = self.t, self.n
        return (t >= h) & (t < n - 1) if right else (t + h <= n - 1) & (t > 0)

    def gets(self, h, right):
        return self.t - 1 - h >= 0 if right else self.t + 1 + h <= self.n - 1

    def receive(self, h, c, right):
        b = self.t - 1 - h if right else self.t + 1 + h
        dst = self.place(b, c)
        s, r = self.sems[:2] if right else self.sems[2:]
        pltpu.make_async_remote_copy(
            dst,
            dst,
            s.at[h, c],
            r.at[h, c],
            device_id=along(self.t - 1 if right else self.t + 1),
            device_id_type=MESH,
        ).wait_recv()

    def start(self):
        for c in range(self.chunks):
            for right in (True, False):

                @pl.when(self.sends(0, right))
                def _():
                    self.copy(0, c, right).start()

    def forward(self):
        for h in range(self.n - 1):
            for c in range(self.chunks):
                for right in (True, False):

                    @pl.when(self.gets(h, right))
                    def _():
                        self.receive(h, c, right)

                    if h + 1 < self.n - 1:

                        @pl.when(self.sends(h + 1, right))
                        def _():
                            self.copy(h + 1, c, right).start()

    def finish(self):
        for h in range(self.n - 1):
            for c in range(self.chunks):
                for right in (True, False):

                    @pl.when(self.sends(h, right))
                    def _():
                        self.copy(h, c, right).wait_send()


def gather_sems(n, chunks):
    return [DMA((n - 1, chunks))] * 4


def gather_rows_kernel(n, chunks, x_ref, o_ref, sa, ra, sb, rb, own_sem):
    t = lax.axis_index("tensor")
    rows = x_ref.shape[0]
    step = rows // chunks
    greet_line(t, n)
    job = LineGather(
        t,
        n,
        chunks,
        lambda c: x_ref.at[pl.ds(c * step, step)],
        lambda b, c: o_ref.at[pl.ds(b * rows + c * step, step)],
        (sa, ra, sb, rb),
    )
    job.start()
    own = pltpu.make_async_copy(x_ref, o_ref.at[pl.ds(t * rows, rows)], own_sem)
    own.start()
    job.forward()
    own.wait()
    job.finish()


def gather_rows(x, n, collective_id, chunks=4):
    rows, cols = x.shape
    return pl.pallas_call(
        functools.partial(gather_rows_kernel, n, chunks),
        out_shape=jax.ShapeDtypeStruct((n * rows, cols), x.dtype),
        in_specs=[IN_PLACE],
        out_specs=IN_PLACE,
        scratch_shapes=gather_sems(n, chunks) + [DMA],
        compiler_params=pltpu.CompilerParams(collective_id=collective_id, has_side_effects=True),
        name="gather_rows",
    )(x)


def gather_cols_kernel(n, chunks, count, x_ref, *refs):
    t = lax.axis_index("tensor")
    outs, sems = refs[:count], refs[count:]
    rows = x_ref.shape[0]
    cols = x_ref.shape[1] // count
    step = rows // chunks
    greet_line(t, n)
    jobs, owns = [], []
    for i, o_ref in enumerate(outs):
        jobs.append(
            LineGather(
                t,
                n,
                chunks,
                lambda c, i=i: x_ref.at[pl.ds(c * step, step), pl.ds(i * cols, cols)],
                lambda b, c, o_ref=o_ref: o_ref.at[
                    pl.ds(c * step, step), pl.ds(pl.multiple_of(b * cols, cols), cols)
                ],
                sems[5 * i : 5 * i + 4],
            )
        )
        owns.append(
            pltpu.make_async_copy(
                x_ref.at[:, pl.ds(i * cols, cols)],
                o_ref.at[:, pl.ds(pl.multiple_of(t * cols, cols), cols)],
                sems[5 * i + 4],
            )
        )
    for job, own in zip(jobs, owns):
        job.start()
        own.start()
    for job in jobs:
        job.forward()
    for job, own in zip(jobs, owns):
        own.wait()
        job.finish()


def gather_cols(x, count, n, collective_id, chunks=4):
    rows, cols = x.shape
    shape = jax.ShapeDtypeStruct((rows, n * cols // count), x.dtype)
    return pl.pallas_call(
        functools.partial(gather_cols_kernel, n, chunks, count),
        out_shape=(shape,) * count,
        in_specs=[IN_PLACE],
        out_specs=(IN_PLACE,) * count,
        scratch_shapes=(gather_sems(n, chunks) + [DMA]) * count,
        compiler_params=pltpu.CompilerParams(collective_id=collective_id, has_side_effects=True),
        name="gather_cols",
    )(x)


def split_in_kernel(n, chunks, x_ref, rows_ref, cols_ref, ss, rs, own_s, sa, ra, sb, rb, own_g):
    t = lax.axis_index("tensor")
    total = x_ref.shape[0]
    rows, cols = total // n, x_ref.shape[1] // 2
    step = total // chunks
    greet_all(t, n)
    mine = pl.ds(pl.multiple_of(t * cols, cols), cols)

    def block(p):
        return x_ref.at[pl.ds(p * rows, rows), pl.ds(0, cols)]

    copies = []
    for k in range(1, n):
        p = lax.rem(t + k, n)
        copies.append(
            pltpu.make_async_remote_copy(
                block(p),
                rows_ref.at[:, mine],
                ss.at[k - 1],
                rs.at[k - 1],
                device_id=along(p),
                device_id_type=MESH,
            )
        )
    for copy in copies:
        copy.start()
    owns = [
        pltpu.make_async_copy(block(t), rows_ref.at[:, mine], own_s),
        pltpu.make_async_copy(x_ref.at[:, pl.ds(cols, cols)], cols_ref.at[:, mine], own_g),
    ]
    job = LineGather(
        t,
        n,
        chunks,
        lambda c: x_ref.at[pl.ds(c * step, step), pl.ds(cols, cols)],
        lambda b, c: cols_ref.at[
            pl.ds(c * step, step), pl.ds(pl.multiple_of(b * cols, cols), cols)
        ],
        (sa, ra, sb, rb),
    )
    job.start()
    for own in owns:
        own.start()
    job.forward()
    for own in owns:
        own.wait()
    job.finish()
    for copy in copies:
        copy.wait()


def split_in(x, n, collective_id, chunks=4):
    total, both = x.shape
    cols = both // 2
    return pl.pallas_call(
        functools.partial(split_in_kernel, n, chunks),
        out_shape=(
            jax.ShapeDtypeStruct((total // n, n * cols), x.dtype),
            jax.ShapeDtypeStruct((total, n * cols), x.dtype),
        ),
        in_specs=[IN_PLACE],
        out_specs=(IN_PLACE, IN_PLACE),
        scratch_shapes=[DMA((n - 1,)), DMA((n - 1,)), DMA] + gather_sems(n, chunks) + [DMA],
        compiler_params=pltpu.CompilerParams(collective_id=collective_id, has_side_effects=True),
        name="split_in",
    )(x)


def split_out_kernel(n, count, *refs):
    t = lax.axis_index("tensor")
    xs, o_ref = refs[:count], refs[count]
    sends, receives, own_sems = refs[count + 1 :]
    rows = xs[0].shape[0]
    cols = xs[0].shape[1] // n
    greet_all(t, n)

    def source(i, p):
        return xs[i].at[:, pl.ds(pl.multiple_of(p * cols, cols), cols)]

    def target(i):
        return o_ref.at[pl.ds(t * rows, rows), pl.ds(i * cols, cols)]

    copies = []
    for i in range(count):
        for k in range(1, n):
            p = lax.rem(t + k, n)
            copies.append(
                pltpu.make_async_remote_copy(
                    source(i, p),
                    target(i),
                    sends.at[i, k - 1],
                    receives.at[i, k - 1],
                    device_id=along(p),
                    device_id_type=MESH,
                )
            )
    for copy in copies:
        copy.start()
    owns = [pltpu.make_async_copy(source(i, t), target(i), own_sems.at[i]) for i in range(count)]
    for own in owns:
        own.start()
    for own in owns:
        own.wait()
    for copy in copies:
        copy.wait()


def split_out(xs, n, collective_id):
    count = len(xs)
    rows, cols = xs[0].shape
    return pl.pallas_call(
        functools.partial(split_out_kernel, n, count),
        out_shape=jax.ShapeDtypeStruct((n * rows, count * cols // n), xs[0].dtype),
        in_specs=[IN_PLACE] * count,
        out_specs=IN_PLACE,
        scratch_shapes=[DMA((count, n - 1)), DMA((count, n - 1)), DMA((count,))],
        compiler_params=pltpu.CompilerParams(collective_id=collective_id, has_side_effects=True),
        name="split_out",
    )(*xs)


def scatter_rows_kernel(n, chunks, x_ref, o_ref, from_left, from_right, sa, ra, sb, rb):
    t = lax.axis_index("tensor")
    rows = x_ref.shape[0] // n
    step = rows // chunks
    greet_line(t, n)

    def parts(k, c, right):
        held, s, r = (from_left, sa, ra) if right else (from_right, sb, rb)
        return held.at[k, pl.ds(c * step, step)], s.at[k, c], r.at[k, c]

    def send(k, c, right, first):
        slot, s, r = parts(k, c, right)
        d = n - 1 - k if right else k
        return pltpu.make_async_remote_copy(
            x_ref.at[pl.ds(d * rows + c * step, step)] if first else slot,
            slot,
            s,
            r,
            device_id=along(t + 1 if right else t - 1),
            device_id_type=MESH,
        )

    def receive(k, c, right):
        slot, s, r = parts(k, c, right)
        pltpu.make_async_remote_copy(
            slot,
            slot,
            s,
            r,
            device_id=along(t - 1 if right else t + 1),
            device_id_type=MESH,
        ).wait_recv()

    every = [
        (k, c, right, n - 1 - k if right else k)
        for k in range(n - 1)
        for c in range(chunks)
        for right in (True, False)
    ]
    for k, c, right, d in every:

        @pl.when((t == (0 if right else n - 1)) & (t != d))
        def _():
            send(k, c, right, True).start()

    for k, c, right, d in every:

        @pl.when((t > 0) & (t < d) if right else (t < n - 1) & (t > d))
        def _():
            receive(k, c, right)
            slot = parts(k, c, right)[0]
            mine = x_ref[pl.ds(d * rows + c * step, step)]
            slot[...] = (slot[...].astype(jnp.float32) + mine.astype(jnp.float32)).astype(
                slot.dtype
            )
            send(k, c, right, False).start()

    for k, c, right, d in every:

        @pl.when(t == d)
        def _():
            receive(k, c, right)

    o_ref[...] = x_ref[pl.ds(pl.multiple_of(t * rows, rows), rows)].astype(jnp.float32)

    @pl.when(t > 0)
    def _():
        o_ref[...] += from_left[n - 1 - t].astype(jnp.float32)

    @pl.when(t < n - 1)
    def _():
        o_ref[...] += from_right[t].astype(jnp.float32)

    for k, c, right, d in every:

        @pl.when(t < d if right else t > d)
        def _():
            send(k, c, right, False).wait_send()


def scatter_rows(x, n, collective_id, chunks=4):
    rows, cols = x.shape[0] // n, x.shape[1]
    return pl.pallas_call(
        functools.partial(scatter_rows_kernel, n, chunks),
        out_shape=jax.ShapeDtypeStruct((rows, cols), jnp.float32),
        in_specs=[IN_VMEM],
        out_specs=IN_VMEM,
        scratch_shapes=[pltpu.VMEM((n - 1, rows, cols), x.dtype)] * 2
        + [DMA((n - 1, chunks))] * 4,
        compiler_params=pltpu.CompilerParams(
            collective_id=collective_id, has_side_effects=True, vmem_limit_bytes=40 * MIB
        ),
        name="scatter_rows",
    )(x)


def sum_all_kernel(n_dp, n, x_ref, o_ref, from_z, from_dp, part, s1, r1, s2, r2, s3, r3):
    g, t = lax.axis_index("dp"), lax.axis_index("tensor")
    rows = x_ref.shape[0] // n
    barrier = pltpu.get_barrier_semaphore()
    for k in range(1, n):
        pl.semaphore_signal(
            barrier, inc=1, device_id=(g, lax.rem(t + k, n)), device_id_type=MESH
        )
    for k in range(1, n_dp):
        pl.semaphore_signal(
            barrier, inc=1, device_id=(lax.rem(g + k, n_dp), t), device_id_type=MESH
        )
    pl.semaphore_wait(barrier, n - 1 + n_dp - 1)

    def piece(p):
        return pl.ds(pl.multiple_of(p * rows, rows), rows)

    first = []
    for k in range(1, n):
        p = lax.rem(t + k, n)
        first.append(
            pltpu.make_async_remote_copy(
                x_ref.at[piece(p)],
                from_z.at[k - 1],
                s1.at[k - 1],
                r1.at[k - 1],
                device_id=(g, p),
                device_id_type=MESH,
            )
        )
    for copy in first:
        copy.start()
    for copy in first:
        copy.wait()
    total = x_ref[piece(t)]
    for k in range(1, n):
        total = total + from_z[k - 1]
    part[...] = total
    second = []
    for k in range(1, n_dp):
        second.append(
            pltpu.make_async_remote_copy(
                part,
                from_dp.at[g],
                s2.at[k - 1],
                r2.at[k - 1],
                device_id=(lax.rem(g + k, n_dp), t),
                device_id_type=MESH,
            )
        )
    for copy in second:
        copy.start()
    from_dp[g] = part[...]
    for copy in second:
        copy.wait()
    total = from_dp[0]
    for k in range(1, n_dp):
        total = total + from_dp[k]
    o_ref[piece(t)] = total
    third = []
    for k in range(1, n):
        third.append(
            pltpu.make_async_remote_copy(
                o_ref.at[piece(t)],
                o_ref.at[piece(t)],
                s3.at[k - 1],
                r3.at[k - 1],
                device_id=(g, lax.rem(t + k, n)),
                device_id_type=MESH,
            )
        )
    for copy in third:
        copy.start()
    for copy in third:
        copy.wait()


def sum_all(x, n_dp, n, collective_id):
    rows = x.shape[0] // n
    return pl.pallas_call(
        functools.partial(sum_all_kernel, n_dp, n),
        out_shape=jax.ShapeDtypeStruct(x.shape, x.dtype),
        in_specs=[IN_VMEM],
        out_specs=IN_VMEM,
        scratch_shapes=[
            pltpu.VMEM((n - 1, rows, 128), x.dtype),
            pltpu.VMEM((n_dp, rows, 128), x.dtype),
            pltpu.VMEM((rows, 128), x.dtype),
        ]
        + [DMA((n - 1,))] * 2
        + [DMA((n_dp - 1,))] * 2
        + [DMA((n - 1,))] * 2,
        compiler_params=pltpu.CompilerParams(collective_id=collective_id, has_side_effects=True),
        name="sum_all",
    )(x)


def local(
    tokens,
    cotangent,
    lengths,
    counts,
    query_weight,
    query_moment,
    query_square,
    shared_weight,
    shared_moment,
    shared_square,
    project_weight,
    project_moment,
    project_square,
    expand_weight,
    expand_moment,
    expand_square,
    shrink_weight,
    shrink_moment,
    shrink_square,
    vectors_value,
    vectors_moment,
    vectors_square,
):
    device = lax.axis_index("dp")
    n_dp = lax.axis_size("dp")
    t = lax.axis_index("tensor")
    n = lax.axis_size("tensor")
    row_count, width = tokens.shape
    slots = 2 * row_count // n_dp
    part_rows, part_cols = row_count // n, width // n
    send_start = lax.dynamic_index_in_dim(exclusive_sum(counts, 1), device, 0, keepdims=False)
    send_amount = lax.dynamic_index_in_dim(counts, device, 0, keepdims=False)
    recv_start = lax.dynamic_index_in_dim(exclusive_sum(counts, 0), device, 1, keepdims=False)
    recv_amount = lax.dynamic_index_in_dim(counts, device, 1, keepdims=False)
    send_slots = slot_matrix(send_start, send_amount, slots, row_count)
    recv_slots = slot_matrix(recv_start, recv_amount, slots, row_count)

    def exchange(rows, out_slots, in_slots):
        packed = mul_plain(out_slots, rows).astype(jnp.bfloat16)
        arrived = lax.all_to_all(
            packed.reshape(n_dp, slots, rows.shape[1]), "dp", split_axis=0, concat_axis=0, tiled=True
        )
        return mul_left_t(in_slots, arrived.reshape(n_dp * slots, rows.shape[1])).astype(
            jnp.bfloat16
        )

    query_all = lax.all_gather(
        gather_cols(query_weight.astype(jnp.bfloat16), 1, n, 1, 1)[0], "dp", axis=0, tiled=True
    )
    shared_all = lax.all_gather(
        shared_weight.astype(jnp.bfloat16), ("dp", "tensor"), axis=0, tiled=True
    )
    project_all = lax.all_gather(
        gather_rows(project_weight.astype(jnp.bfloat16), n, 2, 1), "dp", axis=1, tiled=True
    )
    expand_cols = lax.all_gather(expand_weight.astype(jnp.bfloat16), "dp", axis=0, tiled=True)
    shrink_rows = lax.all_gather(shrink_weight.astype(jnp.bfloat16), "dp", axis=1, tiled=True)

    mine_cols = [
        lax.dynamic_slice_in_dim(a, t * part_cols, part_cols, 1) for a in (tokens, cotangent)
    ]
    owned = exchange(jnp.concatenate(mine_cols, axis=1), send_slots, recv_slots)
    owned_rows, owned_grad = split_in(owned, n, 3)

    head_size = shared_all.shape[1] // 2
    heads = width // head_size
    hidden_width = expand_cols.shape[1]
    hidden_total = hidden_width * n
    gain_one = vectors_value[0:width]
    shift_one = vectors_value[width : 2 * width]
    gain_two = vectors_value[2 * width : 3 * width]
    shift_two = vectors_value[3 * width : 4 * width]
    query_bias = vectors_value[4 * width : 5 * width]
    project_bias = vectors_value[5 * width : 6 * width]
    shrink_bias = vectors_value[6 * width : 7 * width]
    expand_bias = lax.dynamic_slice_in_dim(
        vectors_value, 7 * width + t * hidden_width, hidden_width, 0
    )
    value_bias = vectors_value[7 * width + hidden_total : 7 * width + hidden_total + head_size]

    inputs_float = owned_rows.astype(jnp.float32)
    normed_one, norm_one_back = jax.vjp(layer_norm, inputs_float, gain_one, shift_one)
    normed_low = normed_one.astype(jnp.bfloat16)
    queries = (mul_plain(normed_low, query_all) + query_bias).astype(jnp.bfloat16)
    shared_out = mul_plain(normed_low, shared_all) + jnp.concatenate(
        [jnp.zeros((head_size,), jnp.float32), value_bias]
    )
    shared_rows = gather_rows(shared_out.astype(jnp.bfloat16), n, 4, 1)
    key_rows, value_rows = shared_rows[:, :head_size], shared_rows[:, head_size:]
    query_heads = queries.reshape(part_rows, heads, head_size)
    segment, position = segment_ids(lengths[0], row_count)
    my_segment = lax.dynamic_slice_in_dim(segment, t * part_rows, part_rows, 0)
    my_position = lax.dynamic_slice_in_dim(position, t * part_rows, part_rows, 0)
    allowed = (my_segment[:, None] == segment[None, :]) & (
        my_position[:, None] >= position[None, :]
    )
    score_scale = head_size ** (-0.5)

    def masked_scores():
        scores = (
            jnp.einsum("bhd,kd->hbk", query_heads, key_rows, preferred_element_type=jnp.float32)
            * score_scale
        )
        return jnp.where(allowed[None], scores, masked_score)

    scores = masked_scores()
    row_max = jnp.max(scores, axis=-1, keepdims=True)
    expo = jnp.exp(scores - row_max)
    row_total = jnp.sum(expo, axis=-1, keepdims=True)
    probs = expo / row_total
    heads_out = (
        jnp.einsum(
            "hbk,kd->bhd",
            probs.astype(jnp.bfloat16),
            value_rows,
            preferred_element_type=jnp.float32,
        )
        .reshape(part_rows, width)
        .astype(jnp.bfloat16)
    )
    log_total = row_max + jnp.log(row_total)
    hidden_one = inputs_float + (mul_plain(heads_out, project_all) + project_bias)
    normed_two, norm_two_back = jax.vjp(layer_norm, hidden_one, gain_two, shift_two)

    normed_two_low = gather_rows(normed_two.astype(jnp.bfloat16), n, 5)
    expand_pre = mul_plain(normed_two_low, expand_cols) + expand_bias
    activated, gelu_back = jax.vjp(gelu_tanh, expand_pre)
    activated_low = activated.astype(jnp.bfloat16)
    ffn_partial = mul_plain(activated_low, shrink_rows).astype(jnp.bfloat16)
    shrink_grad = mul_left_t(activated_low, owned_grad)
    activated_grad = mul_right_t(owned_grad, shrink_rows)
    expand_pre_grad = gelu_back(activated_grad)[0].astype(jnp.bfloat16)
    expand_grad = mul_left_t(normed_two_low, expand_pre_grad)
    expand_bias_grad = jnp.sum(expand_pre_grad.astype(jnp.float32), axis=0)
    normed_two_part = mul_right_t(expand_pre_grad, expand_cols).astype(jnp.bfloat16)

    normed_two_grad = scatter_rows(normed_two_part, n, 6)
    ffn_branch = scatter_rows(ffn_partial, n, 7) + shrink_bias
    layer_result = (hidden_one + ffn_branch).astype(jnp.bfloat16)
    output_float = lax.dynamic_slice_in_dim(owned_grad, t * part_rows, part_rows, 0).astype(
        jnp.float32
    )
    shrink_bias_grad = jnp.sum(output_float, axis=0)
    hidden_from_norm, gain_two_grad, shift_two_grad = norm_two_back(normed_two_grad)
    hidden_grad = output_float + hidden_from_norm
    branch_grad = hidden_grad.astype(jnp.bfloat16)
    project_bias_grad = jnp.sum(branch_grad.astype(jnp.float32), axis=0)
    project_grad = mul_left_t(heads_out, branch_grad)
    heads_grad = (
        mul_right_t(branch_grad, project_all)
        .astype(jnp.bfloat16)
        .reshape(part_rows, heads, head_size)
    )
    probs = jnp.exp(masked_scores() - log_total)
    prob_grad = jnp.einsum(
        "bhd,kd->hbk", heads_grad, value_rows, preferred_element_type=jnp.float32
    )
    score_grad = (
        probs * (prob_grad - jnp.sum(probs * prob_grad, axis=-1, keepdims=True))
    ).astype(jnp.bfloat16)
    query_grad = (
        (
            jnp.einsum("hbk,kd->bhd", score_grad, key_rows, preferred_element_type=jnp.float32)
            * score_scale
        )
        .reshape(part_rows, width)
        .astype(jnp.bfloat16)
    )
    key_grad = (
        jnp.einsum("hbk,bhd->kd", score_grad, query_heads, preferred_element_type=jnp.float32)
        * score_scale
    )
    value_grad = jnp.einsum(
        "hbk,bhd->kd",
        probs.astype(jnp.bfloat16),
        heads_grad,
        preferred_element_type=jnp.float32,
    )
    shared_grad = scatter_rows(
        jnp.concatenate([key_grad, value_grad], axis=1).astype(jnp.bfloat16), n, 8, 1
    ).astype(jnp.bfloat16)
    query_bias_grad = jnp.sum(query_grad.astype(jnp.float32), axis=0)
    query_weight_grad = mul_left_t(normed_low, query_grad)
    normed_one_grad = mul_right_t(query_grad, query_all) + mul_right_t(shared_grad, shared_all)
    inputs_from_norm, gain_one_grad, shift_one_grad = norm_one_back(normed_one_grad)
    input_result = (hidden_grad + inputs_from_norm).astype(jnp.bfloat16)
    shared_weight_grad = mul_left_t(normed_low, shared_grad)
    value_bias_grad = jnp.sum(shared_grad[:, head_size:].astype(jnp.float32), axis=0)

    back = exchange(split_out((layer_result, input_result), n, 9), recv_slots, send_slots)
    output_rows, grad_rows = gather_cols(back, 2, n, 10)
    output_back = output_rows.astype(jnp.float32)
    token_rms = jnp.sqrt(jnp.mean(output_back * output_back, axis=1))

    def over_dp(partial, dimension):
        return lax.psum_scatter(
            partial.astype(jnp.bfloat16), "dp", scatter_dimension=dimension, tiled=True
        )

    def over_tensor(partial, dimension):
        return lax.psum_scatter(partial, "tensor", scatter_dimension=dimension, tiled=True).astype(
            jnp.float32
        )

    expand_part = over_dp(expand_grad, 0).astype(jnp.float32)
    shrink_part = over_dp(shrink_grad, 1).astype(jnp.float32)
    query_part = over_tensor(over_dp(query_weight_grad, 0), 1)
    project_part = over_tensor(over_dp(project_grad, 1), 0)
    shared_piece = over_tensor(over_dp(shared_weight_grad, 0), 0)
    split_part = lax.dynamic_update_slice_in_dim(
        jnp.zeros((hidden_total,), jnp.float32), expand_bias_grad, t * hidden_width, 0
    )
    vector_part = jnp.concatenate(
        [
            gain_one_grad,
            shift_one_grad,
            gain_two_grad,
            shift_two_grad,
            query_bias_grad,
            project_bias_grad,
            shrink_bias_grad,
            split_part,
            value_bias_grad,
        ]
    )
    local_squares = (
        jnp.sum(query_part * query_part)
        + jnp.sum(expand_part * expand_part)
        + jnp.sum(shared_piece * shared_piece)
        + jnp.sum(project_part * project_part)
        + jnp.sum(shrink_part * shrink_part)
    )
    length = vector_part.shape[0]
    unit = n * 8 * 128
    padded = -(-(length + 1) // unit) * unit
    everything = jnp.concatenate(
        [vector_part, local_squares[None], jnp.zeros((padded - length - 1,), jnp.float32)]
    )
    summed = sum_all(everything.reshape(padded // 128, 128), n_dp, n, 11).reshape(padded)
    vector_grad, weight_squares = summed[:length], summed[length]
    grad_size = jnp.sqrt(weight_squares + jnp.sum(vector_grad * vector_grad))
    clip_factor = jnp.minimum(1.0, clip_level / (grad_size + 1e-06))
    clipped_vectors = clip_factor * vector_grad
    query_new = adamw_step(
        query_weight,
        query_moment,
        query_square,
        clip_factor * query_part,
        rate_matrix * width ** (-0.5),
    )
    shared_new = adamw_step(
        shared_weight,
        shared_moment,
        shared_square,
        clip_factor * shared_piece,
        rate_attention * width ** (-0.5),
    )
    project_new = adamw_step(
        project_weight,
        project_moment,
        project_square,
        clip_factor * project_part,
        rate_attention * width ** (-0.5),
    )
    expand_new = adamw_step(
        expand_weight,
        expand_moment,
        expand_square,
        clip_factor * expand_part,
        rate_matrix * width ** (-0.5),
    )
    shrink_new = adamw_step(
        shrink_weight,
        shrink_moment,
        shrink_square,
        clip_factor * shrink_part,
        rate_matrix * hidden_total ** (-0.5),
    )
    vectors_new = adamw_step(
        vectors_value, vectors_moment, vectors_square, clipped_vectors, rate_vector
    )
    return (
        output_rows,
        grad_rows,
        grad_size,
        *query_new,
        *shared_new,
        *project_new,
        *expand_new,
        *shrink_new,
        *vectors_new,
        clipped_vectors,
        token_rms,
    )


def solution(mesh):
    by_rows = P("dp", None)
    query = P("dp", "tensor")
    shared = P(("dp", "tensor"), None)
    project = P("tensor", "dp")
    return jax.shard_map(
        local,
        mesh=mesh,
        in_specs=(
            *(by_rows,) * 3,
            P(),
            *(query,) * 3,
            *(shared,) * 3,
            *(project,) * 3,
            *(query,) * 3,
            *(project,) * 3,
            *(P(),) * 3,
        ),
        out_specs=(
            *(by_rows,) * 2,
            P(),
            *(query,) * 3,
            *(shared,) * 3,
            *(project,) * 3,
            *(query,) * 3,
            *(project,) * 3,
            *(P(),) * 4,
            P("dp"),
        ),
        check_vma=False,
    )
```

time: 2040 us -> 1160 us (0.57)
  waiting for transfers between devices: 1210 us -> 240 us
  Pallas kernels: 0 us -> 583 us
  blocking collectives: 329 us -> 0 us
  local copies, waits for them, and re-layouts: 147 us -> 16.3 us
  other arithmetic: 135 us -> 72.4 us
  matrix products: 173 us -> 210 us
    psum x5 -> x0, waiting for transfers between devices: 846 us -> none  [the longest x1 275 us: local(): normed_two_grad = lax.psum(normed_two_part, 'tensor')]
    pallas_call x0 -> x11, Pallas kernels: none -> 583 us  [the longest x3 175 us: scatter_rows(): pl.pallas_call(functools.partial(scatter_rows_kernel, n, chunks), out_sha...]
    all_to_all x2 -> x0, blocking collectives: 214 us -> none  [the longest x1 114 us: local(): lax.all_to_all(pack_slots(input_result, recv_start, recv_amount, slots),...]
    gather x8 -> x0, local copies, waits for them, and re-layouts: 130 us -> none  [the longest x4 76.5 us: pack_slots(): jnp.take(rows_in, picked.reshape(-1), axis=0)]
    psum x2 -> x0, blocking collectives: 114 us -> none  [the longest x1 75 us: local(): lax.psum((normed_one_local, kv_local), 'tensor')]
    all_gather x1, waiting for transfers between devices: 45.6 us -> 0.02 us  [local(): lax.all_gather(expand_weight.astype(jnp.bfloat16), 'dp', axis=0, tiled=True)]
    all_gather x1, waiting for transfers between devices: 42.5 us -> 0.01 us  [local(): lax.all_gather(shrink_weight.astype(jnp.bfloat16), 'dp', axis=1, tiled=True)]
    select_n x5 -> x0, other arithmetic: 29.2 us -> none  [the longest x2 14.2 us: pack_slots(): jnp.take(rows_in, picked.reshape(-1), axis=0)]
  transfers between devices with their start and end apart: 17 -> 15, of which waited for: 10 -> 6; matrix products, arithmetic and copies ran while one was open for 17% -> 15% of each run, Pallas kernels for 0% -> 34%
where the time goes in v1:
time: 1160 us; the launch traced here: 1150 us
  Pallas kernels  583 us (50%)
  waiting for transfers between devices  240 us (21%)
  matrix products  210 us (18%)
  other arithmetic  72.4 us (6%)
  between operations  21.2 us (2%)
  local copies, waits for them, and re-layouts  16.3 us (1%)
    pallas_call x3, Pallas kernels, scatter_rows(): pl.pallas_call(functools.partial(scatter_rows_kernel, n, chunks), out_sha...  175 us
    pallas_call x2, Pallas kernels, gather_cols(): pl.pallas_call(functools.partial(gather_cols_kernel, n, chunks, count), o...  161 us
    reduce_scatter x5, waiting for transfers between devices, over_dp(): lax.psum_scatter(partial.astype(jnp.bfloat16), 'dp', scatter_dimension=di...  106 us
    pallas_call x3, Pallas kernels, gather_rows(): pl.pallas_call(functools.partial(gather_rows_kernel, n, chunks), out_shap...  103 us
    pallas_call x1, Pallas kernels, split_in(): pl.pallas_call(functools.partial(split_in_kernel, n, chunks), out_shape=(...  83.9 us
    reduce_scatter x3, waiting for transfers between devices, over_tensor(): lax.psum_scatter(partial, 'tensor', scatter_dimension=dimension, tiled=True)  68.9 us
    all_to_all x2, waiting for transfers between devices, exchange(): lax.all_to_all(packed.reshape(n_dp, slots, rows.shape[1]), 'dp', split_ax...  64.6 us
    dot_general x7, matrix products, mul_left_t(): lax.dot_general(left, right, (((0,), (0,)), ((), ())), preferred_element_...  62 us
  transfers between devices with their start and end apart: 15, of which 6 were waited for; matrix products, arithmetic and copies ran while one was open for 15% of the time, Pallas kernels for 34%

profile of v1, /device:TPU:0, one launch (start us, length us, event | category | flops | bytes accessed | tf_op | source)
XLA Modules:
  0.0 1153.5 jit_solution(11335900552475896358)
XLA Ops:
  10.6 24.7 %gather_cols.2 = bf16[256,2048]{1,0:T(8,128)(2,1)} custom-call(bf16[256,512]{1,0:T(8,128)(2,1)} %convert_element_type.161.x_ref), custom_call_target="tpu_custom_call" | custom-call | tf_op jit(solution)/shard_map/gather_cols/pallas_call | solution.py:265
  36.1 21.0 %gather_rows.4 = bf16[2048,256]{1,0:T(8,128)(2,1)} custom-call(bf16[512,256]{1,0:T(8,128)(2,1)} %convert_element_type.167.x_ref), custom_call_target="tpu_custom_call" | custom-call | tf_op jit(solution)/shard_map/gather_rows/pallas_call | solution.py:213
  57.2 2.9 convert_element_type.169
  63.2 6.1 fusion.24
  69.4 4.7 all-to-all-start
  75.2 64.6 %all-to-all-done = bf16[8,256,1024]{2,1,0:T(8,128)(2,1)} async-done(((bf16[8,256,1024]{2,1,0:T(8,128)(2,1)}), bf16[8,256,1024]{2,1,0:T(8,128)(2,1)}, u32[]{:S(2)}, u32[]{:S(2)}) %all-to-all-start) | async-done | bytes 4194336 | tf_op jit(solution)/shard_map/all_to_all | solution.py:630
  139.8 8.2 fusion.50.x_ref
  148.0 83.9 %split_in.1 = (bf16[256,2048]{1,0:T(8,128)(2,1)}, bf16[1024,2048]{1,0:T(8,128)(2,1)}) custom-call(bf16[1024,1024]{1,0:T(8,128)(2,1)} %fusion.50.x_ref), custom_call_target="tpu_custom_call" | custom-call | tf_op jit(solution)/shard_map/split_in/pallas_call | solution.py:330
  237.7 14.1 %gather_rows.3 = bf16[1024,256]{1,0:T(8,128)(2,1)} custom-call(bf16[256,256]{1,0:T(8,128)(2,1)} %fusion.61.x_ref), custom_call_target="tpu_custom_call" | custom-call | tf_op jit(solution)/shard_map/gather_rows/pallas_call | solution.py:213
  251.9 6.9 fusion.30
  260.3 7.4 fusion.112
  267.7 8.1 fusion.3
  275.8 9.3 fusion.51
  285.1 6.2 fusion.113
  293.1 68.2 %gather_rows.5 = bf16[1024,2048]{1,0:T(8,128)(2,1)} custom-call(bf16[256,2048]{1,0:T(8,128)(2,1)} %add_convert_fusion.2.x_ref), custom_call_target="tpu_custom_call" | custom-call | tf_op jit(solution)/shard_map/gather_rows/pallas_call | solution.py:213
  361.4 14.5 %fusion.114 = f32[1024,2048]{1,0:T(8,128)} fusion(bf16[1024,2048]{1,0:T(8,128)(2,1)} %gather_rows.5, bf16[2048,2048]{1,0:T(8,128)(2,1)} %all-gather.12.cloned.1.call-done), kind=kOutput, calls=%fused_computation.185 | convolution fusion | flops 8589934592 | bytes 20971520 | tf_op jit(solution)/shard_map/dot_general | solution.py:32
  375.9 19.4 %convert_reduce_fusion = (f32[2048]{0:T(1024)}, bf16[1024,2048]{1,0:T(8,128)(2,1)S(1)}) fusion(f32[1024,2048]{1,0:T(8,128)} %fusion.114, f32[2048]{0:T(1024)S(1)} %get-tuple-element.67, bf16[1024,2048]{1,0:T(8,128)(2,1)} %get-tuple-element.28, bf16[2048,2048]{1,0:T(8,128)(2,1)} %all-gather.14.cloned.1.call-done), kind=kOutput, calls=%fused_computation.22 | convolution fusion | flops 8638167040 | bytes 25182208 | tf_op jit(solution)/shard_map/dot_general | solution.py:36
  395.3 9.3 convolution_convert_fusion.4.x_ref
  404.6 73.0 %scatter_rows.4 = f32[256,2048]{1,0:T(8,128)S(1)} custom-call(bf16[1024,2048]{1,0:T(8,128)(2,1)S(1)} %convolution_convert_fusion.4.x_ref), custom_call_target="tpu_custom_call" | custom-call | tf_op jit(solution)/shard_map/scatter_rows/pallas_call | solution.py:479
  478.9 15.5 %convolution_convert_fusion.5.x_ref = bf16[1024,2048]{1,0:T(8,128)(2,1)S(1)} fusion(bf16[2048,2048]{1,0:T(8,128)(2,1)} %all-gather.14.cloned.1.call-done, f32[1024,2048]{1,0:T(8,128)} %fusion.114, f32[2048]{0:T(1024)S(1)} %get-tuple-element.67), kind=kOutput, calls=%fused_computation.41 | convolution fusion | flops 8613003264 | bytes 20979712 | tf_op jit(solution)/shard_map/dot_general | solution.py:32
  494.5 77.8 %scatter_rows.3 = f32[256,2048]{1,0:T(8,128)S(1)} custom-call(bf16[1024,2048]{1,0:T(8,128)(2,1)S(1)} %convolution_convert_fusion.5.x_ref), custom_call_target="tpu_custom_call" | custom-call | tf_op jit(solution)/shard_map/scatter_rows/pallas_call | solution.py:479
  577.4 3.3 convolution_convert_fusion.7
  582.4 13.4 %fusion = (f32[16,256]{1,0:T(8,128)S(1)}, f32[1024,256,16]{1,0,2:T(8,128)}) fusion(f32[16,256,1024]{1,2,0:T(8,128)} %get-tuple-element.77, f32[16,256]{1,0:T(8,128)S(1)} %log_add_fusion, bf16[256,16,128]{0,2,1:T(8,128)(2,1)S(1)} %bitcast.110, bf16[1024,256]{1,0:T(8,128)(2,1)S(1)} %copy-done.15), kind=kOutput, calls=%fused_computation.2 | convolution fusion | flops 1086320640 | bytes 34897920 | tf_op jit(solution)/shard_map/bhd,kd->hbk/dot_general | solution.py:745
  595.8 8.9 fusion.57
  604.7 10.4 fusion.2
  615.2 5.7 fusion.60
  621.0 24.0 %scatter_rows.5 = f32[256,256]{1,0:T(8,128)S(1)} custom-call(bf16[1024,256]{1,0:T(8,128)(2,1)S(1)} %pad_maximum_fusion.x_ref), custom_call_target="tpu_custom_call" | custom-call | tf_op jit(solution)/shard_map/scatter_rows/pallas_call | solution.py:479
  646.9 4.9 convert_reduce_fusion.4
  651.8 5.8 convolution_convert_fusion.3
  658.7 6.8 convolution_convert_fusion.1
  665.6 14.9 %reduce-scatter.15.cloned.1.call-done = bf16[256,256]{1,0:T(8,128)(2,1)} async-done(((bf16[2048,256]{1,0:T(8,128)(2,1)}), bf16[256,256]{1,0:T(8,128)(2,1)}) %reduce-scatter.15.cloned.1.call-update) | async-done | bytes 131088 | tf_op jit(solution)/shard_map/reduce_scatter | solution.py:786
  680.6 14.3 %convolution_convert_fusion.2 = bf16[2048,2048]{1,0:T(8,128)(2,1)} fusion(bf16[1024,2048]{1,0:T(8,128)(2,1)} %gather_rows.5, bf16[1024,2048]{1,0:T(8,128)(2,1)} %copy-done.57), kind=kOutput, calls=%fused_computation.34 | convolution fusion | flops 8594128896 | bytes 16777216 | tf_op jit(solution)/shard_map/dot_general | solution.py:42
  695.1 17.2 %convolution_convert_fusion = bf16[2048,2048]{1,0:T(8,128)(2,1)} fusion(bf16[1024,2048]{1,0:T(8,128)(2,1)} %get-tuple-element.28, f32[1024,2048]{1,0:T(8,128)} %fusion.114, f32[2048]{0:T(1024)S(1)} %get-tuple-element.67), kind=kOutput, calls=%fused_computation.32 | convolution fusion | flops 8615100416 | bytes 20979712 | tf_op jit(solution)/shard_map/dot_general | solution.py:42
  712.4 5.9 fusion.115
  720.7 3.5 convert_reduce_fusion.2
  724.2 44.3 %split_out.1 = bf16[1024,1024]{1,0:T(8,128)(2,1)} custom-call(bf16[256,2048]{1,0:T(8,128)(2,1)} %get-tuple-element.65.refs_0_, bf16[256,2048]{1,0:T(8,128)(2,1)} %get-tuple-element.64.refs_1_), custom_call_target="tpu_custom_call" | custom-call | tf_op jit(solution)/shard_map/split_out/pallas_call | solution.py:386
  768.5 8.4 fusion.25
  776.9 4.7 all-to-all-start.1
  782.6 91.3 %reduce-scatter.19.cloned.1.call-done = bf16[2048,256]{1,0:T(8,128)(2,1)} async-done(((bf16[2048,2048]{1,0:T(8,128)(2,1)}), bf16[2048,256]{1,0:T(8,128)(2,1)}) %reduce-scatter.19.cloned.1.call-update) | async-done | bytes 1048592 | tf_op jit(solution)/shard_map/reduce_scatter | solution.py:786
  873.9 21.4 %reduce-scatter.17.cloned.1.call-done = bf16[64,256]{1,0:T(8,128)(2,1)} async-done(((bf16[256,256]{1,0:T(8,128)(2,1)}), bf16[64,256]{1,0:T(8,128)(2,1)}) %reduce-scatter.17.cloned.1.call-update) | async-done | bytes 32784 | tf_op jit(solution)/shard_map/reduce_scatter | solution.py:791
  896.7 8.1 fusion.49.x_ref
  904.8 136.2 %gather_cols.3 = (bf16[1024,2048]{1,0:T(8,128)(2,1)}, bf16[1024,2048]{1,0:T(8,128)(2,1)}) custom-call(bf16[1024,1024]{1,0:T(8,128)(2,1)} %fusion.49.x_ref), custom_call_target="tpu_custom_call" | custom-call | tf_op jit(solution)/shard_map/gather_cols/pallas_call | solution.py:265
  1041.0 3.1 multiply_reduce_fusion
  1049.7 23.0 %reduce-scatter.11.cloned.1.call-done = bf16[256,512]{1,0:T(8,128)(2,1)} async-done(((bf16[256,2048]{1,0:T(8,128)(2,1)}), bf16[256,512]{1,0:T(8,128)(2,1)}) %reduce-scatter.11.cloned.1.call-update) | async-done | bytes 262160 | tf_op jit(solution)/shard_map/reduce_scatter | solution.py:791
  1076.3 24.5 %reduce-scatter.21.cloned.1.call-done = bf16[512,256]{1,0:T(8,128)(2,1)} async-done(((bf16[2048,256]{1,0:T(8,128)(2,1)}), bf16[512,256]{1,0:T(8,128)(2,1)}) %reduce-scatter.21.cloned.1.call-update) | async-done | bytes 262160 | tf_op jit(solution)/shard_map/reduce_scatter | solution.py:791
  1104.6 15.5 %sum_all.1 = f32[192,128]{1,0:T(8,128)} custom-call(f32[192,128]{1,0:T(8,128)} %bitcast.121), custom_call_target="tpu_custom_call" | custom-call | tf_op jit(solution)/shard_map/sum_all/pallas_call | solution.py:572
  1125.9 6.1 multiply_subtract_fusion
  1132.2 3.9 multiply_subtract_fusion.1
  (233 shorter events, 57.1 us)
Async XLA Ops:
  7.2 28.2 %copy-start.17 = (f32[512,256]{1,0:T(8,128)S(1)}, f32[512,256]{1,0:T(8,128)}, u32[]{:S(2)}) copy-start(f32[512,256]{1,0:T(8,128)} %param.32) | copy-start | bytes 1572868
  7.2 228.0 %all-gather.6.cloned.1.call-start = ((), (), s32[]{:S(2)}) async-start(), calls=%async_computation.10 | async-start | bytes 1081344 | tf_op jit(solution)/shard_map/all_gather | solution.py:640
  8.8 243.0 %all-gather.8.cloned.1.call-start = ((), (), s32[]{:S(2)}) async-start(), calls=%async_computation.11 | async-start | bytes 9437184 | tf_op jit(solution)/shard_map/all_gather | solution.py:637
  35.3 249.8 %all-gather.10.cloned.1.call-start = ((), (), s32[]{:S(2)}) async-start(), calls=%async_computation.12 | async-start | bytes 9437184 | tf_op jit(solution)/shard_map/all_gather | solution.py:643
  57.1 304.3 %all-gather.12.cloned.1.call-start = ((), (), s32[]{:S(2)}) async-start(), calls=%async_computation.13 | async-start | bytes 9437184 | tf_op jit(solution)/shard_map/all_gather | solution.py:646
  60.1 315.9 %all-gather.14.cloned.1.call-start = ((), (), s32[]{:S(2)}) async-start(), calls=%async_computation.14 | async-start | bytes 9437184 | tf_op jit(solution)/shard_map/all_gather | solution.py:647
  69.4 70.5 %all-to-all-start = ((bf16[8,256,1024]{2,1,0:T(8,128)(2,1)}), bf16[8,256,1024]{2,1,0:T(8,128)(2,1)}, u32[]{:S(2)}, u32[]{:S(2)}) async-start(bf16[8,256,1024]{2,1,0:T(8,128)(2,1)} %bitcast.116), calls=%async_computation | async-start | bytes 8388608 | tf_op jit(solution)/shard_map/all_to_all | solution.py:630
  74.1 606.4 %reduce-scatter.15.cloned.1.call-start = ((), (), s32[]{:S(2)}) async-start(), calls=%async_computation.18 | async-start | bytes 1179648 | tf_op jit(solution)/shard_map/reduce_scatter | solution.py:786
  74.4 73.6 %copy-start.52 = (s32[1,2,8,128]{3,1,2,0:T(2,128)}, s32[1,2,8,128]{3,1,2,0:T(2,128)S(1)}, u32[]{:S(2)}) copy-start(s32[1,2,8,128]{3,1,2,0:T(2,128)S(1)} %copy.96) | copy-start | bytes 24580
  75.0 176.8 %copy-start.29 = (f32[2048]{0:T(1024)}, f32[2048]{0:T(1024)S(1)}, u32[]{:S(2)}) copy-start(f32[2048]{0:T(1024)S(1)} %get-tuple-element.73) | copy-start | bytes 24580
  75.0 176.8 %copy-start.34 = (f32[2048]{0:T(1024)}, f32[2048]{0:T(1024)S(1)}, u32[]{:S(2)}) copy-start(f32[2048]{0:T(1024)S(1)} %get-tuple-element.72) | copy-start | bytes 24580
  233.5 18.4 %copy-start.42 = (f32[256]{0:T(256)}, f32[256]{0:T(256)S(1)}, u32[]{:S(2)}) copy-start(f32[256]{0:T(256)S(1)} %broadcast_multiply_fusion.1) | copy-start | bytes 3076
  235.1 16.7 %copy-start.46 = (f32[256]{0:T(256)}, f32[256]{0:T(256)S(1)}, u32[]{:S(2)}) copy-start(f32[256]{0:T(256)S(1)} %fusion.85) | copy-start | bytes 3076
  260.3 7.4 copy-start.8
  375.9 19.4 %copy-start.55 = (bf16[2048,2048]{1,0:T(8,128)(2,1)S(1)}, bf16[2048,2048]{1,0:T(8,128)(2,1)}, u32[]{:S(2)}) copy-start(bf16[2048,2048]{1,0:T(8,128)(2,1)} %all-gather.12.cloned.1.call-done) | copy-start | bytes 25165828
  395.3 9.3 copy-start.57
  494.5 83.0 %slice-start.4 = ((s8[8388608]{0:T(1024)(128)(4,1)}), s8[4194304]{0:T(1024)(128)(4,1)S(1)}, s32[]{:S(2)}) async-start(s8[8388608]{0:T(1024)(128)(4,1)} %bitcast.108), calls=%async_computation.27 | async-start | bytes 8388608
  582.3 22.3 %slice-start = ((s8[16777216]{0:T(1024)(128)(4,1)}), s8[4194304]{0:T(1024)(128)(4,1)S(1)}, s32[]{:S(2)}) async-start(s8[16777216]{0:T(1024)(128)(4,1)} %bitcast.106), calls=%async_computation.23 | async-start | bytes 8388608
  582.3 22.3 %slice-start.1 = ((s8[16777216]{0:T(1024)(128)(4,1)}), s8[4194304]{0:T(1024)(128)(4,1)S(1)}, s32[]{:S(2)}) async-start(s8[16777216]{0:T(1024)(128)(4,1)} %bitcast.106), calls=%async_computation.24 | async-start | bytes 8388608
  582.3 22.3 %slice-start.2 = ((s8[16777216]{0:T(1024)(128)(4,1)}), s8[4194304]{0:T(1024)(128)(4,1)S(1)}, s32[]{:S(2)}) async-start(s8[16777216]{0:T(1024)(128)(4,1)} %bitcast.106), calls=%async_computation.25 | async-start | bytes 8388608
  595.8 8.9 slice-start.3
  604.7 10.5 copy-start.9
  620.9 24.2 %copy-start.30 = (f32[2048]{0:T(1024)S(1)}, f32[2048]{0:T(1024)}, u32[]{:S(2)}) copy-start(f32[2048]{0:T(1024)} %copy-done.29) | copy-start | bytes 24580
  620.9 24.2 %copy-start.35 = (f32[2048]{0:T(1024)S(1)}, f32[2048]{0:T(1024)}, u32[]{:S(2)}) copy-start(f32[2048]{0:T(1024)} %copy-done.34) | copy-start | bytes 24580
  620.9 24.2 %copy-start.43 = (f32[256]{0:T(256)S(1)}, f32[256]{0:T(256)}, u32[]{:S(2)}) copy-start(f32[256]{0:T(256)} %copy-done.42) | copy-start | bytes 3076
  620.9 24.2 %copy-start.47 = (f32[256]{0:T(256)S(1)}, f32[256]{0:T(256)}, u32[]{:S(2)}) copy-start(f32[256]{0:T(256)} %copy-done.46) | copy-start | bytes 3076
  646.8 134.9 %reduce-scatter.9.cloned.1.call-start = ((), (), s32[]{:S(2)}) async-start(), calls=%async_computation.15 | async-start | bytes 9437184 | tf_op jit(solution)/shard_map/reduce_scatter | solution.py:786
  657.5 216.4 %reduce-scatter.19.cloned.1.call-start = ((), (), s32[]{:S(2)}) async-start(), calls=%async_computation.20 | async-start | bytes 9437184 | tf_op jit(solution)/shard_map/reduce_scatter | solution.py:786
  665.6 229.8 %reduce-scatter.17.cloned.1.call-start = ((), (), s32[]{:S(2)}) async-start(), calls=%async_computation.19 | async-start | bytes 163840 | tf_op jit(solution)/shard_map/reduce_scatter | solution.py:791
  680.5 364.2 %reduce-scatter.13.cloned.1.call-start = ((), (), s32[]{:S(2)}) async-start(), calls=%async_computation.17 | async-start | bytes 9437184 | tf_op jit(solution)/shard_map/reduce_scatter | solution.py:786
  694.9 352.4 %reduce-scatter.23.cloned.1.call-start = ((), (), s32[]{:S(2)}) async-start(), calls=%async_computation.22 | async-start | bytes 9437184 | tf_op jit(solution)/shard_map/reduce_scatter | solution.py:786
  724.2 44.3 %copy-start.53 = (s32[1,2,8,128]{3,1,2,0:T(2,128)S(1)}, s32[1,2,8,128]{3,1,2,0:T(2,128)}, u32[]{:S(2)}) copy-start(s32[1,2,8,128]{3,1,2,0:T(2,128)} %copy-done.52) | copy-start | bytes 24580
  776.9 119.8 %all-to-all-start.1 = ((bf16[8,256,1024]{2,1,0:T(8,128)(2,1)}), bf16[8,256,1024]{2,1,0:T(8,128)(2,1)}, u32[]{:S(2)}, u32[]{:S(2)}) async-start(bf16[8,256,1024]{2,1,0:T(8,128)(2,1)} %bitcast.117), calls=%async_computation.1 | async-start | bytes 8388608 | tf_op jit(solution)/shard_map/all_to_all | solution.py:630
  781.6 115.1 %copy-start.51 = (s32[1,2,8,128]{3,1,2,0:T(2,128)S(1)}, s32[1,2,8,128]{3,1,2,0:T(2,128)}, u32[]{:S(2)}) copy-start(s32[1,2,8,128]{3,1,2,0:T(2,128)} %copy-done.50) | copy-start | bytes 24580
  781.6 291.1 %reduce-scatter.11.cloned.1.call-start = ((), (), s32[]{:S(2)}) async-start(), calls=%async_computation.16 | async-start | bytes 1310720 | tf_op jit(solution)/shard_map/reduce_scatter | solution.py:791
  782.2 318.6 %reduce-scatter.21.cloned.1.call-start = ((), (), s32[]{:S(2)}) async-start(), calls=%async_computation.21 | async-start | bytes 1310720 | tf_op jit(solution)/shard_map/reduce_scatter | solution.py:791
  1044.1 59.8 %copy-start.44 = (f32[2048]{0:T(1024)S(1)}, f32[2048]{0:T(1024)}, u32[]{:S(2)}) copy-start(f32[2048]{0:T(1024)} %get-tuple-element.31) | copy-start | bytes 24580
  1044.1 59.8 %copy-start.45 = (f32[2048]{0:T(1024)S(1)}, f32[2048]{0:T(1024)}, u32[]{:S(2)}) copy-start(f32[2048]{0:T(1024)} %get-tuple-element.35) | copy-start | bytes 24580
  1044.1 80.0 %copy-start.32 = (f32[22656]{0:T(1024)S(1)}, f32[22656]{0:T(1024)}, u32[]{:S(2)}) copy-start(f32[22656]{0:T(1024)} %param.41) | copy-start | bytes 271876
  1044.1 80.0 %copy-start.37 = (f32[22656]{0:T(1024)S(1)}, f32[22656]{0:T(1024)}, u32[]{:S(2)}) copy-start(f32[22656]{0:T(1024)} %param.42) | copy-start | bytes 271876
  1044.1 80.0 %copy-start.38 = (f32[22656]{0:T(1024)S(1)}, f32[22656]{0:T(1024)}, u32[]{:S(2)}) copy-start(f32[22656]{0:T(1024)} %param.43) | copy-start | bytes 271876
  1044.1 81.7 %copy-start.5 = (f32[2048,256]{1,0:T(8,128)S(1)}, f32[2048,256]{1,0:T(8,128)}, u32[]{:S(2)}) copy-start(f32[2048,256]{1,0:T(8,128)} %param.38) | copy-start | bytes 6291460
  1047.3 78.6 %copy-start.13 = (bf16[2048,256]{1,0:T(8,128)(2,1)S(1)}, bf16[2048,256]{1,0:T(8,128)(2,1)}, u32[]{:S(2)}) copy-start(bf16[2048,256]{1,0:T(8,128)(2,1)} %reduce-scatter.23.cloned.1.call-done) | copy-start | bytes 3145732
  1125.8 6.2 copy-start.6
  1125.8 6.2 copy-start.12
  1125.8 6.2 copy-start.20
  1125.9 6.2 copy-start.21
  1132.1 6.1 copy-start.19
  (32 other events, 119.5 us)
Sparse Core Ops, SparseCore 0:
  11.6 56.7 all-gather.5
  70.3 88.4 all-gather.7
  160.6 53.5 all-gather.9
  216.6 54.3 all-gather.11
  273.3 55.9 all-gather.13
  646.9 33.5 reduce-scatter.14
  684.0 71.2 reduce-scatter.8
  759.1 114.7 reduce-scatter.18
  876.2 19.1 reduce-scatter.16
  899.1 69.4 reduce-scatter.12
  972.0 71.2 reduce-scatter.22
  1045.6 27.0 reduce-scatter.10
  1075.0 25.7 reduce-scatter.20

commit v2 on v1

v2 whole, which is shorter than its diff:
```python
import functools

import jax
import jax.numpy as jnp
from jax import lax
from jax.experimental import pallas as pl
from jax.experimental.pallas import tpu as pltpu
from jax.sharding import PartitionSpec as P

STEP = 10


beta_one = 0.9
beta_two = 0.95
adam_epsilon = 1e-08
decay_rate = 0.1
clip_level = 1.0
norm_epsilon = 1e-05
rate_matrix = 0.6
rate_attention = 2.4
rate_vector = 0.3
masked_score = -1e30

MESH = pl.DeviceIdType.MESH
IN_PLACE = pl.BlockSpec(memory_space=pl.ANY)
IN_VMEM = pl.BlockSpec(memory_space=pltpu.VMEM)
DMA = pltpu.SemaphoreType.DMA
MIB = 2**20


def mul_plain(left, right):
    return jnp.dot(left, right, preferred_element_type=jnp.float32)


def mul_right_t(left, right):
    return lax.dot_general(
        left, right, (((1,), (1,)), ((), ())), preferred_element_type=jnp.float32
    )


def mul_left_t(left, right):
    return lax.dot_general(
        left, right, (((0,), (0,)), ((), ())), preferred_element_type=jnp.float32
    )


def layer_norm(values, scaling, offset):
    average = jnp.mean(values, axis=-1, keepdims=True)
    centered = values - average
    variance = jnp.mean(centered * centered, axis=-1, keepdims=True)
    return centered * lax.rsqrt(variance + norm_epsilon) * scaling + offset


def gelu_tanh(values):
    return jax.nn.gelu(values, approximate=True)


def exclusive_sum(table, axis_index):
    return jnp.cumsum(table, axis=axis_index) - table


def segment_ids(seq_lengths, row_count):
    position = jnp.arange(row_count, dtype=jnp.int32)
    starts = jnp.cumsum(seq_lengths) - seq_lengths
    segment = jnp.sum((starts[None, :] <= position[:, None]).astype(jnp.int32), axis=1)
    return (segment, position)


def slot_matrix(starts, amounts, slots, row_count):
    offsets = jnp.arange(slots, dtype=jnp.int32)
    picked = jnp.where(offsets[None, :] < amounts[:, None], starts[:, None] + offsets[None, :], -1)
    position = jnp.arange(row_count, dtype=jnp.int32)
    return (picked.reshape(-1)[:, None] == position[None, :]).astype(jnp.bfloat16)


def adamw_step(weight, moment, square, gradient, rate):
    moment_new = beta_one * moment + (1.0 - beta_one) * gradient
    square_new = beta_two * square + (1.0 - beta_two) * gradient * gradient
    moment_hat = moment_new / (1.0 - beta_one**STEP)
    square_hat = square_new / (1.0 - beta_two**STEP)
    weight_new = weight - rate * (
        moment_hat / (jnp.sqrt(square_hat) + adam_epsilon) + decay_rate * weight
    )
    return (weight_new, moment_new, square_new)


def remote(src, dst, send_sem, recv_sem, device):
    return pltpu.make_async_remote_copy(
        src, dst, send_sem, recv_sem, device_id=device, device_id_type=MESH
    )


class Place:
    def __init__(self, n_dp, n):
        self.n, self.chips = n, n_dp // 2
        self.dp, self.t = lax.axis_index("dp"), lax.axis_index("tensor")
        self.core, chip = lax.rem(self.dp, 2), lax.div(self.dp, 2)
        side = round(self.chips**0.5)
        self.side = side if side * side == self.chips else self.chips
        self.pos = self.snake(chip)
        self.sign = 2 * self.core - 1
        self.sibling = (self.dp + 1 - 2 * self.core, self.t)
        self.after = (self.block(self.ring(self.pos - self.sign), self.core), self.t)
        self.before = (self.block(self.ring(self.pos + self.sign), self.core), self.t)
        self.left, self.right = (self.dp, self.t - 1), (self.dp, self.t + 1)

    def snake(self, index):
        row, col = lax.div(index, self.side), lax.rem(index, self.side)
        odd = lax.rem(row, 2)
        return row * self.side + col + odd * (self.side - 1 - 2 * col)

    def ring(self, pos):
        return lax.rem(pos + 2 * self.chips, self.chips)

    def block(self, pos, core):
        return self.snake(pos) * 2 + core

    def behind(self, steps, core):
        return self.block(self.ring(self.pos + (2 * core - 1) * steps), core)

    def greet(self, line=False, line_all=False, ring=False):
        barrier = pltpu.get_barrier_semaphore()
        peers = 0

        def call(device):
            pl.semaphore_signal(barrier, inc=1, device_id=device, device_id_type=MESH)

        if ring:
            for device in (self.sibling, self.after, self.before):
                call(device)
            peers += 3
        if line_all:
            for k in range(1, self.n):
                call((self.dp, lax.rem(self.t + k, self.n)))
            peers += self.n - 1
        elif line:
            pl.when(self.t > 0)(lambda: call(self.left))
            pl.when(self.t < self.n - 1)(lambda: call(self.right))
            peers += (self.t > 0).astype(jnp.int32) + (self.t < self.n - 1).astype(jnp.int32)
        pl.semaphore_wait(barrier, peers)


class LineGather:
    @staticmethod
    def sems(n, chunks):
        return [DMA((n - 1, chunks))] * 4 + [DMA]

    def __init__(self, at, chunks, first, place, sems, whole, unit=1.0):
        self.unit = unit
        self.at, self.chunks, self.first, self.place, self.sems = at, chunks, first, place, sems
        self.own = pltpu.make_async_copy(whole[0], whole[1], sems[4])

    def copy(self, h, c, right):
        at = self.at
        dst = self.place(at.t - h if right else at.t + h, c)
        src = self.first(c) if h == 0 else dst
        s, r = self.sems[0:2] if right else self.sems[2:4]
        return remote(src, dst, s.at[h, c], r.at[h, c], at.right if right else at.left)

    def receive(self, h, c, right):
        at = self.at
        dst = self.place(at.t - 1 - h if right else at.t + 1 + h, c)
        s, r = self.sems[0:2] if right else self.sems[2:4]
        remote(dst, dst, s.at[h, c], r.at[h, c], at.left if right else at.right).wait_recv()

    def sends(self, h, right):
        t, n = self.at.t, self.at.n
        return (t >= h) & (t < n - 1) if right else (t + h <= n - 1) & (t > 0)

    def gets(self, h, right):
        return self.at.t - 1 - h >= 0 if right else self.at.t + 1 + h <= self.at.n - 1

    def every(self):
        for h in range(self.at.n - 1):
            for c in range(self.chunks):
                for right in (True, False):
                    yield h, c, right

    def start(self):
        for h, c, right in self.every():
            if h == 0:
                pl.when(self.sends(h, right))(lambda: self.copy(h, c, right).start())
        self.own.start()

    def step(self, h, c, right):
        pl.when(self.gets(h, right))(lambda: self.receive(h, c, right))
        if h + 1 < self.at.n - 1:
            pl.when(self.sends(h + 1, right))(lambda: self.copy(h + 1, c, right).start())

    def steps(self):
        return [
            (self.unit * (which[0] + (which[1] + 1) / self.chunks), functools.partial(self.step, *which))
            for which in self.every()
        ]

    def finish(self):
        self.own.wait()
        for h, c, right in self.every():
            pl.when(self.sends(h, right))(lambda: self.copy(h, c, right).wait_send())


class LineScatter:
    @staticmethod
    def scratch(n, chunks, block, dtype):
        return [pltpu.VMEM((n - 1, *block), dtype)] * 2 + [DMA((n - 1, chunks))] * 4

    def __init__(self, at, chunks, own, out, scratch, unit=1.0):
        self.unit = unit
        self.at, self.chunks, self.own, self.out = at, chunks, own, out
        self.held, self.sems = scratch[:2], scratch[2:6]
        self.rows = self.held[0].shape[1] // chunks

    def parts(self, k, c, right):
        side = 0 if right else 1
        s, r = self.sems[2 * side : 2 * side + 2]
        return self.held[side].at[k, pl.ds(c * self.rows, self.rows)], s.at[k, c], r.at[k, c]

    def send(self, k, c, right, first):
        slot, s, r = self.parts(k, c, right)
        src = self.own(self.target(k, right), c) if first else slot
        return remote(src, slot, s, r, self.at.right if right else self.at.left)

    def receive(self, k, c, right):
        slot, s, r = self.parts(k, c, right)
        remote(slot, slot, s, r, self.at.left if right else self.at.right).wait_recv()

    def target(self, k, right):
        return self.at.n - 1 - k if right else k

    def every(self):
        for k in range(self.at.n - 1):
            for c in range(self.chunks):
                for right in (True, False):
                    yield k, c, right

    def start(self):
        t, n = self.at.t, self.at.n
        for k, c, right in self.every():
            first = (t == (0 if right else n - 1)) & (t != self.target(k, right))
            pl.when(first)(lambda: self.send(k, c, right, True).start())

    def add(self, k, c, right):
        self.receive(k, c, right)
        slot = self.parts(k, c, right)[0]
        mine = self.own(self.target(k, right), c)[...]
        slot[...] = (slot[...].astype(jnp.float32) + mine.astype(jnp.float32)).astype(slot.dtype)
        self.send(k, c, right, False).start()

    def step(self, k, c, right):
        t, n, d = self.at.t, self.at.n, self.target(k, right)
        passes = (t > 0) & (t < d) if right else (t < n - 1) & (t > d)
        pl.when(passes)(lambda: self.add(k, c, right))

    def steps(self):
        return [
            (self.unit * (which[0] + (which[1] + 1) / self.chunks), functools.partial(self.step, *which))
            for which in self.every()
        ]

    def finish(self):
        t, n = self.at.t, self.at.n
        for k, c, right in self.every():
            pl.when(t == self.target(k, right))(lambda: self.receive(k, c, right))
        for c in range(self.chunks):
            span = pl.ds(c * self.rows, self.rows)
            self.out[span] = self.own(t, c)[...].astype(self.out.dtype)

        def more(block):
            self.out[...] += block[...].astype(self.out.dtype)

        pl.when(t > 0)(lambda: more(self.held[0].at[n - 1 - t]))
        pl.when(t < n - 1)(lambda: more(self.held[1].at[t]))
        for k, c, right in self.every():
            d = self.target(k, right)
            pl.when(t < d if right else t > d)(lambda: self.send(k, c, right, False).wait_send())


class RingGather:
    @staticmethod
    def sems(chips, chunks):
        return [DMA((chips - 1, chunks))] * 2 + [DMA((chips, chunks))] * 2 + [DMA]

    def __init__(self, at, chunks, first, place, sems, whole, unit=1.0):
        self.unit = unit
        self.at, self.chunks, self.first, self.place, self.sems = at, chunks, first, place, sems
        self.own = pltpu.make_async_copy(whole[0], whole[1], sems[4])

    def held(self, h, c):
        return self.place(self.at.behind(h, self.at.core), c)

    def onward(self, h, c):
        src = self.first(c) if h == 0 else self.held(h, c)
        s, r = self.sems[0:2]
        return remote(src, self.held(h, c), s.at[h, c], r.at[h, c], self.at.after)

    def across(self, h, c):
        src = self.first(c) if h == 0 else self.held(h, c)
        s, r = self.sems[2:4]
        return remote(src, self.held(h, c), s.at[h, c], r.at[h, c], self.at.sibling)

    def start(self):
        for c in range(self.chunks):
            self.onward(0, c).start()
        for c in range(self.chunks):
            self.across(0, c).start()
        self.own.start()

    def step(self, h, c):
        dst = self.held(h + 1, c)
        s, r = self.sems[0:2]
        remote(dst, dst, s.at[h, c], r.at[h, c], self.at.before).wait_recv()
        if h + 1 < self.at.chips - 1:
            self.onward(h + 1, c).start()
        self.across(h + 1, c).start()

    def steps(self):
        return [
            (self.unit * (h + (c + 1) / self.chunks), functools.partial(self.step, h, c))
            for h in range(self.at.chips - 1)
            for c in range(self.chunks)
        ]

    def finish(self):
        self.own.wait()
        s, r = self.sems[2:4]
        for h in range(self.at.chips):
            for c in range(self.chunks):
                dst = self.place(self.at.behind(h, 1 - self.at.core), c)
                remote(dst, dst, s.at[h, c], r.at[h, c], self.at.sibling).wait_recv()
                self.across(h, c).wait_send()
                if h < self.at.chips - 1:
                    self.onward(h, c).wait_send()


class RingScatter:
    @staticmethod
    def scratch(chips, chunks, block, dtype):
        return (
            [pltpu.VMEM((chips, *block), dtype)] * 2
            + [pltpu.VMEM((chips - 1, *block), dtype)]
            + [DMA((chips, chunks))] * 3
            + [DMA((chips - 1, chunks))] * 2
        )

    def __init__(self, at, chunks, source, out, scratch, unit=1.0):
        self.unit = unit
        self.at, self.chunks, self.source, self.out = at, chunks, source, out
        self.mine, self.other, self.held = scratch[:3]
        self.load_sem, self.s1, self.r1, self.s2, self.r2 = scratch[3:8]
        self.rows = self.held.shape[1] // chunks

    def span(self, c):
        return pl.ds(c * self.rows, self.rows)

    def target(self, s, core):
        return self.at.behind(s + 1, core)

    def load(self, s, c):
        src = self.source(self.target(s, self.at.core), c)
        return pltpu.make_async_copy(src, self.mine.at[s, self.span(c)], self.load_sem.at[s, c])

    def across(self, s, c):
        src = self.source(self.target(s, 1 - self.at.core), c)
        dst = self.other.at[s, self.span(c)]
        return remote(src, dst, self.s1.at[s, c], self.r1.at[s, c], self.at.sibling)

    def onward(self, s, c):
        src, dst = self.mine.at[s, self.span(c)], self.held.at[s, self.span(c)]
        return remote(src, dst, self.s2.at[s, c], self.r2.at[s, c], self.at.after)

    def every(self):
        return [(s, c) for s in range(self.at.chips) for c in range(self.chunks)]

    def start(self):
        for s, c in self.every():
            self.across(s, c).start()
            self.load(s, c).start()

    def step(self, s, c):
        self.load(s, c).wait()
        self.across(s, c).wait_recv()
        total = self.mine[s, self.span(c)].astype(jnp.float32)
        total += self.other[s, self.span(c)].astype(jnp.float32)
        if s > 0:
            dst = self.held.at[s - 1, self.span(c)]
            remote(
                dst, dst, self.s2.at[s - 1, c], self.r2.at[s - 1, c], self.at.before
            ).wait_recv()
            total += self.held[s - 1, self.span(c)].astype(jnp.float32)
        if s < self.at.chips - 1:
            self.mine[s, self.span(c)] = total.astype(self.mine.dtype)
            self.onward(s, c).start()
        else:
            self.out[self.span(c)] = total.astype(self.out.dtype)

    def steps(self):
        return [
            (self.unit * (max(s - 1, -0.5) + (c + 1) / self.chunks), functools.partial(self.step, s, c))
            for s, c in self.every()
        ]

    def finish(self):
        for s, c in self.every():
            self.across(s, c).wait_send()
            if s < self.at.chips - 1:
                self.onward(s, c).wait_send()


class LineSwitch:
    @staticmethod
    def sems(n):
        return [DMA((n - 1,))] * 2 + [DMA]

    def __init__(self, at, source, target, sems):
        self.own = pltpu.make_async_copy(source(at.t), target, sems[2])
        self.copies = []
        for k in range(1, at.n):
            p = lax.rem(at.t + k, at.n)
            self.copies.append(
                remote(source(p), target, sems[0].at[k - 1], sems[1].at[k - 1], (at.dp, p))
            )

    def start(self):
        for copy in self.copies:
            copy.start()
        self.own.start()

    def steps(self):
        return []

    def finish(self):
        self.own.wait()
        for copy in self.copies:
            copy.wait()


def run_jobs(jobs):
    for job in jobs:
        job.start()
    ordered = []
    for i, job in enumerate(jobs):
        ordered += [(when, i, j, step) for j, (when, step) in enumerate(job.steps())]
    for _, _, _, step in sorted(ordered, key=lambda entry: entry[:3]):
        step()
    for job in jobs:
        job.finish()


def rows_of(ref, step):
    return lambda c: ref.at[pl.ds(c * step, step)]


def lanes(index, count):
    return pl.ds(pl.multiple_of(index * count, count), count)


def move(kernel, inputs, in_vmem, outs, out_vmem, scratch, collective_id, name):
    return pl.pallas_call(
        kernel,
        out_shape=tuple(outs),
        in_specs=[IN_VMEM if i < in_vmem else IN_PLACE for i in range(len(inputs))],
        out_specs=tuple(IN_VMEM if i < out_vmem else IN_PLACE for i in range(len(outs))),
        scratch_shapes=scratch,
        compiler_params=pltpu.CompilerParams(
            collective_id=collective_id, has_side_effects=True, vmem_limit_bytes=56 * MIB
        ),
        name=name,
    )(*inputs)


def line_gather(at, x, out, axis, chunks, sems, unit=1.0):
    rows, cols = x.shape
    step = rows // chunks
    if axis == 0:
        place = lambda b, c: out.at[pl.ds(b * rows + c * step, step)]
        whole = out.at[pl.ds(at.t * rows, rows)]
    else:
        place = lambda b, c: out.at[pl.ds(c * step, step), lanes(b, cols)]
        whole = out.at[:, lanes(at.t, cols)]
    return LineGather(at, chunks, rows_of(x, step), place, sems, (x, whole), unit)


def ring_gather(at, x, out, axis, chunks, sems, unit=1.0):
    rows, cols = x.shape
    step = rows // chunks
    if axis == 0:
        place = lambda b, c: out.at[pl.ds(b * rows + c * step, step)]
        whole = out.at[pl.ds(at.dp * rows, rows)]
    else:
        place = lambda b, c: out.at[pl.ds(c * step, step), lanes(b, cols)]
        whole = out.at[:, lanes(at.dp, cols)]
    return RingGather(at, chunks, rows_of(x, step), place, sems, (x, whole), unit)


def blocks_of(x, out, axis, chunks):
    rows, cols = out.shape
    step = rows // chunks
    if axis == 0:
        return lambda b, c: x.at[pl.ds(pl.multiple_of(b * rows + c * step, step), step)]
    return lambda b, c: x.at[pl.ds(c * step, step), lanes(b, cols)]


def line_scatter(at, x, out, axis, chunks, scratch, unit=1.0):
    return LineScatter(at, chunks, blocks_of(x, out, axis, chunks), out, scratch, unit)


def ring_scatter(at, x, out, axis, chunks, scratch, unit=1.0):
    return RingScatter(at, chunks, blocks_of(x, out, axis, chunks), out, scratch, unit)


def like(x, rows, cols, dtype=None):
    return jax.ShapeDtypeStruct((x.shape[0] * rows, x.shape[1] * cols), dtype or x.dtype)


def fold(x, parts):
    rows, cols = x.shape[0], x.shape[1] // parts
    if cols % 128 == 0:
        return x, 1
    return x.reshape(rows, parts, cols).swapaxes(0, 1).reshape(parts * rows * cols // 128, 128), 0


def unfold(x, rows, parts):
    if x.shape[0] == rows:
        return x
    cols = x.size // rows // parts
    return x.reshape(parts, rows, cols).swapaxes(0, 1).reshape(rows, parts * cols)


def like_over(x, parts, axis):
    return like(x, parts, 1) if axis == 0 else like(x, 1, parts)


def part_of(x, parts, axis):
    return (x.shape[0] // parts, x.shape[1]) if axis == 0 else (x.shape[0], x.shape[1] // parts)


def gather_lines(n_dp, n, query, shared):
    def kernel(a, b, a_out, b_out, *sems):
        at = Place(n_dp, n)
        at.greet(line=True)
        run_jobs(
            [
                line_gather(at, a, a_out, 1, 1, sems[0:5]),
                line_gather(at, b, b_out, 0, 1, sems[5:10]),
            ]
        )

    return move(
        kernel,
        (query, shared),
        0,
        (like(query, 1, n), like(shared, n, 1)),
        0,
        LineGather.sems(n, 1) * 2,
        1,
        "gather_lines",
    )


def rows_and_weights(n_dp, n, owned, project, query, shared):
    chips, chunks = n_dp // 2, 2
    total, cols = owned.shape
    rows = total // n

    def kernel(x, p, a, b, x_out, p_out, a_out, b_out, *sems):
        at = Place(n_dp, n)
        at.greet(line_all=True, ring=True)
        run_jobs(
            [
                LineSwitch(
                    at,
                    lambda p: x.at[pl.ds(pl.multiple_of(p * rows, rows), rows)],
                    x_out.at[:, lanes(at.t, cols)],
                    sems[0:3],
                ),
                ring_gather(at, a, a_out, 0, chunks, sems[3:8], 11.0),
                ring_gather(at, b, b_out, 0, 1, sems[8:13], 11.0),
                line_gather(at, p, p_out, 0, 1, sems[13:18], 12.0),
            ]
        )

    return move(
        kernel,
        (owned, project, query, shared),
        0,
        (
            jax.ShapeDtypeStruct((rows, n * cols), owned.dtype),
            like(project, n, 1),
            like(query, n_dp, 1),
            like(shared, n_dp, 1),
        ),
        0,
        LineSwitch.sems(n)
        + RingGather.sems(chips, chunks)
        + RingGather.sems(chips, 1)
        + LineGather.sems(n, 1),
        2,
        "rows_and_weights",
    )


def shared_and_project(n_dp, n, shared_rows, project):
    chips, chunks = n_dp // 2, 2
    tall = project.shape[0]
    project, axis = fold(project, 1)

    def kernel(x, a, x_out, a_out, *sems):
        at = Place(n_dp, n)
        at.greet(line=True, ring=True)
        run_jobs(
            [
                line_gather(at, x, x_out, 0, 1, sems[0:5], 4.0),
                ring_gather(at, a, a_out, axis, chunks, sems[5:10], 11.0),
            ]
        )

    rows, full = move(
        kernel,
        (shared_rows, project),
        0,
        (like(shared_rows, n, 1), like_over(project, n_dp, axis)),
        0,
        LineGather.sems(n, 1) + RingGather.sems(chips, chunks),
        3,
        "shared_and_project",
    )
    return rows, unfold(full, tall, n_dp)


def rows_and_expanded(n_dp, n, x, expand, shrink):
    chips, chunks, halves = n_dp // 2, 4, 2
    tall = shrink.shape[0]
    shrink, axis = fold(shrink, 1)

    def kernel(x_ref, a, b, x_out, a_out, b_out, *sems):
        at = Place(n_dp, n)
        at.greet(line=True, ring=True)
        run_jobs(
            [
                line_gather(at, x_ref, x_out, 0, chunks, sems[0:5], 22.0),
                ring_gather(at, a, a_out, 0, halves, sems[5:10], 22.0),
                ring_gather(at, b, b_out, axis, halves, sems[10:15], 22.0),
            ]
        )

    rows, expand_full, shrink_full = move(
        kernel,
        (x, expand, shrink),
        0,
        (like(x, n, 1), like(expand, n_dp, 1), like_over(shrink, n_dp, axis)),
        0,
        LineGather.sems(n, chunks) + RingGather.sems(chips, halves) * 2,
        4,
        "rows_and_expanded",
    )
    return rows, expand_full, unfold(shrink_full, tall, n_dp)


def scatter_expanded(n_dp, n, x, expand, shrink):
    chips, chunks = n_dp // 2, 4
    block = (x.shape[0] // n, x.shape[1])
    tall = shrink.shape[0]
    shrink, axis = fold(shrink, n_dp)
    a_block = (expand.shape[0] // n_dp, expand.shape[1])
    b_block = part_of(shrink, n_dp, axis)

    def kernel(x_ref, a, b, x_out, a_out, b_out, *scratch):
        at = Place(n_dp, n)
        at.greet(line=True, ring=True)
        run_jobs(
            [
                line_scatter(at, x_ref, x_out, 0, chunks, scratch[0:6], 20.0),
                ring_scatter(at, a, a_out, 0, chunks, scratch[6:14], 24.0),
                ring_scatter(at, b, b_out, axis, chunks, scratch[14:22], 24.0),
            ]
        )

    rows, expand_part, shrink_part = move(
        kernel,
        (x, expand, shrink),
        1,
        [jax.ShapeDtypeStruct(shape, jnp.float32) for shape in (block, a_block, b_block)],
        3,
        LineScatter.scratch(n, chunks, block, x.dtype)
        + RingScatter.scratch(chips, chunks, a_block, x.dtype)
        + RingScatter.scratch(chips, chunks, b_block, x.dtype),
        5,
        "scatter_expanded",
    )
    return rows, expand_part, shrink_part.reshape(tall, -1)


def scatter_shared(n_dp, n, x, project):
    chips, chunks = n_dp // 2, 4
    block = (x.shape[0] // n, x.shape[1])
    tall = project.shape[0]
    project, axis = fold(project, n_dp)
    a_block = part_of(project, n_dp, axis)

    def kernel(x_ref, a, x_out, a_out, *scratch):
        at = Place(n_dp, n)
        at.greet(line=True, ring=True)
        run_jobs(
            [
                line_scatter(at, x_ref, x_out, 0, 1, scratch[0:6], 4.0),
                ring_scatter(at, a, a_out, axis, chunks, scratch[6:14], 11.0),
            ]
        )

    rows, part = move(
        kernel,
        (x, project),
        1,
        (jax.ShapeDtypeStruct(block, jnp.float32), jax.ShapeDtypeStruct(a_block, x.dtype)),
        2,
        LineScatter.scratch(n, 1, block, x.dtype)
        + RingScatter.scratch(chips, chunks, a_block, x.dtype),
        6,
        "scatter_shared",
    )
    return rows, part.reshape(tall, -1)


def cols_and_grads(n_dp, n, rows, project, query, shared):
    chips, chunks = n_dp // 2, 4
    count, width = rows.shape
    cols = width // n
    p_block = (project.shape[0] // n, project.shape[1])
    a_block = (query.shape[0] // n_dp, query.shape[1])
    b_block = (shared.shape[0] // n_dp, shared.shape[1])

    def kernel(p, x, a, b, p_out, a_out, b_out, x_out, *scratch):
        at = Place(n_dp, n)
        at.greet(line_all=True, ring=True)
        run_jobs(
            [
                LineSwitch(
                    at,
                    lambda p: x.at[:, lanes(p, cols)],
                    x_out.at[pl.ds(at.t * count, count)],
                    scratch[0:3],
                ),
                line_scatter(at, p, p_out, 0, 1, scratch[3:9], 12.0),
                ring_scatter(at, a, a_out, 0, chunks, scratch[9:17], 11.0),
                ring_scatter(at, b, b_out, 0, 1, scratch[17:25], 11.0),
            ]
        )

    return move(
        kernel,
        (project, rows, query, shared),
        1,
        [
            jax.ShapeDtypeStruct(p_block, jnp.float32),
            jax.ShapeDtypeStruct(a_block, query.dtype),
            jax.ShapeDtypeStruct(b_block, query.dtype),
            jax.ShapeDtypeStruct((n * count, cols), rows.dtype),
        ],
        3,
        LineSwitch.sems(n)
        + LineScatter.scratch(n, 1, p_block, project.dtype)
        + RingScatter.scratch(chips, chunks, a_block, query.dtype)
        + RingScatter.scratch(chips, 1, b_block, query.dtype),
        7,
        "cols_and_grads",
    )


def scatter_grads(n_dp, n, query, shared):
    a_block = (query.shape[0], query.shape[1] // n)
    b_block = (shared.shape[0] // n, shared.shape[1])

    def kernel(a, b, a_out, b_out, *scratch):
        at = Place(n_dp, n)
        at.greet(line=True)
        run_jobs(
            [
                line_scatter(at, a, a_out, 1, 1, scratch[0:6]),
                line_scatter(at, b, b_out, 0, 1, scratch[6:12]),
            ]
        )

    return move(
        kernel,
        (query, shared),
        2,
        [jax.ShapeDtypeStruct(block, jnp.float32) for block in (a_block, b_block)],
        2,
        LineScatter.scratch(n, 1, a_block, query.dtype)
        + LineScatter.scratch(n, 1, b_block, query.dtype),
        8,
        "scatter_grads",
    )


def sum_all_kernel(n_dp, n, x_ref, o_ref, from_z, from_dp, part, s1, r1, s2, r2, s3, r3):
    g, t = lax.axis_index("dp"), lax.axis_index("tensor")
    rows = x_ref.shape[0] // n
    barrier = pltpu.get_barrier_semaphore()
    for k in range(1, n):
        pl.semaphore_signal(
            barrier, inc=1, device_id=(g, lax.rem(t + k, n)), device_id_type=MESH
        )
    for k in range(1, n_dp):
        pl.semaphore_signal(
            barrier, inc=1, device_id=(lax.rem(g + k, n_dp), t), device_id_type=MESH
        )
    pl.semaphore_wait(barrier, n - 1 + n_dp - 1)

    def piece(p):
        return pl.ds(pl.multiple_of(p * rows, rows), rows)

    first = []
    for k in range(1, n):
        p = lax.rem(t + k, n)
        first.append(
            pltpu.make_async_remote_copy(
                x_ref.at[piece(p)],
                from_z.at[k - 1],
                s1.at[k - 1],
                r1.at[k - 1],
                device_id=(g, p),
                device_id_type=MESH,
            )
        )
    for copy in first:
        copy.start()
    for copy in first:
        copy.wait()
    total = x_ref[piece(t)]
    for k in range(1, n):
        total = total + from_z[k - 1]
    part[...] = total
    second = []
    for k in range(1, n_dp):
        second.append(
            pltpu.make_async_remote_copy(
                part,
                from_dp.at[g],
                s2.at[k - 1],
                r2.at[k - 1],
                device_id=(lax.rem(g + k, n_dp), t),
                device_id_type=MESH,
            )
        )
    for copy in second:
        copy.start()
    from_dp[g] = part[...]
    for copy in second:
        copy.wait()
    total = from_dp[0]
    for k in range(1, n_dp):
        total = total + from_dp[k]
    o_ref[piece(t)] = total
    third = []
    for k in range(1, n):
        third.append(
            pltpu.make_async_remote_copy(
                o_ref.at[piece(t)],
                o_ref.at[piece(t)],
                s3.at[k - 1],
                r3.at[k - 1],
                device_id=(g, lax.rem(t + k, n)),
                device_id_type=MESH,
            )
        )
    for copy in third:
        copy.start()
    for copy in third:
        copy.wait()


def sum_all(x, n_dp, n, collective_id):
    rows = x.shape[0] // n
    return pl.pallas_call(
        functools.partial(sum_all_kernel, n_dp, n),
        out_shape=jax.ShapeDtypeStruct(x.shape, x.dtype),
        in_specs=[IN_VMEM],
        out_specs=IN_VMEM,
        scratch_shapes=[
            pltpu.VMEM((n - 1, rows, 128), x.dtype),
            pltpu.VMEM((n_dp, rows, 128), x.dtype),
            pltpu.VMEM((rows, 128), x.dtype),
        ]
        + [DMA((n - 1,))] * 2
        + [DMA((n_dp - 1,))] * 2
        + [DMA((n - 1,))] * 2,
        compiler_params=pltpu.CompilerParams(collective_id=collective_id, has_side_effects=True),
        name="sum_all",
    )(x)


def local(
    tokens,
    cotangent,
    lengths,
    counts,
    query_weight,
    query_moment,
    query_square,
    shared_weight,
    shared_moment,
    shared_square,
    project_weight,
    project_moment,
    project_square,
    expand_weight,
    expand_moment,
    expand_square,
    shrink_weight,
    shrink_moment,
    shrink_square,
    vectors_value,
    vectors_moment,
    vectors_square,
):
    device = lax.axis_index("dp")
    n_dp = lax.axis_size("dp")
    t = lax.axis_index("tensor")
    n = lax.axis_size("tensor")
    row_count, width = tokens.shape
    slots = 2 * row_count // n_dp
    part_rows, part_cols = row_count // n, width // n
    send_start = lax.dynamic_index_in_dim(exclusive_sum(counts, 1), device, 0, keepdims=False)
    send_amount = lax.dynamic_index_in_dim(counts, device, 0, keepdims=False)
    recv_start = lax.dynamic_index_in_dim(exclusive_sum(counts, 0), device, 1, keepdims=False)
    recv_amount = lax.dynamic_index_in_dim(counts, device, 1, keepdims=False)
    send_slots = slot_matrix(send_start, send_amount, slots, row_count)
    recv_slots = slot_matrix(recv_start, recv_amount, slots, row_count)

    def low(x):
        return x.astype(jnp.bfloat16)

    def pack(rows, out_slots):
        return low(mul_plain(out_slots, rows)).reshape(n_dp, slots, rows.shape[1])

    def exchange(packed):
        return lax.all_to_all(packed, "dp", split_axis=0, concat_axis=0, tiled=True)

    def unpack(arrived, in_slots):
        return low(mul_left_t(in_slots, arrived.reshape(n_dp * slots, arrived.shape[2])))

    mine_cols = [
        lax.dynamic_slice_in_dim(a, t * part_cols, part_cols, 1) for a in (tokens, cotangent)
    ]
    packed, query_low, project_low, shared_low = lax.optimization_barrier(
        (
            pack(jnp.concatenate(mine_cols, axis=1), send_slots),
            low(query_weight),
            low(project_weight),
            low(shared_weight),
        )
    )
    query_line, shared_line = gather_lines(n_dp, n, query_low, shared_low)
    owned = unpack(exchange(packed), recv_slots)
    owned_rows, project_line, query_all, shared_all = rows_and_weights(
        n_dp, n, owned[:, :part_cols], project_low, query_line, shared_line
    )
    owned_grad = lax.all_gather(owned[:, part_cols:], "tensor", axis=1, tiled=True)

    head_size = shared_all.shape[1] // 2
    heads = width // head_size
    hidden_width = expand_weight.shape[1]
    hidden_total = hidden_width * n
    gain_one = vectors_value[0:width]
    shift_one = vectors_value[width : 2 * width]
    gain_two = vectors_value[2 * width : 3 * width]
    shift_two = vectors_value[3 * width : 4 * width]
    query_bias = vectors_value[4 * width : 5 * width]
    project_bias = vectors_value[5 * width : 6 * width]
    shrink_bias = vectors_value[6 * width : 7 * width]
    expand_bias = lax.dynamic_slice_in_dim(
        vectors_value, 7 * width + t * hidden_width, hidden_width, 0
    )
    value_bias = vectors_value[7 * width + hidden_total : 7 * width + hidden_total + head_size]

    inputs_float = owned_rows.astype(jnp.float32)
    normed_one, norm_one_back = jax.vjp(layer_norm, inputs_float, gain_one, shift_one)
    normed_low = normed_one.astype(jnp.bfloat16)
    queries = (mul_plain(normed_low, query_all) + query_bias).astype(jnp.bfloat16)
    shared_out = mul_plain(normed_low, shared_all) + jnp.concatenate(
        [jnp.zeros((head_size,), jnp.float32), value_bias]
    )
    shared_rows, project_all = shared_and_project(
        n_dp, n, shared_out.astype(jnp.bfloat16), project_line
    )
    key_rows, value_rows = shared_rows[:, :head_size], shared_rows[:, head_size:]
    query_heads = queries.reshape(part_rows, heads, head_size)
    segment, position = segment_ids(lengths[0], row_count)
    my_segment = lax.dynamic_slice_in_dim(segment, t * part_rows, part_rows, 0)
    my_position = lax.dynamic_slice_in_dim(position, t * part_rows, part_rows, 0)
    allowed = (my_segment[:, None] == segment[None, :]) & (
        my_position[:, None] >= position[None, :]
    )
    score_scale = head_size ** (-0.5)

    def masked_scores():
        scores = (
            jnp.einsum("bhd,kd->hbk", query_heads, key_rows, preferred_element_type=jnp.float32)
            * score_scale
        )
        return jnp.where(allowed[None], scores, masked_score)

    scores = masked_scores()
    row_max = jnp.max(scores, axis=-1, keepdims=True)
    expo = jnp.exp(scores - row_max)
    row_total = jnp.sum(expo, axis=-1, keepdims=True)
    probs = expo / row_total
    heads_out = (
        jnp.einsum(
            "hbk,kd->bhd",
            probs.astype(jnp.bfloat16),
            value_rows,
            preferred_element_type=jnp.float32,
        )
        .reshape(part_rows, width)
        .astype(jnp.bfloat16)
    )
    log_total = row_max + jnp.log(row_total)
    hidden_one = inputs_float + (mul_plain(heads_out, project_all) + project_bias)
    normed_two, norm_two_back = jax.vjp(layer_norm, hidden_one, gain_two, shift_two)

    normed_two_here, owned_grad = lax.optimization_barrier((low(normed_two), owned_grad))
    normed_two_low, expand_cols, shrink_rows = rows_and_expanded(
        n_dp, n, normed_two_here, low(expand_weight), low(shrink_weight)
    )
    expand_pre = mul_plain(normed_two_low, expand_cols) + expand_bias
    activated, gelu_back = jax.vjp(gelu_tanh, expand_pre)
    activated_low = activated.astype(jnp.bfloat16)
    skipped = lax.dynamic_update_slice_in_dim(
        jnp.zeros((row_count, width), jnp.float32), hidden_one + shrink_bias, t * part_rows, 0
    )
    result_part = low(mul_plain(activated_low, shrink_rows) + skipped)
    result_part, owned_grad = lax.optimization_barrier((result_part, owned_grad))
    layer_cols = lax.psum_scatter(result_part, "tensor", scatter_dimension=1, tiled=True)
    shrink_grad = low(mul_left_t(activated_low, owned_grad))
    activated_grad = mul_right_t(owned_grad, shrink_rows)
    expand_pre_grad = gelu_back(activated_grad)[0].astype(jnp.bfloat16)
    expand_grad = low(mul_left_t(normed_two_low, expand_pre_grad))
    expand_bias_grad = jnp.sum(expand_pre_grad.astype(jnp.float32), axis=0)
    normed_two_part = mul_right_t(expand_pre_grad, expand_cols).astype(jnp.bfloat16)

    normed_two_grad, expand_part, shrink_part = scatter_expanded(
        n_dp, n, normed_two_part, expand_grad, shrink_grad
    )
    output_cols = unpack(exchange(pack(layer_cols, recv_slots)), send_slots)
    output_float = lax.dynamic_slice_in_dim(owned_grad, t * part_rows, part_rows, 0).astype(
        jnp.float32
    )
    shrink_bias_grad = jnp.sum(output_float, axis=0)
    hidden_from_norm, gain_two_grad, shift_two_grad = norm_two_back(normed_two_grad)
    hidden_grad = output_float + hidden_from_norm
    branch_grad = hidden_grad.astype(jnp.bfloat16)
    project_bias_grad = jnp.sum(branch_grad.astype(jnp.float32), axis=0)
    project_grad = low(mul_left_t(heads_out, branch_grad))
    heads_grad = (
        mul_right_t(branch_grad, project_all)
        .astype(jnp.bfloat16)
        .reshape(part_rows, heads, head_size)
    )
    probs = jnp.exp(masked_scores() - log_total)
    prob_grad = jnp.einsum(
        "bhd,kd->hbk", heads_grad, value_rows, preferred_element_type=jnp.float32
    )
    score_grad = (
        probs * (prob_grad - jnp.sum(probs * prob_grad, axis=-1, keepdims=True))
    ).astype(jnp.bfloat16)
    query_grad = (
        (
            jnp.einsum("hbk,kd->bhd", score_grad, key_rows, preferred_element_type=jnp.float32)
            * score_scale
        )
        .reshape(part_rows, width)
        .astype(jnp.bfloat16)
    )
    key_grad = (
        jnp.einsum("hbk,bhd->kd", score_grad, query_heads, preferred_element_type=jnp.float32)
        * score_scale
    )
    value_grad = jnp.einsum(
        "hbk,bhd->kd",
        probs.astype(jnp.bfloat16),
        heads_grad,
        preferred_element_type=jnp.float32,
    )
    shared_part, output_cols = lax.optimization_barrier(
        (low(jnp.concatenate([key_grad, value_grad], axis=1)), output_cols)
    )
    shared_grad, project_sum = scatter_shared(n_dp, n, shared_part, project_grad)
    shared_grad = low(shared_grad)
    output_rows = lax.all_gather(output_cols, "tensor", axis=1, tiled=True)
    query_bias_grad = jnp.sum(query_grad.astype(jnp.float32), axis=0)
    query_weight_grad = mul_left_t(normed_low, query_grad)
    normed_one_grad = mul_right_t(query_grad, query_all) + mul_right_t(shared_grad, shared_all)
    inputs_from_norm, gain_one_grad, shift_one_grad = norm_one_back(normed_one_grad)
    input_result = (hidden_grad + inputs_from_norm).astype(jnp.bfloat16)
    shared_weight_grad = mul_left_t(normed_low, shared_grad)
    value_bias_grad = jnp.sum(shared_grad[:, head_size:].astype(jnp.float32), axis=0)

    project_part, query_sum, shared_sum, input_cols = cols_and_grads(
        n_dp, n, input_result, project_sum, low(query_weight_grad), low(shared_weight_grad)
    )
    input_cols, output_rows = lax.optimization_barrier(
        (unpack(exchange(pack(input_cols, recv_slots)), send_slots), output_rows)
    )
    grad_rows = lax.all_gather(input_cols, "tensor", axis=1, tiled=True)
    query_part, shared_piece = scatter_grads(n_dp, n, query_sum, shared_sum)
    output_back = output_rows.astype(jnp.float32)
    token_rms = jnp.sqrt(jnp.mean(output_back * output_back, axis=1))

    split_part = lax.dynamic_update_slice_in_dim(
        jnp.zeros((hidden_total,), jnp.float32), expand_bias_grad, t * hidden_width, 0
    )
    vector_part = jnp.concatenate(
        [
            gain_one_grad,
            shift_one_grad,
            gain_two_grad,
            shift_two_grad,
            query_bias_grad,
            project_bias_grad,
            shrink_bias_grad,
            split_part,
            value_bias_grad,
        ]
    )
    local_squares = (
        jnp.sum(query_part * query_part)
        + jnp.sum(expand_part * expand_part)
        + jnp.sum(shared_piece * shared_piece)
        + jnp.sum(project_part * project_part)
        + jnp.sum(shrink_part * shrink_part)
    )
    length = vector_part.shape[0]
    unit = n * 8 * 128
    padded = -(-(length + 1) // unit) * unit
    everything = jnp.concatenate(
        [vector_part, local_squares[None], jnp.zeros((padded - length - 1,), jnp.float32)]
    )
    summed = sum_all(everything.reshape(padded // 128, 128), n_dp, n, 9).reshape(padded)
    vector_grad, weight_squares = summed[:length], summed[length]
    grad_size = jnp.sqrt(weight_squares + jnp.sum(vector_grad * vector_grad))
    clip_factor = jnp.minimum(1.0, clip_level / (grad_size + 1e-06))
    clipped_vectors = clip_factor * vector_grad
    query_new = adamw_step(
        query_weight,
        query_moment,
        query_square,
        clip_factor * query_part,
        rate_matrix * width ** (-0.5),
    )
    shared_new = adamw_step(
        shared_weight,
        shared_moment,
        shared_square,
        clip_factor * shared_piece,
        rate_attention * width ** (-0.5),
    )
    project_new = adamw_step(
        project_weight,
        project_moment,
        project_square,
        clip_factor * project_part,
        rate_attention * width ** (-0.5),
    )
    expand_new = adamw_step(
        expand_weight,
        expand_moment,
        expand_square,
        clip_factor * expand_part,
        rate_matrix * width ** (-0.5),
    )
    shrink_new = adamw_step(
        shrink_weight,
        shrink_moment,
        shrink_square,
        clip_factor * shrink_part,
        rate_matrix * hidden_total ** (-0.5),
    )
    vectors_new = adamw_step(
        vectors_value, vectors_moment, vectors_square, clipped_vectors, rate_vector
    )
    return (
        output_rows,
        grad_rows,
        grad_size,
        *query_new,
        *shared_new,
        *project_new,
        *expand_new,
        *shrink_new,
        *vectors_new,
        clipped_vectors,
        token_rms,
    )


def solution(mesh):
    by_rows = P("dp", None)
    query = P("dp", "tensor")
    shared = P(("dp", "tensor"), None)
    project = P("tensor", "dp")
    return jax.shard_map(
        local,
        mesh=mesh,
        in_specs=(
            *(by_rows,) * 3,
            P(),
            *(query,) * 3,
            *(shared,) * 3,
            *(project,) * 3,
            *(query,) * 3,
            *(project,) * 3,
            *(P(),) * 3,
        ),
        out_specs=(
            *(by_rows,) * 2,
            P(),
            *(query,) * 3,
            *(shared,) * 3,
            *(project,) * 3,
            *(query,) * 3,
            *(project,) * 3,
            *(P(),) * 4,
            P("dp"),
        ),
        check_vma=False,
    )
```

time: 1160 us -> 994 us (0.86)
  waiting for transfers between devices: 240 us -> 27.6 us
  blocking collectives: 0 us -> 29.8 us
    reduce_scatter x8 -> x1, waiting for transfers between devices: 175 us -> 0.01 us  [local(): lax.psum_scatter(result_part, 'tensor', scatter_dimension=1, tiled=True)]
    all_to_all x2, waiting for transfers between devices: 64.6 us -> 27.5 us  [exchange(): return lax.all_to_all(packed, 'dp', split_axis=0, concat_axis=0, tiled=True)]
    all_to_all x0 -> x1, blocking collectives: none -> 29.8 us  [exchange(): return lax.all_to_all(packed, 'dp', split_axis=0, concat_axis=0, tiled=True)]
    pallas_call x1, Pallas kernels: 15.5 us -> 29.2 us  [sum_all(): pl.pallas_call(functools.partial(sum_all_kernel, n_dp, n), out_shape=jax....]
    pallas_call x10 -> x8, Pallas kernels: 567 us -> 559 us  [move(): pl.pallas_call(kernel, out_shape=tuple(outs), in_specs=[IN_VMEM if i < in...]
    dot_general x7 -> x8, matrix products: 62 us -> 58.9 us  [mul_left_t(): lax.dot_general(left, right, (((0,), (0,)), ((), ())), preferred_element_...]
    dot_general x7 -> x8, matrix products: 60.1 us -> 57.6 us  [mul_plain(): return jnp.dot(left, right, preferred_element_type=jnp.float32)]
  transfers between devices with their start and end apart: 15 -> 6, of which waited for: 6 -> 2; matrix products, arithmetic and copies ran while one was open for 15% -> 20% of each run, Pallas kernels for 34% -> 44%
where the time goes in v2:
time: 994 us; the launch traced here: 985 us
  Pallas kernels  588 us (59%)
  matrix products  207 us (21%)
  other arithmetic  77.1 us (8%)
  blocking collectives  29.8 us (3%)
  waiting for transfers between devices  27.6 us (3%)
  local copies, waits for them, and re-layouts  23.3 us (2%)
  between operations  20.8 us (2%)
  starting transfers between devices  10.7 us (1%)
    pallas_call x8, Pallas kernels, move(): pl.pallas_call(kernel, out_shape=tuple(outs), in_specs=[IN_VMEM if i < in...  559 us
    dot_general x8, matrix products, mul_left_t(): lax.dot_general(left, right, (((0,), (0,)), ((), ())), preferred_element_...  58.9 us
    dot_general x8, matrix products, mul_plain(): return jnp.dot(left, right, preferred_element_type=jnp.float32)  57.6 us
    dot_general x5, matrix products, mul_right_t(): lax.dot_general(left, right, (((1,), (1,)), ((), ())), preferred_element_...  44.6 us
    all_to_all x1, blocking collectives, exchange(): return lax.all_to_all(packed, 'dp', split_axis=0, concat_axis=0, tiled=True)  29.8 us
    pallas_call x1, Pallas kernels, sum_all(): pl.pallas_call(functools.partial(sum_all_kernel, n_dp, n), out_shape=jax....  29.2 us
    all_to_all x2, waiting for transfers between devices, exchange(): return lax.all_to_all(packed, 'dp', split_axis=0, concat_axis=0, tiled=True)  27.5 us
  transfers between devices with their start and end apart: 6, of which 2 were waited for; matrix products, arithmetic and copies ran while one was open for 20% of the time, Pallas kernels for 44%

profile of v2, /device:TPU:0, one launch (start us, length us, event | category | flops | bytes accessed | tf_op | source)
XLA Modules:
  0.0 984.8 jit_solution(15241112031647521002)
XLA Ops:
  16.9 6.1 fusion.28
  23.0 5.3 all-to-all-start
  32.0 26.0 %gather_lines.1 = (bf16[256,2048]{1,0:T(8,128)(2,1)}, bf16[256,256]{1,0:T(8,128)(2,1)}) custom-call(bf16[256,512]{1,0:T(8,128)(2,1)} %convert_element_type.144.a, bf16[64,256]{1,0:T(8,128)(2,1)} %convert_element_type.146.b), custom_call_target="tpu_custom_call" | custom-call | tf_op jit(solution)/shard_map/gather_lines/pallas_call | solution.py:458
  58.3 19.2 %all-to-all-done = bf16[8,256,1024]{2,1,0:T(8,128)(2,1)} async-done(((bf16[8,256,1024]{2,1,0:T(8,128)(2,1)}), bf16[8,256,1024]{2,1,0:T(8,128)(2,1)}, u32[]{:S(2)}, u32[]{:S(2)}) %all-to-all-start) | async-done | bytes 4194336 | tf_op jit(solution)/shard_map/all_to_all | solution.py:938
  77.6 6.9 fusion.48
  85.9 57.6 %rows_and_weights.1 = (bf16[256,2048]{1,0:T(8,128)(2,1)}, bf16[2048,256]{1,0:T(8,128)(2,1)}, bf16[2048,2048]{1,0:T(8,128)(2,1)}, bf16[2048,256]{1,0:T(8,128)(2,1)}) custom-call(bf16[1024,512]{1,0:T(8,128)(2,1)} %get-tuple-element.126.x, bf16[512,256]{1,0:T(8,128)(2,1)} %convert_element_type.145.p, bf16[256,2048]{1,0:T(8,128)(2,1)} %get-tuple-element.61.a, ...), custom_call_target="tpu_custom_call" | custom-call | tf_op jit(solution)/shard_map/rows_and_weights/pallas_call | solution.py:458
  147.0 6.7 fusion.35
  155.3 2.8 fusion.61.x
  158.1 53.9 %shared_and_project.1 = (bf16[1024,256]{1,0:T(8,128)(2,1)}, bf16[2048,2048]{1,0:T(8,128)(2,1)}) custom-call(bf16[256,256]{1,0:T(8,128)(2,1)} %fusion.61.x, bf16[2048,256]{1,0:T(8,128)(2,1)} %get-tuple-element.65.a), custom_call_target="tpu_custom_call" | custom-call | tf_op jit(solution)/shard_map/shared_and_project/pallas_call | solution.py:458
  212.0 8.2 fusion.100
  220.2 8.2 fusion.3
  228.4 7.7 fusion.49
  236.1 6.2 fusion.101
  244.1 98.9 %rows_and_expanded.1 = (bf16[1024,2048]{1,0:T(8,128)(2,1)}, bf16[2048,2048]{1,0:T(8,128)(2,1)}, bf16[2048,2048]{1,0:T(8,128)(2,1)}) custom-call(bf16[256,2048]{1,0:T(8,128)(2,1)} %add_convert_fusion.1.x_ref, bf16[256,2048]{1,0:T(8,128)(2,1)} %convert_element_type.157.a, bf16[2048,256]{1,0:T(8,128)(2,1)} %convert_element_type.158.b), custom_call_target="tpu_custom_call" | custom-call | tf_op jit(solution)/shard_map/rows_and_expanded/pallas_call | solution.py:458
  343.1 14.7 %fusion.102 = f32[1024,2048]{1,0:T(8,128)} fusion(bf16[1024,2048]{1,0:T(8,128)(2,1)} %get-tuple-element.70, bf16[2048,2048]{1,0:T(8,128)(2,1)} %get-tuple-element.71), kind=kOutput, calls=%fused_computation.177 | convolution fusion | flops 8589934592 | bytes 20971520 | tf_op jit(solution)/shard_map/dot_general | solution.py:32
  357.7 12.4 %fusion.82 = f32[1024,2048]{1,0:T(8,128)S(1)} fusion(bf16[2048,2048]{1,0:T(8,128)(2,1)S(1)} %copy-done.53, f32[1024,2048]{1,0:T(8,128)} %fusion.102, f32[2048]{0:T(1024)S(1)} %get-tuple-element.128), kind=kOutput, calls=%fused_computation.169 | convolution fusion | flops 8610906112 | bytes 25174016 | tf_op jit(solution)/shard_map/dot_general | solution.py:32
  370.7 2.7 convert_element_type.160
  373.3 19.8 %convert_reduce_fusion = (f32[2048]{0:T(1024)}, bf16[1024,2048]{1,0:T(8,128)(2,1)S(1)}) fusion(f32[1024,2048]{1,0:T(8,128)} %fusion.102, f32[2048]{0:T(1024)S(1)} %get-tuple-element.128, bf16[1024,2048]{1,0:T(8,128)(2,1)} %all-gather.4.cloned.1.call-done, bf16[2048,2048]{1,0:T(8,128)(2,1)} %get-tuple-element.72), kind=kOutput, calls=%fused_computation.22 | convolution fusion | flops 8638167040 | bytes 25182208 | tf_op jit(solution)/shard_map/dot_general | solution.py:36
  395.1 11.4 %convolution_convert_fusion.3.a = bf16[2048,2048]{1,0:T(8,128)(2,1)} fusion(bf16[1024,2048]{1,0:T(8,128)(2,1)S(1)} %copy-done.54, bf16[1024,2048]{1,0:T(8,128)(2,1)S(1)} %get-tuple-element.118), kind=kOutput, calls=%fused_computation.37 | convolution fusion | flops 8594128896 | bytes 16777216 | tf_op jit(solution)/shard_map/dot_general | solution.py:42
  406.6 14.4 %convolution_convert_fusion.4.x_ref = bf16[1024,2048]{1,0:T(8,128)(2,1)} fusion(bf16[1024,2048]{1,0:T(8,128)(2,1)} %copy-done.56, bf16[2048,2048]{1,0:T(8,128)(2,1)} %get-tuple-element.71), kind=kOutput, calls=%fused_computation.44 | convolution fusion | flops 8592031744 | bytes 16777216 | tf_op jit(solution)/shard_map/dot_general | solution.py:36
  421.0 18.4 %convolution_convert_fusion.2.b = bf16[2048,2048]{1,0:T(8,128)(2,1)} fusion(bf16[1024,2048]{1,0:T(8,128)(2,1)S(1)} %copy-done.28, f32[1024,2048]{1,0:T(8,128)} %fusion.102, f32[2048]{0:T(1024)S(1)} %get-tuple-element.128), kind=kOutput, calls=%fused_computation.36 | convolution fusion | flops 8615100416 | bytes 20979712 | tf_op jit(solution)/shard_map/dot_general | solution.py:42
  439.4 110.2 %scatter_expanded.1 = (f32[256,2048]{1,0:T(8,128)}, f32[256,2048]{1,0:T(8,128)}, f32[2048,256]{1,0:T(8,128)}) custom-call(bf16[1024,2048]{1,0:T(8,128)(2,1)} %convolution_convert_fusion.4.x_ref, bf16[2048,2048]{1,0:T(8,128)(2,1)} %convolution_convert_fusion.3.a, bf16[2048,2048]{1,0:T(8,128)(2,1)} %convolution_convert_fusion.2.b), custom_call_target="tpu_custom_call" | custom-call | tf_op jit(solution)/shard_map/scatter_expanded/pallas_call | solution.py:458
  549.6 2.4 multiply_reduce_fusion.3
  554.0 6.7 convolution_convert_fusion.6
  562.3 13.4 %fusion = (f32[16,256]{1,0:T(8,128)S(1)}, f32[1024,256,16]{1,0,2:T(8,128)}) fusion(f32[16,256,1024]{1,2,0:T(8,128)} %get-tuple-element.138, f32[16,256]{1,0:T(8,128)S(1)} %log_add_fusion, bf16[256,16,128]{0,2,1:T(8,128)(2,1)S(1)} %bitcast.114, bf16[1024,256]{1,0:T(8,128)(2,1)S(1)} %copy-done.26), kind=kOutput, calls=%fused_computation.2 | convolution fusion | flops 1086320640 | bytes 34897920 | tf_op jit(solution)/shard_map/bhd,kd->hbk/dot_general | solution.py:1062
  578.7 10.3 %fusion.2 = bf16[16,256,1024]{1,2,0:T(8,128)(2,1)} fusion(f32[1024,256,16]{1,0,2:T(8,128)} %get-tuple-element.142, f32[16,256,1024]{1,2,0:T(8,128)S(1)} %bitcast.111, f32[16,256]{1,0:T(8,128)S(1)} %get-tuple-element.141, f32[16,256]{1,0:T(8,128)S(1)} %log_add_fusion), kind=kLoop, calls=%fused_computation.4 | loop fusion | flops 16777216 | bytes 41975808 | tf_op jit(solution)/shard_map/convert_element_type | solution.py:1067
  589.1 4.8 fusion.33
  593.9 4.5 all-to-all-start.1
  598.9 5.9 fusion.60
  604.7 8.3 fusion.57
  613.9 2.9 convert_reduce_fusion.4
  616.8 8.3 all-to-all-done.1
  625.0 5.5 fusion.50
  630.8 5.6 convolution_convert_fusion.1.a
  636.5 5.8 convolution_convert_fusion.a
  644.6 63.3 %scatter_shared.1 = (f32[256,256]{1,0:T(8,128)}, bf16[2048,256]{1,0:T(8,128)(2,1)}) custom-call(bf16[1024,256]{1,0:T(8,128)(2,1)} %pad_maximum_fusion.x_ref, bf16[2048,2048]{1,0:T(8,128)(2,1)} %convolution_convert_fusion.1.a), custom_call_target="tpu_custom_call" | custom-call | tf_op jit(solution)/shard_map/scatter_shared/pallas_call | solution.py:458
  713.4 3.9 convert_reduce_fusion.2
  717.3 62.9 %cols_and_grads.1 = (f32[512,256]{1,0:T(8,128)}, bf16[256,2048]{1,0:T(8,128)(2,1)}, bf16[256,256]{1,0:T(8,128)(2,1)}, bf16[1024,512]{1,0:T(8,128)(2,1)}) custom-call(bf16[2048,256]{1,0:T(8,128)(2,1)} %get-tuple-element.78.p, bf16[256,2048]{1,0:T(8,128)(2,1)} %get-tuple-element.124.x, bf16[2048,2048]{1,0:T(8,128)(2,1)} %convolution_convert_fusion.a, ...), custom_call_target="tpu_custom_call" | custom-call | tf_op jit(solution)/shard_map/cols_and_grads/pallas_call | solution.py:458
  780.3 3.9 fusion.34
  784.1 29.8 %all_to_all.15 = bf16[8,256,512]{2,1,0:T(8,128)(2,1)S(1)} all-to-all(bf16[8,256,512]{2,1,0:T(8,128)(2,1)S(1)} %bitcast.124), channel_id=1, replica_groups=mesh['dp'=8,'tensor'=4] {'dp'}, dimensions={0} | all-to-all | bytes 4194304 | tf_op jit(solution)/shard_map/all_to_all | solution.py:938
  814.0 3.8 fusion.51
  818.1 2.9 multiply_reduce_fusion.2
  822.2 86.1 %scatter_grads.1 = (f32[256,512]{1,0:T(8,128)}, f32[64,256]{1,0:T(8,128)}) custom-call(bf16[256,2048]{1,0:T(8,128)(2,1)} %get-tuple-element.84.a, bf16[256,256]{1,0:T(8,128)(2,1)} %get-tuple-element.85.b), custom_call_target="tpu_custom_call" | custom-call | tf_op jit(solution)/shard_map/scatter_grads/pallas_call | solution.py:458
  917.1 29.2 %sum_all.1 = f32[192,128]{1,0:T(8,128)} custom-call(f32[192,128]{1,0:T(8,128)} %bitcast.127), custom_call_target="tpu_custom_call" | custom-call | tf_op jit(solution)/shard_map/sum_all/pallas_call | solution.py:875
  952.2 2.9 multiply_subtract_fusion.3
  958.7 5.8 multiply_subtract_fusion.1
  964.5 3.7 multiply_subtract_fusion
  969.7 4.9 copy.101
  (213 shorter events, 58.9 us)
Async XLA Ops:
  10.2 6.7 copy-start.48
  23.0 6.1 copy-start.6
  23.0 54.5 %all-to-all-start = ((bf16[8,256,1024]{2,1,0:T(8,128)(2,1)}), bf16[8,256,1024]{2,1,0:T(8,128)(2,1)}, u32[]{:S(2)}, u32[]{:S(2)}) async-start(bf16[8,256,1024]{2,1,0:T(8,128)(2,1)} %bitcast.120), calls=%async_computation | async-start | bytes 8388608 | tf_op jit(solution)/shard_map/all_to_all | solution.py:938
  28.3 215.8 %all-gather.4.cloned.1.call-start = ((), (), s32[]{:S(2)}) async-start(), calls=%async_computation.4 | async-start | bytes 5242880 | tf_op jit(solution)/shard_map/all_gather | solution.py:959
  28.7 48.9 %copy-start.50 = (s32[1,2,8,128]{3,1,2,0:T(2,128)}, s32[1,2,8,128]{3,1,2,0:T(2,128)S(1)}, u32[]{:S(2)}) copy-start(s32[1,2,8,128]{3,1,2,0:T(2,128)S(1)} %copy.96) | copy-start | bytes 24580
  30.9 27.1 %slice-start.6 = ((f32[22656]{0:T(1024)}), f32[128]{0:T(128)S(1)}, s32[]{:S(2)}) async-start(f32[22656]{0:T(1024)} %param.41), calls=%async_computation.14 | async-start | bytes 1024 | tf_op jit(solution)/shard_map/slice | solution.py:975
  30.9 27.1 %copy-start.35 = (f32[22656]{0:T(1024)S(1)}, f32[22656]{0:T(1024)}, u32[]{:S(2)}) copy-start(f32[22656]{0:T(1024)} %param.41) | copy-start | bytes 271876
  58.1 97.2 %copy-start.33 = (f32[2048]{0:T(1024)}, f32[2048]{0:T(1024)S(1)}, u32[]{:S(2)}) copy-start(f32[2048]{0:T(1024)S(1)} %get-tuple-element.134) | copy-start | bytes 24580
  58.1 97.2 %copy-start.38 = (f32[2048]{0:T(1024)}, f32[2048]{0:T(1024)S(1)}, u32[]{:S(2)}) copy-start(f32[2048]{0:T(1024)S(1)} %get-tuple-element.133) | copy-start | bytes 24580
  145.1 10.2 %copy-start.42 = (f32[256]{0:T(256)}, f32[256]{0:T(256)S(1)}, u32[]{:S(2)}) copy-start(f32[256]{0:T(256)S(1)} %broadcast_multiply_fusion.1) | copy-start | bytes 3076
  146.7 7.0 copy-start.46
  146.7 8.6 copy-start.44
  146.8 442.3 %reduce-scatter.2.cloned.1.call-start = ((), (), s32[]{:S(2)}) async-start(), calls=%async_computation.5 | async-start | bytes 5242880 | tf_op jit(solution)/shard_map/reduce_scatter | solution.py:1035
  155.3 56.7 %copy-start.14 = (bf16[256,2048]{0,1:T(8,128)(2,1)}, bf16[256,2048]{0,1:T(8,128)(2,1)S(1)}, u32[]{:S(2)}) copy-start(bf16[256,2048]{0,1:T(8,128)(2,1)S(1)} %copy.93) | copy-start | bytes 3145732
  220.2 8.2 copy-start.25
  236.1 6.2 copy-start.12
  343.1 14.7 %copy-start.53 = (bf16[2048,2048]{1,0:T(8,128)(2,1)S(1)}, bf16[2048,2048]{1,0:T(8,128)(2,1)}, u32[]{:S(2)}) copy-start(bf16[2048,2048]{1,0:T(8,128)(2,1)} %get-tuple-element.72) | copy-start | bytes 25165828
  373.3 21.8 %copy-start.54 = (bf16[1024,2048]{1,0:T(8,128)(2,1)S(1)}, bf16[1024,2048]{1,0:T(8,128)(2,1)}, u32[]{:S(2)}) copy-start(bf16[1024,2048]{1,0:T(8,128)(2,1)} %get-tuple-element.70) | copy-start | bytes 12582916
  406.6 14.4 %copy-start.28 = (bf16[1024,2048]{1,0:T(8,128)(2,1)S(1)}, bf16[1024,2048]{1,0:T(8,128)(2,1)}, u32[]{:S(2)}) copy-start(bf16[1024,2048]{1,0:T(8,128)(2,1)} %all-gather.4.cloned.1.call-done) | copy-start | bytes 12582916
  562.3 13.5 %slice-start = ((s8[16777216]{0:T(1024)(128)(4,1)}), s8[4194304]{0:T(1024)(128)(4,1)S(1)}, s32[]{:S(2)}) async-start(s8[16777216]{0:T(1024)(128)(4,1)} %bitcast.110), calls=%async_computation.8 | async-start | bytes 8388608
  562.3 13.4 %slice-start.1 = ((s8[16777216]{0:T(1024)(128)(4,1)}), s8[4194304]{0:T(1024)(128)(4,1)S(1)}, s32[]{:S(2)}) async-start(s8[16777216]{0:T(1024)(128)(4,1)} %bitcast.110), calls=%async_computation.9 | async-start | bytes 8388608
  562.3 15.2 %slice-start.2 = ((s8[16777216]{0:T(1024)(128)(4,1)}), s8[4194304]{0:T(1024)(128)(4,1)S(1)}, s32[]{:S(2)}) async-start(s8[16777216]{0:T(1024)(128)(4,1)} %bitcast.110), calls=%async_computation.10 | async-start | bytes 8388608
  562.3 16.4 %slice-start.3 = ((s8[16777216]{0:T(1024)(128)(4,1)}), s8[4194304]{0:T(1024)(128)(4,1)S(1)}, s32[]{:S(2)}) async-start(s8[16777216]{0:T(1024)(128)(4,1)} %bitcast.110), calls=%async_computation.11 | async-start | bytes 8388608
  578.7 10.3 %copy-start.51 = (s32[1,2,8,128]{3,1,2,0:T(2,128)S(1)}, s32[1,2,8,128]{3,1,2,0:T(2,128)}, u32[]{:S(2)}) copy-start(s32[1,2,8,128]{3,1,2,0:T(2,128)} %copy-done.50) | copy-start | bytes 24580
  593.9 31.1 %all-to-all-start.1 = ((bf16[8,256,512]{2,1,0:T(8,128)(2,1)}), bf16[8,256,512]{2,1,0:T(8,128)(2,1)}, u32[]{:S(2)}, u32[]{:S(2)}) async-start(bf16[8,256,512]{2,1,0:T(8,128)(2,1)} %bitcast.123), calls=%async_computation.2 | async-start | bytes 4194304 | tf_op jit(solution)/shard_map/all_to_all | solution.py:938
  598.4 219.4 %all-gather.6.cloned.1.call-start = ((), (), s32[]{:S(2)}) async-start(), calls=%async_computation.6 | async-start | bytes 5242880 | tf_op jit(solution)/shard_map/all_gather | solution.py:1091
  598.9 15.0 %slice-start.4 = ((s8[8388608]{0:T(1024)(128)(4,1)}), s8[4194304]{0:T(1024)(128)(4,1)S(1)}, s32[]{:S(2)}) async-start(s8[8388608]{0:T(1024)(128)(4,1)} %bitcast.112), calls=%async_computation.12 | async-start | bytes 8388608
  604.7 9.1 slice-start.5
  604.7 9.1 copy-start.27
  613.9 11.2 %copy-start.49 = (s32[1,2,8,128]{3,1,2,0:T(2,128)S(1)}, s32[1,2,8,128]{3,1,2,0:T(2,128)}, u32[]{:S(2)}) copy-start(s32[1,2,8,128]{3,1,2,0:T(2,128)} %copy-done.48) | copy-start | bytes 24580
  630.5 5.9 copy-start.1
  630.5 5.9 copy-start.34
  630.5 5.9 copy-start.39
  630.6 5.9 copy-start.43
  630.6 5.9 copy-start.45
  630.6 339.1 %all-gather.8.cloned.1.call-start = ((), (), s32[]{:S(2)}) async-start(), calls=%async_computation.7 | async-start | bytes 5242880 | tf_op jit(solution)/shard_map/all_gather | solution.py:1106
  630.8 11.4 %slice-start.7 = ((s8[8388608]{0:T(1024)(128)(4,1)}), s8[4194304]{0:T(1024)(128)(4,1)S(1)}, s32[]{:S(2)}) async-start(s8[8388608]{0:T(1024)(128)(4,1)} %bitcast.135), calls=%async_computation.15 | async-start | bytes 8388608
  644.6 64.3 %copy-start.29 = (bf16[2048,256]{1,0:T(8,128)(2,1)S(1)}, bf16[2048,256]{1,0:T(8,128)(2,1)}, u32[]{:S(2)}) copy-start(bf16[2048,256]{1,0:T(8,128)(2,1)} %get-tuple-element.64) | copy-start | bytes 3145732
  821.1 92.4 %copy-start.20 = (f32[512,256]{1,0:T(8,128)S(1)}, f32[512,256]{1,0:T(8,128)}, u32[]{:S(2)}) copy-start(f32[512,256]{1,0:T(8,128)} %get-tuple-element.89) | copy-start | bytes 1572868
  821.1 129.4 %copy-start.37 = (f32[64,256]{1,0:T(8,128)S(1)}, f32[64,256]{1,0:T(8,128)}, u32[]{:S(2)}) copy-start(f32[64,256]{1,0:T(8,128)} %param.29) | copy-start | bytes 196612
  821.1 129.4 %copy-start.41 = (f32[64,256]{1,0:T(8,128)S(1)}, f32[64,256]{1,0:T(8,128)}, u32[]{:S(2)}) copy-start(f32[64,256]{1,0:T(8,128)} %param.30) | copy-start | bytes 196612
  822.2 130.0 %copy-start.18 = (f32[256,512]{1,0:T(8,128)S(1)}, f32[256,512]{1,0:T(8,128)}, u32[]{:S(2)}) copy-start(f32[256,512]{1,0:T(8,128)} %param.26) | copy-start | bytes 1572868
  913.5 43.0 %copy-start.36 = (f32[22656]{0:T(1024)S(1)}, f32[22656]{0:T(1024)}, u32[]{:S(2)}) copy-start(f32[22656]{0:T(1024)} %param.41) | copy-start | bytes 271876
  947.5 7.6 copy-start.19
  952.2 6.5 copy-start.22
  958.7 5.8 copy-start.9
  958.7 5.8 copy-start.23
  958.7 5.8 copy-start.24
  (24 other events, 90.2 us)
Sparse Core Ops, SparseCore 0:
  146.9 84.3 all-gather.3
  406.7 109.3 reduce-scatter.1
  630.6 102.4 all-gather.5
  817.9 103.0 all-gather.7

commit v3 on v2

--- a/solution.py
+++ b/solution.py
@@ -3,6 +3,7 @@
 import jax
 import jax.numpy as jnp
 from jax import lax
+from jax.experimental.layout import Layout, with_layout_constraint
 from jax.experimental import pallas as pl
 from jax.experimental.pallas import tpu as pltpu
 from jax.sharding import PartitionSpec as P
@@ -20,6 +21,7 @@
 rate_attention = 2.4
 rate_vector = 0.3
 masked_score = -1e30
+longest = 512
 
 MESH = pl.DeviceIdType.MESH
 IN_PLACE = pl.BlockSpec(memory_space=pl.ANY)
@@ -71,6 +73,10 @@
     picked = jnp.where(offsets[None, :] < amounts[:, None], starts[:, None] + offsets[None, :], -1)
     position = jnp.arange(row_count, dtype=jnp.int32)
     return (picked.reshape(-1)[:, None] == position[None, :]).astype(jnp.bfloat16)
+
+
+def turned(x):
+    return with_layout_constraint(x.T, Layout(major_to_minor=(0, 1)))
 
 
 def adamw_step(weight, moment, square, gradient, rate):
@@ -98,10 +104,9 @@
         side = round(self.chips**0.5)
         self.side = side if side * side == self.chips else self.chips
         self.pos = self.snake(chip)
-        self.sign = 2 * self.core - 1
         self.sibling = (self.dp + 1 - 2 * self.core, self.t)
-        self.after = (self.block(self.ring(self.pos - self.sign), self.core), self.t)
-        self.before = (self.block(self.ring(self.pos + self.sign), self.core), self.t)
+        self.after = (self.block(self.ring(self.pos + 1), self.core), self.t)
+        self.before = (self.block(self.ring(self.pos - 1), self.core), self.t)
         self.left, self.right = (self.dp, self.t - 1), (self.dp, self.t + 1)
 
     def snake(self, index):
@@ -114,9 +119,6 @@
 
     def block(self, pos, core):
         return self.snake(pos) * 2 + core
-
-    def behind(self, steps, core):
-        return self.block(self.ring(self.pos + (2 * core - 1) * steps), core)
 
     def greet(self, line=False, line_all=False, ring=False):
         barrier = pltpu.get_barrier_semaphore()
@@ -137,7 +139,7 @@
             pl.when(self.t > 0)(lambda: call(self.left))
             pl.when(self.t < self.n - 1)(lambda: call(self.right))
             peers += (self.t > 0).astype(jnp.int32) + (self.t < self.n - 1).astype(jnp.int32)
-        pl.semaphore_wait(barrier, peers)
+        return lambda: pl.semaphore_wait(barrier, peers)
 
 
 class LineGather:
@@ -176,11 +178,16 @@
                 for right in (True, False):
                     yield h, c, right
 
+    def prepare(self):
+        self.own.start()
+
+    def prepared(self):
+        self.own.wait()
+
     def start(self):
         for h, c, right in self.every():
             if h == 0:
                 pl.when(self.sends(h, right))(lambda: self.copy(h, c, right).start())
-        self.own.start()
 
     def step(self, h, c, right):
         pl.when(self.gets(h, right))(lambda: self.receive(h, c, right))
@@ -194,7 +201,6 @@
         ]
 
     def finish(self):
-        self.own.wait()
         for h, c, right in self.every():
             pl.when(self.sends(h, right))(lambda: self.copy(h, c, right).wait_send())
 
@@ -232,6 +238,12 @@
             for c in range(self.chunks):
                 for right in (True, False):
                     yield k, c, right
+
+    def prepare(self):
+        pass
+
+    def prepared(self):
+        pass
 
     def start(self):
         t, n = self.at.t, self.at.n
@@ -275,135 +287,245 @@
             pl.when(t < d if right else t > d)(lambda: self.send(k, c, right, False).wait_send())
 
 
+class LineExchange:
+    @staticmethod
+    def scratch(n, block, dtype):
+        return [pltpu.VMEM((n - 1, *block), dtype)] + [DMA((n - 1,))] * 2
+
+    def __init__(self, at, source, out, scratch):
+        self.at, self.source, self.out = at, source, out
+        self.held = scratch[0]
+        self.copies = []
+        for k in range(1, at.n):
+            p = lax.rem(at.t + k, at.n)
+            self.copies.append(
+                remote(
+                    source(p),
+                    self.held.at[k - 1],
+                    scratch[1].at[k - 1],
+                    scratch[2].at[k - 1],
+                    (at.dp, p),
+                )
+            )
+
+    def prepare(self):
+        pass
+
+    def prepared(self):
+        pass
+
+    def start(self):
+        for copy in self.copies:
+            copy.start()
+
+    def steps(self):
+        return []
+
+    def finish(self):
+        for copy in self.copies:
+            copy.wait()
+        total = self.source(self.at.t)[...].astype(jnp.float32)
+        for k in range(self.at.n - 1):
+            total = total + self.held[k].astype(jnp.float32)
+        self.out[...] = total.astype(self.out.dtype)
+
+
 class RingGather:
     @staticmethod
     def sems(chips, chunks):
-        return [DMA((chips - 1, chunks))] * 2 + [DMA((chips, chunks))] * 2 + [DMA]
+        hops = chips // 2
+        return [DMA((2, hops, chunks))] * 4 + [DMA((chunks,))] * 2 + [DMA]
 
     def __init__(self, at, chunks, first, place, sems, whole, unit=1.0):
         self.unit = unit
         self.at, self.chunks, self.first, self.place, self.sems = at, chunks, first, place, sems
-        self.own = pltpu.make_async_copy(whole[0], whole[1], sems[4])
-
-    def held(self, h, c):
-        return self.place(self.at.behind(h, self.at.core), c)
-
-    def onward(self, h, c):
-        src = self.first(c) if h == 0 else self.held(h, c)
+        self.hops = at.chips // 2
+        self.own = pltpu.make_async_copy(whole[0], whole[1], sems[6])
+
+    def every(self):
+        for h in range(self.hops):
+            for c in range(self.chunks):
+                for way in (0, 1):
+                    if h < self.hops - 1 or c % 2 == way:
+                        yield h, c, way
+
+    def origin(self, steps, way, core):
+        return self.at.block(self.at.ring(self.at.pos + (steps if way else -steps)), core)
+
+    def onward(self, h, c, way):
+        dst = self.place(self.origin(h, way, self.at.core), c)
+        src = self.first(c) if h == 0 else dst
         s, r = self.sems[0:2]
-        return remote(src, self.held(h, c), s.at[h, c], r.at[h, c], self.at.after)
-
-    def across(self, h, c):
-        src = self.first(c) if h == 0 else self.held(h, c)
+        device = self.at.before if way else self.at.after
+        return remote(src, dst, s.at[way, h, c], r.at[way, h, c], device)
+
+    def arrival(self, h, c, way):
+        dst = self.place(self.origin(h + 1, way, self.at.core), c)
+        s, r = self.sems[0:2]
+        device = self.at.after if way else self.at.before
+        return remote(dst, dst, s.at[way, h, c], r.at[way, h, c], device)
+
+    def across(self, h, c, way, core):
+        dst = self.place(self.origin(h + 1, way, core), c)
         s, r = self.sems[2:4]
-        return remote(src, self.held(h, c), s.at[h, c], r.at[h, c], self.at.sibling)
+        return remote(dst, dst, s.at[way, h, c], r.at[way, h, c], self.at.sibling)
+
+    def across_own(self, c, core):
+        dst = self.place(self.origin(0, 0, core), c)
+        s, r = self.sems[4:6]
+        return remote(self.first(c), dst, s.at[c], r.at[c], self.at.sibling)
+
+    def prepare(self):
+        self.own.start()
+
+    def prepared(self):
+        self.own.wait()
 
     def start(self):
+        for h, c, way in self.every():
+            if h == 0:
+                self.onward(h, c, way).start()
         for c in range(self.chunks):
-            self.onward(0, c).start()
+            self.across_own(c, self.at.core).start()
+
+    def step(self, h, c, way):
+        self.arrival(h, c, way).wait_recv()
+        if (h + 1, c, way) in list(self.every()):
+            self.onward(h + 1, c, way).start()
+        self.across(h, c, way, self.at.core).start()
+
+    def steps(self):
+        when = 0.0
+        for h, c, way in self.every():
+            when += self.unit / self.chunks / 2
+            yield when, functools.partial(self.step, h, c, way)
+
+    def finish(self):
+        other = 1 - self.at.core
         for c in range(self.chunks):
-            self.across(0, c).start()
-        self.own.start()
-
-    def step(self, h, c):
-        dst = self.held(h + 1, c)
-        s, r = self.sems[0:2]
-        remote(dst, dst, s.at[h, c], r.at[h, c], self.at.before).wait_recv()
-        if h + 1 < self.at.chips - 1:
-            self.onward(h + 1, c).start()
-        self.across(h + 1, c).start()
-
-    def steps(self):
-        return [
-            (self.unit * (h + (c + 1) / self.chunks), functools.partial(self.step, h, c))
-            for h in range(self.at.chips - 1)
-            for c in range(self.chunks)
-        ]
-
-    def finish(self):
-        self.own.wait()
-        s, r = self.sems[2:4]
-        for h in range(self.at.chips):
-            for c in range(self.chunks):
-                dst = self.place(self.at.behind(h, 1 - self.at.core), c)
-                remote(dst, dst, s.at[h, c], r.at[h, c], self.at.sibling).wait_recv()
-                self.across(h, c).wait_send()
-                if h < self.at.chips - 1:
-                    self.onward(h, c).wait_send()
+            self.across_own(c, other).wait_recv()
+            self.across_own(c, self.at.core).wait_send()
+        for h, c, way in self.every():
+            self.across(h, c, way, other).wait_recv()
+            self.across(h, c, way, self.at.core).wait_send()
+            self.onward(h, c, way).wait_send()
 
 
 class RingScatter:
     @staticmethod
     def scratch(chips, chunks, block, dtype):
+        hops = chips // 2
         return (
             [pltpu.VMEM((chips, *block), dtype)] * 2
-            + [pltpu.VMEM((chips - 1, *block), dtype)]
+            + [pltpu.VMEM((2, hops, *block), dtype)]
             + [DMA((chips, chunks))] * 3
-            + [DMA((chips - 1, chunks))] * 2
+            + [DMA((2, hops, chunks))] * 2
         )
 
     def __init__(self, at, chunks, source, out, scratch, unit=1.0):
         self.unit = unit
         self.at, self.chunks, self.source, self.out = at, chunks, source, out
+        self.hops = at.chips // 2
         self.mine, self.other, self.held = scratch[:3]
         self.load_sem, self.s1, self.r1, self.s2, self.r2 = scratch[3:8]
-        self.rows = self.held.shape[1] // chunks
+        self.rows = self.held.shape[2] // chunks
 
     def span(self, c):
         return pl.ds(c * self.rows, self.rows)
 
-    def target(self, s, core):
-        return self.at.behind(s + 1, core)
-
-    def load(self, s, c):
-        src = self.source(self.target(s, self.at.core), c)
-        return pltpu.make_async_copy(src, self.mine.at[s, self.span(c)], self.load_sem.at[s, c])
-
-    def across(self, s, c):
-        src = self.source(self.target(s, 1 - self.at.core), c)
-        dst = self.other.at[s, self.span(c)]
-        return remote(src, dst, self.s1.at[s, c], self.r1.at[s, c], self.at.sibling)
-
-    def onward(self, s, c):
-        src, dst = self.mine.at[s, self.span(c)], self.held.at[s, self.span(c)]
-        return remote(src, dst, self.s2.at[s, c], self.r2.at[s, c], self.at.after)
+    def target(self, place, core):
+        return self.at.block(self.at.ring(self.at.pos + place), core)
+
+    def load(self, place, c):
+        src = self.source(self.target(place, self.at.core), c)
+        dst = self.mine.at[place, self.span(c)]
+        return pltpu.make_async_copy(src, dst, self.load_sem.at[place, c])
+
+    def across(self, place, c):
+        src = self.source(self.target(place, 1 - self.at.core), c)
+        dst = self.other.at[place, self.span(c)]
+        return remote(src, dst, self.s1.at[place, c], self.r1.at[place, c], self.at.sibling)
+
+    def sent(self, e, c, way):
+        return e < self.hops or c % 2 == way
+
+    def onward(self, e, c, way):
+        place = self.at.chips - e if way else e
+        src, dst = self.mine.at[place, self.span(c)], self.held.at[way, e - 1, self.span(c)]
+        device = self.at.before if way else self.at.after
+        return remote(src, dst, self.s2.at[way, e - 1, c], self.r2.at[way, e - 1, c], device)
+
+    def arrival(self, e, c, way):
+        dst = self.held.at[way, e, self.span(c)]
+        device = self.at.after if way else self.at.before
+        return remote(dst, dst, self.s2.at[way, e, c], self.r2.at[way, e, c], device)
+
+    def places(self):
+        order = []
+        for e in range(self.hops, 0, -1):
+            order += [e] if e == self.hops else [e, self.at.chips - e]
+        return order + [0]
+
+    def prepare(self):
+        for place in self.places():
+            for c in range(self.chunks):
+                self.load(place, c).start()
+
+    def prepared(self):
+        for place in self.places():
+            for c in range(self.chunks):
+                self.load(place, c).wait()
+
+    def start(self):
+        for place in self.places():
+            for c in range(self.chunks):
+                self.across(place, c).start()
+
+    def base(self, place, c):
+        self.across(place, c).wait_recv()
+        total = self.mine[place, self.span(c)].astype(jnp.float32)
+        return total + self.other[place, self.span(c)].astype(jnp.float32)
+
+    def arrived(self, e, c, way):
+        self.arrival(e, c, way).wait_recv()
+        return self.held[way, e, self.span(c)].astype(jnp.float32)
+
+    def step(self, e, c, way):
+        place = self.at.chips - e if way else e
+        total = self.base(place, c)
+        if e < self.hops and self.sent(e + 1, c, way):
+            total += self.arrived(e, c, way)
+        self.mine[place, self.span(c)] = total.astype(self.mine.dtype)
+        self.onward(e, c, way).start()
+
+    def last(self, c):
+        total = self.base(0, c)
+        for way in (0, 1):
+            if self.sent(1, c, way):
+                total += self.arrived(0, c, way)
+        self.out[self.span(c)] = total.astype(self.out.dtype)
 
     def every(self):
-        return [(s, c) for s in range(self.at.chips) for c in range(self.chunks)]
-
-    def start(self):
-        for s, c in self.every():
-            self.across(s, c).start()
-            self.load(s, c).start()
-
-    def step(self, s, c):
-        self.load(s, c).wait()
-        self.across(s, c).wait_recv()
-        total = self.mine[s, self.span(c)].astype(jnp.float32)
-        total += self.other[s, self.span(c)].astype(jnp.float32)
-        if s > 0:
-            dst = self.held.at[s - 1, self.span(c)]
-            remote(
-                dst, dst, self.s2.at[s - 1, c], self.r2.at[s - 1, c], self.at.before
-            ).wait_recv()
-            total += self.held[s - 1, self.span(c)].astype(jnp.float32)
-        if s < self.at.chips - 1:
-            self.mine[s, self.span(c)] = total.astype(self.mine.dtype)
-            self.onward(s, c).start()
-        else:
-            self.out[self.span(c)] = total.astype(self.out.dtype)
+        for e in range(self.hops, 0, -1):
+            for c in range(self.chunks):
+                for way in (0, 1):
+                    if self.sent(e, c, way):
+                        yield e, c, way
 
     def steps(self):
-        return [
-            (self.unit * (max(s - 1, -0.5) + (c + 1) / self.chunks), functools.partial(self.step, s, c))
-            for s, c in self.every()
-        ]
+        when = 0.0
+        for e, c, way in self.every():
+            yield when, functools.partial(self.step, e, c, way)
+            when += self.unit / self.chunks / 2
+        for c in range(self.chunks):
+            yield when + self.unit * (c + 1) / self.chunks, functools.partial(self.last, c)
 
     def finish(self):
-        for s, c in self.every():
-            self.across(s, c).wait_send()
-            if s < self.at.chips - 1:
-                self.onward(s, c).wait_send()
+        for place in self.places():
+            for c in range(self.chunks):
+                self.across(place, c).wait_send()
+        for e, c, way in self.every():
+            self.onward(e, c, way).wait_send()
 
 
 class LineSwitch:
@@ -420,21 +542,30 @@
                 remote(source(p), target, sems[0].at[k - 1], sems[1].at[k - 1], (at.dp, p))
             )
 
+    def prepare(self):
+        self.own.start()
+
+    def prepared(self):
+        self.own.wait()
+
     def start(self):
         for copy in self.copies:
             copy.start()
-        self.own.start()
 
     def steps(self):
         return []
 
     def finish(self):
-        self.own.wait()
         for copy in self.copies:
             copy.wait()
 
 
-def run_jobs(jobs):
+def run_jobs(met, jobs):
+    for job in jobs:
+        job.prepare()
+    for job in jobs:
+        job.prepared()
+    met()
     for job in jobs:
         job.start()
     ordered = []
@@ -454,7 +585,7 @@
     return pl.ds(pl.multiple_of(index * count, count), count)
 
 
-def move(kernel, inputs, in_vmem, outs, out_vmem, scratch, collective_id, name):
+def move(kernel, inputs, in_vmem, outs, out_vmem, scratch, collective_id, name, aliases=None):
     return pl.pallas_call(
         kernel,
         out_shape=tuple(outs),
@@ -464,6 +595,7 @@
         compiler_params=pltpu.CompilerParams(
             collective_id=collective_id, has_side_effects=True, vmem_limit_bytes=56 * MIB
         ),
+        input_output_aliases=aliases or {},
         name=name,
     )(*inputs)
 
@@ -500,6 +632,11 @@
     return lambda b, c: x.at[pl.ds(c * step, step), lanes(b, cols)]
 
 
+def line_exchange(at, x, out, axis, scratch):
+    block = blocks_of(x, out, axis, 1)
+    return LineExchange(at, lambda p: block(p, 0), out, scratch)
+
+
 def line_scatter(at, x, out, axis, chunks, scratch, unit=1.0):
     return LineScatter(at, chunks, blocks_of(x, out, axis, chunks), out, scratch, unit)
 
@@ -512,285 +649,384 @@
     return jax.ShapeDtypeStruct((x.shape[0] * rows, x.shape[1] * cols), dtype or x.dtype)
 
 
-def fold(x, parts):
-    rows, cols = x.shape[0], x.shape[1] // parts
-    if cols % 128 == 0:
-        return x, 1
-    return x.reshape(rows, parts, cols).swapaxes(0, 1).reshape(parts * rows * cols // 128, 128), 0
-
-
-def unfold(x, rows, parts):
-    if x.shape[0] == rows:
-        return x
-    cols = x.size // rows // parts
-    return x.reshape(parts, rows, cols).swapaxes(0, 1).reshape(rows, parts * cols)
-
-
-def like_over(x, parts, axis):
-    return like(x, parts, 1) if axis == 0 else like(x, 1, parts)
-
-
-def part_of(x, parts, axis):
-    return (x.shape[0] // parts, x.shape[1]) if axis == 0 else (x.shape[0], x.shape[1] // parts)
-
-
-def gather_lines(n_dp, n, query, shared):
-    def kernel(a, b, a_out, b_out, *sems):
+class Parts:
+    def __init__(self, refs):
+        self.refs = list(refs)
+
+    def take(self, shapes):
+        taken, self.refs = self.refs[: len(shapes)], self.refs[len(shapes) :]
+        return taken
+
+
+def gather_lines(n_dp, n, query, project, shared):
+    sems = LineGather.sems(n, 1)
+
+    def kernel(a, b, c, a_out, b_out, c_out, *refs):
+        parts = Parts(refs)
         at = Place(n_dp, n)
-        at.greet(line=True)
         run_jobs(
+            at.greet(line=True),
             [
-                line_gather(at, a, a_out, 1, 1, sems[0:5]),
-                line_gather(at, b, b_out, 0, 1, sems[5:10]),
-            ]
+                line_gather(at, a, a_out, 1, 1, parts.take(sems), 6.0),
+                line_gather(at, c, c_out, 0, 1, parts.take(sems), 6.5),
+                line_gather(at, b, b_out, 1, 1, parts.take(sems), 12.0),
+            ],
         )
 
     return move(
         kernel,
-        (query, shared),
+        (query, project, shared),
+        3,
+        (like(query, 1, n), like(project, 1, n), like(shared, n, 1)),
         0,
-        (like(query, 1, n), like(shared, n, 1)),
-        0,
-        LineGather.sems(n, 1) * 2,
+        sems * 3,
         1,
         "gather_lines",
     )
 
 
-def rows_and_weights(n_dp, n, owned, project, query, shared):
+def rows_and_weights(n_dp, n, owned, query, shared):
     chips, chunks = n_dp // 2, 2
-    total, cols = owned.shape
-    rows = total // n
-
-    def kernel(x, p, a, b, x_out, p_out, a_out, b_out, *sems):
+    total, cols = owned.shape[0], owned.shape[1] // 2
+    rows, half = total // n, total // 2
+    switch, line = LineSwitch.sems(n), LineGather.sems(n, chunks)
+    ring = RingGather.sems(chips, chunks)
+
+    def kernel(x, a, b, x_out, y_out, a_out, b_out, *refs):
+        parts = Parts(refs)
         at = Place(n_dp, n)
-        at.greet(line_all=True, ring=True)
         run_jobs(
+            at.greet(line_all=True, ring=True),
             [
                 LineSwitch(
                     at,
-                    lambda p: x.at[pl.ds(pl.multiple_of(p * rows, rows), rows)],
+                    lambda p: x.at[pl.ds(pl.multiple_of(p * rows, rows), rows), pl.ds(0, cols)],
                     x_out.at[:, lanes(at.t, cols)],
-                    sems[0:3],
+                    parts.take(switch),
                 ),
-                ring_gather(at, a, a_out, 0, chunks, sems[3:8], 11.0),
-                ring_gather(at, b, b_out, 0, 1, sems[8:13], 11.0),
-                line_gather(at, p, p_out, 0, 1, sems[13:18], 12.0),
-            ]
+                ring_gather(at, b, b_out, 0, chunks, parts.take(ring), 4.0),
+                ring_gather(at, a, a_out, 0, chunks, parts.take(ring), 22.0),
+                line_gather(
+                    at,
+                    x.at[pl.ds(0, half), pl.ds(cols, cols)],
+                    y_out.at[pl.ds(0, half)],
+                    1,
+                    chunks,
+                    parts.take(line),
+                    16.0,
+                ),
+            ],
         )
 
     return move(
         kernel,
-        (owned, project, query, shared),
-        0,
+        (owned, query, shared),
+        3,
         (
             jax.ShapeDtypeStruct((rows, n * cols), owned.dtype),
-            like(project, n, 1),
+            jax.ShapeDtypeStruct((total, n * cols), owned.dtype),
             like(query, n_dp, 1),
             like(shared, n_dp, 1),
         ),
         0,
-        LineSwitch.sems(n)
-        + RingGather.sems(chips, chunks)
-        + RingGather.sems(chips, 1)
-        + LineGather.sems(n, 1),
+        switch + ring * 2 + line,
         2,
         "rows_and_weights",
     )
 
 
-def shared_and_project(n_dp, n, shared_rows, project):
+def shared_and_project(n_dp, n, owned, shared_rows, project, gathered):
     chips, chunks = n_dp // 2, 2
-    tall = project.shape[0]
-    project, axis = fold(project, 1)
-
-    def kernel(x, a, x_out, a_out, *sems):
+    total, cols = owned.shape[0], owned.shape[1] // 2
+    half = total // 2
+    small, line = LineGather.sems(n, 1), LineGather.sems(n, chunks)
+    ring = RingGather.sems(chips, chunks)
+
+    def kernel(y, x, a, _, x_out, a_out, y_out, *refs):
+        parts = Parts(refs)
         at = Place(n_dp, n)
-        at.greet(line=True, ring=True)
+        lower = pl.ds(half, half)
         run_jobs(
+            at.greet(line=True, ring=True),
             [
-                line_gather(at, x, x_out, 0, 1, sems[0:5], 4.0),
-                ring_gather(at, a, a_out, axis, chunks, sems[5:10], 11.0),
-            ]
+                line_gather(at, x, x_out, 0, 1, parts.take(small), 4.0),
+                ring_gather(at, a, a_out, 0, chunks, parts.take(ring), 22.0),
+                line_gather(
+                    at,
+                    y.at[lower, pl.ds(cols, cols)],
+                    y_out.at[lower],
+                    1,
+                    chunks,
+                    parts.take(line),
+                    13.0,
+                ),
+            ],
         )
 
-    rows, full = move(
+    return move(
         kernel,
-        (shared_rows, project),
+        (owned, shared_rows, project, gathered),
+        3,
+        (like(shared_rows, n, 1), like(project, n_dp, 1), like(gathered, 1, 1)),
         0,
-        (like(shared_rows, n, 1), like_over(project, n_dp, axis)),
-        0,
-        LineGather.sems(n, 1) + RingGather.sems(chips, chunks),
+        small + ring + line,
         3,
         "shared_and_project",
-    )
-    return rows, unfold(full, tall, n_dp)
+        {3: 2},
+    )
 
 
 def rows_and_expanded(n_dp, n, x, expand, shrink):
     chips, chunks, halves = n_dp // 2, 4, 2
-    tall = shrink.shape[0]
-    shrink, axis = fold(shrink, 1)
-
-    def kernel(x_ref, a, b, x_out, a_out, b_out, *sems):
+    line, ring = LineGather.sems(n, chunks), RingGather.sems(chips, halves)
+
+    def kernel(x_ref, a, b, x_out, a_out, b_out, *refs):
+        parts = Parts(refs)
         at = Place(n_dp, n)
-        at.greet(line=True, ring=True)
         run_jobs(
+            at.greet(line=True, ring=True),
             [
-                line_gather(at, x_ref, x_out, 0, chunks, sems[0:5], 22.0),
-                ring_gather(at, a, a_out, 0, halves, sems[5:10], 22.0),
-                ring_gather(at, b, b_out, axis, halves, sems[10:15], 22.0),
-            ]
+                line_gather(at, x_ref, x_out, 0, chunks, parts.take(line), 22.0),
+                ring_gather(at, a, a_out, 0, halves, parts.take(ring), 44.0),
+                ring_gather(at, b, b_out, 0, halves, parts.take(ring), 44.0),
+            ],
         )
 
-    rows, expand_full, shrink_full = move(
+    return move(
         kernel,
         (x, expand, shrink),
+        3,
+        (like(x, n, 1), like(expand, n_dp, 1), like(shrink, n_dp, 1)),
         0,
-        (like(x, n, 1), like(expand, n_dp, 1), like_over(shrink, n_dp, axis)),
-        0,
-        LineGather.sems(n, chunks) + RingGather.sems(chips, halves) * 2,
+        line + ring * 2,
         4,
         "rows_and_expanded",
     )
-    return rows, expand_full, unfold(shrink_full, tall, n_dp)
 
 
 def scatter_expanded(n_dp, n, x, expand, shrink):
     chips, chunks = n_dp // 2, 4
     block = (x.shape[0] // n, x.shape[1])
-    tall = shrink.shape[0]
-    shrink, axis = fold(shrink, n_dp)
-    a_block = (expand.shape[0] // n_dp, expand.shape[1])
-    b_block = part_of(shrink, n_dp, axis)
-
-    def kernel(x_ref, a, b, x_out, a_out, b_out, *scratch):
+    w_block = (expand.shape[0] // n_dp, expand.shape[1])
+    line = LineScatter.scratch(n, chunks, block, x.dtype)
+    ring = RingScatter.scratch(chips, chunks, w_block, x.dtype)
+
+    def kernel(x_ref, a, b, x_out, a_out, b_out, *refs):
+        parts = Parts(refs)
         at = Place(n_dp, n)
-        at.greet(line=True, ring=True)
         run_jobs(
+            at.greet(line=True, ring=True),
             [
-                line_scatter(at, x_ref, x_out, 0, chunks, scratch[0:6], 20.0),
-                ring_scatter(at, a, a_out, 0, chunks, scratch[6:14], 24.0),
-                ring_scatter(at, b, b_out, axis, chunks, scratch[14:22], 24.0),
-            ]
+                line_scatter(at, x_ref, x_out, 0, chunks, parts.take(line), 26.0),
+                ring_scatter(at, a, a_out, 0, chunks, parts.take(ring), 22.0),
+                ring_scatter(at, b, b_out, 0, chunks, parts.take(ring), 22.0),
+            ],
         )
 
-    rows, expand_part, shrink_part = move(
+    return move(
         kernel,
         (x, expand, shrink),
         1,
-        [jax.ShapeDtypeStruct(shape, jnp.float32) for shape in (block, a_block, b_block)],
+        [jax.ShapeDtypeStruct(shape, jnp.float32) for shape in (block, w_block, w_block)],
         3,
-        LineScatter.scratch(n, chunks, block, x.dtype)
-        + RingScatter.scratch(chips, chunks, a_block, x.dtype)
-        + RingScatter.scratch(chips, chunks, b_block, x.dtype),
+        line + ring * 2,
         5,
         "scatter_expanded",
     )
-    return rows, expand_part, shrink_part.reshape(tall, -1)
-
-
-def scatter_shared(n_dp, n, x, project):
+
+
+def scatter_shared(n_dp, n, x, result, query, project):
     chips, chunks = n_dp // 2, 4
     block = (x.shape[0] // n, x.shape[1])
-    tall = project.shape[0]
-    project, axis = fold(project, n_dp)
-    a_block = part_of(project, n_dp, axis)
-
-    def kernel(x_ref, a, x_out, a_out, *scratch):
+    w_block = (project.shape[0] // n_dp, project.shape[1])
+    small = LineExchange.scratch(n, block, x.dtype)
+    line = LineGather.sems(n, chunks)
+    ring = RingScatter.scratch(chips, chunks, w_block, x.dtype)
+
+    def kernel(x_ref, y, a, b, x_out, a_out, b_out, y_out, *refs):
+        parts = Parts(refs)
         at = Place(n_dp, n)
-        at.greet(line=True, ring=True)
         run_jobs(
+            at.greet(line_all=True, ring=True),
             [
-                line_scatter(at, x_ref, x_out, 0, 1, scratch[0:6], 4.0),
-                ring_scatter(at, a, a_out, axis, chunks, scratch[6:14], 11.0),
-            ]
+                line_exchange(at, x_ref, x_out, 0, parts.take(small)),
+                line_gather(at, y, y_out, 1, chunks, parts.take(line), 22.0),
+                ring_scatter(at, a, a_out, 0, chunks, parts.take(ring), 24.0),
+                ring_scatter(at, b, b_out, 0, chunks, parts.take(ring), 24.0),
+            ],
         )
 
-    rows, part = move(
+    return move(
         kernel,
-        (x, project),
-        1,
-        (jax.ShapeDtypeStruct(block, jnp.float32), jax.ShapeDtypeStruct(a_block, x.dtype)),
+        (x, result, query, project),
         2,
-        LineScatter.scratch(n, 1, block, x.dtype)
-        + RingScatter.scratch(chips, chunks, a_block, x.dtype),
+        (
+            jax.ShapeDtypeStruct(block, jnp.float32),
+            jax.ShapeDtypeStruct(w_block, x.dtype),
+            jax.ShapeDtypeStruct(w_block, x.dtype),
+            like(result, 1, n),
+        ),
+        3,
+        small + line + ring * 2,
         6,
         "scatter_shared",
     )
-    return rows, part.reshape(tall, -1)
-
-
-def cols_and_grads(n_dp, n, rows, project, query, shared):
-    chips, chunks = n_dp // 2, 4
+
+
+def cols_and_shared(n_dp, n, rows, shared):
+    chips = n_dp // 2
     count, width = rows.shape
     cols = width // n
-    p_block = (project.shape[0] // n, project.shape[1])
-    a_block = (query.shape[0] // n_dp, query.shape[1])
-    b_block = (shared.shape[0] // n_dp, shared.shape[1])
-
-    def kernel(p, x, a, b, p_out, a_out, b_out, x_out, *scratch):
+    s_block = (shared.shape[0] // n_dp, shared.shape[1])
+    switch = LineSwitch.sems(n)
+    ring = RingScatter.scratch(chips, 1, s_block, shared.dtype)
+
+    def kernel(x, c, c_out, x_out, *refs):
+        parts = Parts(refs)
         at = Place(n_dp, n)
-        at.greet(line_all=True, ring=True)
         run_jobs(
+            at.greet(line_all=True, ring=True),
             [
                 LineSwitch(
                     at,
                     lambda p: x.at[:, lanes(p, cols)],
                     x_out.at[pl.ds(at.t * count, count)],
-                    scratch[0:3],
+                    parts.take(switch),
                 ),
-                line_scatter(at, p, p_out, 0, 1, scratch[3:9], 12.0),
-                ring_scatter(at, a, a_out, 0, chunks, scratch[9:17], 11.0),
-                ring_scatter(at, b, b_out, 0, 1, scratch[17:25], 11.0),
-            ]
+                ring_scatter(at, c, c_out, 0, 1, parts.take(ring), 4.0),
+            ],
         )
 
     return move(
         kernel,
-        (project, rows, query, shared),
+        (rows, shared),
         1,
         [
-            jax.ShapeDtypeStruct(p_block, jnp.float32),
-            jax.ShapeDtypeStruct(a_block, query.dtype),
-            jax.ShapeDtypeStruct(b_block, query.dtype),
+            jax.ShapeDtypeStruct(s_block, shared.dtype),
             jax.ShapeDtypeStruct((n * count, cols), rows.dtype),
         ],
-        3,
-        LineSwitch.sems(n)
-        + LineScatter.scratch(n, 1, p_block, project.dtype)
-        + RingScatter.scratch(chips, chunks, a_block, query.dtype)
-        + RingScatter.scratch(chips, 1, b_block, query.dtype),
+        1,
+        switch + ring,
         7,
-        "cols_and_grads",
-    )
-
-
-def scatter_grads(n_dp, n, query, shared):
-    a_block = (query.shape[0], query.shape[1] // n)
-    b_block = (shared.shape[0] // n, shared.shape[1])
-
-    def kernel(a, b, a_out, b_out, *scratch):
+        "cols_and_shared",
+    )
+
+
+def scatter_grads(n_dp, n, query, project, shared):
+    w_block = (query.shape[0], query.shape[1] // n)
+    s_block = (shared.shape[0] // n, shared.shape[1])
+    line = LineScatter.scratch(n, 1, w_block, query.dtype)
+    small = LineExchange.scratch(n, s_block, shared.dtype)
+
+    def kernel(a, b, c, a_out, b_out, c_out, *refs):
+        parts = Parts(refs)
         at = Place(n_dp, n)
-        at.greet(line=True)
         run_jobs(
+            at.greet(line_all=True),
             [
-                line_scatter(at, a, a_out, 1, 1, scratch[0:6]),
-                line_scatter(at, b, b_out, 0, 1, scratch[6:12]),
-            ]
+                line_scatter(at, a, a_out, 1, 1, parts.take(line), 12.0),
+                line_scatter(at, b, b_out, 1, 1, parts.take(line), 12.0),
+                line_exchange(at, c, c_out, 0, parts.take(small)),
+            ],
         )
 
     return move(
         kernel,
-        (query, shared),
-        2,
-        [jax.ShapeDtypeStruct(block, jnp.float32) for block in (a_block, b_block)],
-        2,
-        LineScatter.scratch(n, 1, a_block, query.dtype)
-        + LineScatter.scratch(n, 1, b_block, query.dtype),
+        (query, project, shared),
+        3,
+        [jax.ShapeDtypeStruct(block, jnp.float32) for block in (w_block, w_block, s_block)],
+        3,
+        line * 2 + small,
         8,
         "scatter_grads",
     )
+
+
+def product(left, right, left_dim, right_dim):
+    return lax.dot_general(
+        left, right, (((left_dim,), (right_dim,)), ((), ())), preferred_element_type=jnp.float32
+    )
+
+
+def fill_bias(bias, seg_row, seg_col, pos_row, pos_col):
+    @pl.when(pl.program_id(0) == 0)
+    def _():
+        allowed = (seg_row[...] == seg_col[...]) & (pos_row[...] >= pos_col[...])
+        bias[...] = jnp.where(allowed, 0.0, masked_score)
+
+
+def attend_kernel(scale, q, k, v, seg_row, seg_col, pos_row, pos_col, o, log_total, bias):
+    fill_bias(bias, seg_row, seg_col, pos_row, pos_col)
+    scores = product(q[...], k[...], 1, 1) * scale + bias[...]
+    row_max = jnp.max(scores, axis=1, keepdims=True)
+    expo = jnp.exp(scores - row_max)
+    row_total = jnp.sum(expo, axis=1, keepdims=True)
+    probs = (expo / row_total).astype(jnp.bfloat16)
+    o[...] = product(probs, v[...], 1, 0).astype(jnp.bfloat16)
+    log_total[...] = jnp.broadcast_to(row_max + jnp.log(row_total), log_total.shape)
+
+
+def attend_back_kernel(
+    scale, q, do, log_total, k, v, seg_row, seg_col, pos_row, pos_col, dq, dk, dv, bias
+):
+    fill_bias(bias, seg_row, seg_col, pos_row, pos_col)
+
+    @pl.when(pl.program_id(0) == 0)
+    def _():
+        dk[...] = jnp.zeros_like(dk)
+        dv[...] = jnp.zeros_like(dv)
+
+    scores = product(q[...], k[...], 1, 1) * scale + bias[...]
+    probs = jnp.exp(scores - log_total[:, :1])
+    prob_grad = product(do[...], v[...], 1, 1)
+    inner = jnp.sum(probs * prob_grad, axis=1, keepdims=True)
+    score_grad = (probs * (prob_grad - inner)).astype(jnp.bfloat16)
+    dq[...] = (product(score_grad, k[...], 1, 0) * scale).astype(jnp.bfloat16)
+    dk[...] += product(score_grad, q[...], 0, 0) * scale
+    dv[...] += product(probs.astype(jnp.bfloat16), do[...], 0, 0)
+
+
+def attention_specs(rows, keys, size):
+    head = pl.BlockSpec((rows, size), lambda h: (0, h))
+    whole = lambda *shape: pl.BlockSpec(shape, lambda h: (0, 0))
+    masks = [whole(rows, 1), whole(1, keys), whole(rows, 1), whole(1, keys)]
+    return head, whole(keys, size), masks
+
+
+def attend(q, k, v, masks):
+    rows, width = q.shape
+    keys, size = k.shape
+    head, shared, mask_specs = attention_specs(rows, keys, size)
+    return pl.pallas_call(
+        functools.partial(attend_kernel, size**-0.5),
+        grid=(width // size,),
+        in_specs=[head, shared, shared, *mask_specs],
+        out_specs=(head, head),
+        out_shape=(
+            jax.ShapeDtypeStruct(q.shape, jnp.bfloat16),
+            jax.ShapeDtypeStruct(q.shape, jnp.float32),
+        ),
+        scratch_shapes=[pltpu.VMEM((rows, keys), jnp.float32)],
+        compiler_params=pltpu.CompilerParams(vmem_limit_bytes=32 * 2**20),
+        name="attend",
+    )(q, k, v, *masks)
+
+
+def attend_back(q, do, log_total, k, v, masks):
+    rows, width = q.shape
+    keys, size = k.shape
+    head, shared, mask_specs = attention_specs(rows, keys, size)
+    grad = jax.ShapeDtypeStruct((keys, size), jnp.float32)
+    return pl.pallas_call(
+        functools.partial(attend_back_kernel, size**-0.5),
+        grid=(width // size,),
+        in_specs=[head, head, head, shared, shared, *mask_specs],
+        out_specs=(head, shared, shared),
+        out_shape=(jax.ShapeDtypeStruct(q.shape, jnp.bfloat16), grad, grad),
+        scratch_shapes=[pltpu.VMEM((rows, keys), jnp.float32)],
+        compiler_params=pltpu.CompilerParams(vmem_limit_bytes=32 * 2**20),
+        name="attend_back",
+    )(q, do, log_total, k, v, *masks)
 
 
 def sum_all_kernel(n_dp, n, x_ref, o_ref, from_z, from_dp, part, s1, r1, s2, r2, s3, r3):
@@ -943,23 +1179,26 @@
     mine_cols = [
         lax.dynamic_slice_in_dim(a, t * part_cols, part_cols, 1) for a in (tokens, cotangent)
     ]
-    packed, query_low, project_low, shared_low = lax.optimization_barrier(
+    packed, query_here, project_here, shared_here = lax.optimization_barrier(
         (
             pack(jnp.concatenate(mine_cols, axis=1), send_slots),
-            low(query_weight),
-            low(project_weight),
-            low(shared_weight),
+            query_weight,
+            project_weight,
+            shared_weight,
         )
     )
-    query_line, shared_line = gather_lines(n_dp, n, query_low, shared_low)
-    owned = unpack(exchange(packed), recv_slots)
-    owned_rows, project_line, query_all, shared_all = rows_and_weights(
-        n_dp, n, owned[:, :part_cols], project_low, query_line, shared_line
-    )
-    owned_grad = lax.all_gather(owned[:, part_cols:], "tensor", axis=1, tiled=True)
+    query_line, project_line, shared_line = gather_lines(
+        n_dp, n, low(query_here), low(project_here).T, low(shared_here)
+    )
+    arrived, query_line, shared_line = lax.optimization_barrier(
+        (exchange(packed), query_line, shared_line)
+    )
+    owned = unpack(arrived, recv_slots)
+    owned_rows, owned_grad, query_all, shared_all = rows_and_weights(
+        n_dp, n, owned, query_line, shared_line
+    )
 
     head_size = shared_all.shape[1] // 2
-    heads = width // head_size
     hidden_width = expand_weight.shape[1]
     hidden_total = hidden_width * n
     gain_one = vectors_value[0:width]
@@ -981,48 +1220,26 @@
     shared_out = mul_plain(normed_low, shared_all) + jnp.concatenate(
         [jnp.zeros((head_size,), jnp.float32), value_bias]
     )
-    shared_rows, project_all = shared_and_project(
-        n_dp, n, shared_out.astype(jnp.bfloat16), project_line
-    )
-    key_rows, value_rows = shared_rows[:, :head_size], shared_rows[:, head_size:]
-    query_heads = queries.reshape(part_rows, heads, head_size)
+    shared_rows, project_all_t, owned_grad = shared_and_project(
+        n_dp, n, owned, low(shared_out), project_line, owned_grad
+    )
+    window = min(row_count, part_rows + longest)
+    window_start = jnp.clip((t + 1) * part_rows - window, 0, row_count - window)
+    shared_window = lax.dynamic_slice_in_dim(shared_rows, window_start, window, 0)
+    key_rows, value_rows = shared_window[:, :head_size], shared_window[:, head_size:]
     segment, position = segment_ids(lengths[0], row_count)
-    my_segment = lax.dynamic_slice_in_dim(segment, t * part_rows, part_rows, 0)
-    my_position = lax.dynamic_slice_in_dim(position, t * part_rows, part_rows, 0)
-    allowed = (my_segment[:, None] == segment[None, :]) & (
-        my_position[:, None] >= position[None, :]
-    )
-    score_scale = head_size ** (-0.5)
-
-    def masked_scores():
-        scores = (
-            jnp.einsum("bhd,kd->hbk", query_heads, key_rows, preferred_element_type=jnp.float32)
-            * score_scale
-        )
-        return jnp.where(allowed[None], scores, masked_score)
-
-    scores = masked_scores()
-    row_max = jnp.max(scores, axis=-1, keepdims=True)
-    expo = jnp.exp(scores - row_max)
-    row_total = jnp.sum(expo, axis=-1, keepdims=True)
-    probs = expo / row_total
-    heads_out = (
-        jnp.einsum(
-            "hbk,kd->bhd",
-            probs.astype(jnp.bfloat16),
-            value_rows,
-            preferred_element_type=jnp.float32,
-        )
-        .reshape(part_rows, width)
-        .astype(jnp.bfloat16)
-    )
-    log_total = row_max + jnp.log(row_total)
-    hidden_one = inputs_float + (mul_plain(heads_out, project_all) + project_bias)
+    masks = (
+        lax.dynamic_slice_in_dim(segment, t * part_rows, part_rows, 0)[:, None],
+        lax.dynamic_slice_in_dim(segment, window_start, window, 0)[None, :],
+        lax.dynamic_slice_in_dim(position, t * part_rows, part_rows, 0)[:, None],
+        lax.dynamic_slice_in_dim(position, window_start, window, 0)[None, :],
+    )
+    heads_out, log_total = attend(queries, key_rows, value_rows, masks)
+    hidden_one = inputs_float + (mul_right_t(heads_out, project_all_t) + project_bias)
     normed_two, norm_two_back = jax.vjp(layer_norm, hidden_one, gain_two, shift_two)
 
-    normed_two_here, owned_grad = lax.optimization_barrier((low(normed_two), owned_grad))
-    normed_two_low, expand_cols, shrink_rows = rows_and_expanded(
-        n_dp, n, normed_two_here, low(expand_weight), low(shrink_weight)
+    normed_two_low, expand_cols, shrink_rows_t = rows_and_expanded(
+        n_dp, n, low(normed_two), low(expand_weight), low(shrink_weight).T
     )
     expand_pre = mul_plain(normed_two_low, expand_cols) + expand_bias
     activated, gelu_back = jax.vjp(gelu_tanh, expand_pre)
@@ -1030,19 +1247,20 @@
     skipped = lax.dynamic_update_slice_in_dim(
         jnp.zeros((row_count, width), jnp.float32), hidden_one + shrink_bias, t * part_rows, 0
     )
-    result_part = low(mul_plain(activated_low, shrink_rows) + skipped)
+    result_part = low(mul_right_t(activated_low, shrink_rows_t) + skipped)
     result_part, owned_grad = lax.optimization_barrier((result_part, owned_grad))
     layer_cols = lax.psum_scatter(result_part, "tensor", scatter_dimension=1, tiled=True)
-    shrink_grad = low(mul_left_t(activated_low, owned_grad))
-    activated_grad = mul_right_t(owned_grad, shrink_rows)
+    shrink_grad_t = low(mul_left_t(owned_grad, activated_low))
+    activated_grad = mul_plain(owned_grad, shrink_rows_t)
     expand_pre_grad = gelu_back(activated_grad)[0].astype(jnp.bfloat16)
     expand_grad = low(mul_left_t(normed_two_low, expand_pre_grad))
     expand_bias_grad = jnp.sum(expand_pre_grad.astype(jnp.float32), axis=0)
     normed_two_part = mul_right_t(expand_pre_grad, expand_cols).astype(jnp.bfloat16)
 
-    normed_two_grad, expand_part, shrink_part = scatter_expanded(
-        n_dp, n, normed_two_part, expand_grad, shrink_grad
-    )
+    normed_two_grad, expand_part, shrink_part_t = scatter_expanded(
+        n_dp, n, normed_two_part, expand_grad, shrink_grad_t
+    )
+    shrink_part = turned(shrink_part_t)
     output_cols = unpack(exchange(pack(layer_cols, recv_slots)), send_slots)
     output_float = lax.dynamic_slice_in_dim(owned_grad, t * part_rows, part_rows, 0).astype(
         jnp.float32
@@ -1052,59 +1270,39 @@
     hidden_grad = output_float + hidden_from_norm
     branch_grad = hidden_grad.astype(jnp.bfloat16)
     project_bias_grad = jnp.sum(branch_grad.astype(jnp.float32), axis=0)
-    project_grad = low(mul_left_t(heads_out, branch_grad))
-    heads_grad = (
-        mul_right_t(branch_grad, project_all)
-        .astype(jnp.bfloat16)
-        .reshape(part_rows, heads, head_size)
-    )
-    probs = jnp.exp(masked_scores() - log_total)
-    prob_grad = jnp.einsum(
-        "bhd,kd->hbk", heads_grad, value_rows, preferred_element_type=jnp.float32
-    )
-    score_grad = (
-        probs * (prob_grad - jnp.sum(probs * prob_grad, axis=-1, keepdims=True))
-    ).astype(jnp.bfloat16)
-    query_grad = (
-        (
-            jnp.einsum("hbk,kd->bhd", score_grad, key_rows, preferred_element_type=jnp.float32)
-            * score_scale
-        )
-        .reshape(part_rows, width)
-        .astype(jnp.bfloat16)
-    )
-    key_grad = (
-        jnp.einsum("hbk,bhd->kd", score_grad, query_heads, preferred_element_type=jnp.float32)
-        * score_scale
-    )
-    value_grad = jnp.einsum(
-        "hbk,bhd->kd",
-        probs.astype(jnp.bfloat16),
-        heads_grad,
-        preferred_element_type=jnp.float32,
-    )
-    shared_part, output_cols = lax.optimization_barrier(
-        (low(jnp.concatenate([key_grad, value_grad], axis=1)), output_cols)
-    )
-    shared_grad, project_sum = scatter_shared(n_dp, n, shared_part, project_grad)
+    project_grad_t = low(mul_left_t(branch_grad, heads_out))
+    heads_grad = low(mul_plain(branch_grad, project_all_t))
+    query_grad, key_grad, value_grad = attend_back(
+        queries, heads_grad, log_total, key_rows, value_rows, masks
+    )
+    query_weight_grad = low(mul_left_t(normed_low, query_grad))
+    shared_part = lax.dynamic_update_slice_in_dim(
+        jnp.zeros((row_count, 2 * head_size), jnp.bfloat16),
+        low(jnp.concatenate([key_grad, value_grad], axis=1)),
+        window_start,
+        0,
+    )
+    shared_grad, query_sum, project_sum, output_rows = scatter_shared(
+        n_dp, n, shared_part, output_cols, query_weight_grad, project_grad_t
+    )
     shared_grad = low(shared_grad)
-    output_rows = lax.all_gather(output_cols, "tensor", axis=1, tiled=True)
     query_bias_grad = jnp.sum(query_grad.astype(jnp.float32), axis=0)
-    query_weight_grad = mul_left_t(normed_low, query_grad)
     normed_one_grad = mul_right_t(query_grad, query_all) + mul_right_t(shared_grad, shared_all)
     inputs_from_norm, gain_one_grad, shift_one_grad = norm_one_back(normed_one_grad)
     input_result = (hidden_grad + inputs_from_norm).astype(jnp.bfloat16)
     shared_weight_grad = mul_left_t(normed_low, shared_grad)
     value_bias_grad = jnp.sum(shared_grad[:, head_size:].astype(jnp.float32), axis=0)
 
-    project_part, query_sum, shared_sum, input_cols = cols_and_grads(
-        n_dp, n, input_result, project_sum, low(query_weight_grad), low(shared_weight_grad)
-    )
-    input_cols, output_rows = lax.optimization_barrier(
-        (unpack(exchange(pack(input_cols, recv_slots)), send_slots), output_rows)
-    )
-    grad_rows = lax.all_gather(input_cols, "tensor", axis=1, tiled=True)
-    query_part, shared_piece = scatter_grads(n_dp, n, query_sum, shared_sum)
+    shared_sum, input_cols = cols_and_shared(n_dp, n, input_result, low(shared_weight_grad))
+    packed, query_sum, project_sum, shared_sum = lax.optimization_barrier(
+        (pack(input_cols, recv_slots), query_sum, project_sum, shared_sum)
+    )
+    query_part, project_part_t, shared_piece = scatter_grads(
+        n_dp, n, query_sum, project_sum, shared_sum
+    )
+    project_part = turned(project_part_t)
+    arrived, query_part = lax.optimization_barrier((exchange(packed), query_part))
+    grad_rows = lax.all_gather(unpack(arrived, send_slots), "tensor", axis=1, tiled=True)
     output_back = output_rows.astype(jnp.float32)
     token_rms = jnp.sqrt(jnp.mean(output_back * output_back, axis=1))
 

time: 994 us -> 842 us (0.85)
  matrix products: 207 us -> 153 us
  Pallas kernels: 588 us -> 539 us
  blocking collectives: 29.8 us -> 0 us
  other arithmetic: 77.1 us -> 53.2 us
    pallas_call x8, Pallas kernels: 559 us -> 487 us  [move(): pl.pallas_call(kernel, out_shape=tuple(outs), in_specs=[IN_VMEM if i < in...]
    dot_general x6 -> x0, matrix products: 46.2 us -> none  [the longest x1 13.4 us: local(): jnp.einsum('bhd,kd->hbk', heads_grad, value_rows, preferred_element_type=...]
    pallas_call x0 -> x2, Pallas kernels: none -> 29.9 us  [the longest x1 16.9 us: attend_back(): pl.pallas_call(functools.partial(attend_back_kernel, size ** (-0.5)), gri...]
    all_to_all x1 -> x0, blocking collectives: 29.8 us -> none  [exchange(): return lax.all_to_all(packed, 'dp', split_axis=0, concat_axis=0, tiled=True)]
    all_to_all x2 -> x3, waiting for transfers between devices: 27.5 us -> 0.01 us  [exchange(): return lax.all_to_all(packed, 'dp', split_axis=0, concat_axis=0, tiled=True)]
    all_gather x3 -> x1, waiting for transfers between devices: 0.01 us -> 23.9 us  [local(): lax.all_gather(unpack(arrived, send_slots), 'tensor', axis=1, tiled=True)]
    convert_element_type x1 -> x0, other arithmetic: 10.3 us -> none  [local(): score_grad = (probs * (prob_grad - jnp.sum(probs * prob_grad, axis=-1, ke...]
  transfers between devices with their start and end apart: 6 -> 5, of which waited for: 2 -> 1; matrix products, arithmetic and copies ran while one was open for 20% -> 15% of each run, Pallas kernels for 44% -> 28%
where the time goes in v3:
time: 842 us; the launch traced here: 834 us
  Pallas kernels  539 us (64%)
  matrix products  153 us (18%)
  other arithmetic  53.2 us (6%)
  local copies, waits for them, and re-layouts  29.7 us (4%)
  waiting for transfers between devices  24 us (3%)
  between operations  21.1 us (3%)
  starting transfers between devices  13.5 us (2%)
    pallas_call x8, Pallas kernels, move(): pl.pallas_call(kernel, out_shape=tuple(outs), in_specs=[IN_VMEM if i < in...  487 us
    dot_general x8, matrix products, mul_plain(): return jnp.dot(left, right, preferred_element_type=jnp.float32)  62.7 us
    dot_general x8, matrix products, mul_left_t(): lax.dot_general(left, right, (((0,), (0,)), ((), ())), preferred_element_...  55.3 us
    dot_general x5, matrix products, mul_right_t(): lax.dot_general(left, right, (((1,), (1,)), ((), ())), preferred_element_...  35.3 us
    all_gather x1, waiting for transfers between devices, local(): lax.all_gather(unpack(arrived, send_slots), 'tensor', axis=1, tiled=True)  23.9 us
    pallas_call x1, Pallas kernels, sum_all(): pl.pallas_call(functools.partial(sum_all_kernel, n_dp, n), out_shape=jax....  22.4 us
    pallas_call x1, Pallas kernels, attend_back(): pl.pallas_call(functools.partial(attend_back_kernel, size ** (-0.5)), gri...  16.9 us
  transfers between devices with their start and end apart: 5, of which 1 were waited for; matrix products, arithmetic and copies ran while one was open for 15% of the time, Pallas kernels for 28%

profile of v3, /device:TPU:0, one launch (start us, length us, event | category | flops | bytes accessed | tf_op | source)
XLA Modules:
  0.0 834.1 jit_solution(4733170998044918614)
XLA Ops:
  11.9 6.1 fusion.19
  18.1 5.4 all-to-all-start
  28.4 2.7 convert_element_type.122.a
  31.2 43.8 %gather_lines.1 = (bf16[256,2048]{1,0:T(8,128)(2,1)}, bf16[256,2048]{1,0:T(8,128)(2,1)}, bf16[256,256]{1,0:T(8,128)(2,1)}) custom-call(bf16[256,512]{1,0:T(8,128)(2,1)} %convert_element_type.112.a, bf16[256,512]{1,0:T(8,128)(2,1)} %bitcast.89, bf16[64,256]{1,0:T(8,128)(2,1)} %convert_element_type.114.c), custom_call_target="tpu_custom_call" | custom-call | tf_op jit(solution)/shard_map/gather_lines/pallas_call | solution.py:589
  75.0 8.1 fusion.40.x.y
  83.1 56.8 %rows_and_weights.1 = (bf16[256,2048]{1,0:T(8,128)(2,1)}, bf16[1024,2048]{1,0:T(8,128)(2,1)}, bf16[2048,2048]{1,0:T(8,128)(2,1)}, bf16[2048,256]{1,0:T(8,128)(2,1)}) custom-call(bf16[1024,1024]{1,0:T(8,128)(2,1)} %fusion.40.x.y, bf16[256,2048]{1,0:T(8,128)(2,1)} %get-tuple-element.75.a, bf16[256,256]{1,0:T(8,128)(2,1)} %get-tuple-element.76.b), custom_call_target="tpu_custom_call" | custom-call | tf_op jit(solution)/shard_map/rows_and_weights/pallas_call | solution.py:589
  144.5 45.8 %shared_and_project.1 = (bf16[1024,256]{1,0:T(8,128)(2,1)}, bf16[2048,2048]{1,0:T(8,128)(2,1)}, bf16[1024,2048]{1,0:T(8,128)(2,1)}) custom-call(bf16[1024,1024]{1,0:T(8,128)(2,1)} %fusion.40.x.y, bf16[256,256]{1,0:T(8,128)(2,1)} %fusion.44.x, bf16[256,2048]{1,0:T(8,128)(2,1)} %get-tuple-element.80.a, ...), custom_call_target="tpu_custom_call", output_to_operand_aliasing={{2}: (3, {})} | custom-call | tf_op jit(solution)/shard_map/shared_and_project/pallas_call | solution.py:589
  191.8 6.0 fusion.26.q
  197.8 13.0 %attend.1 = (bf16[256,2048]{1,0:T(8,128)(2,1)S(1)}, f32[256,2048]{1,0:T(8,128)S(1)}) custom-call(bf16[256,2048]{1,0:T(8,128)(2,1)S(1)} %fusion.26.q, bf16[768,128]{1,0:T(8,128)(2,1)S(1)} %get-tuple-element.148.k, bf16[768,128]{1,0:T(8,128)(2,1)S(1)} %get-tuple-element.147.v, s32[256,1]{1,0:T(8,128)S(1)} %copy.59.seg_row, ...), custom_call_target="tpu_custom_call" | custom-call | tf_op jit(solution)/shard_map/attend/pallas_call | solution.py:1000
  211.8 2.5 fusion.74
  216.1 76.8 %rows_and_expanded.1 = (bf16[1024,2048]{1,0:T(8,128)(2,1)}, bf16[2048,2048]{1,0:T(8,128)(2,1)}, bf16[2048,2048]{1,0:T(8,128)(2,1)}) custom-call(bf16[256,2048]{1,0:T(8,128)(2,1)} %add_convert_fusion.1.x_ref, bf16[256,2048]{1,0:T(8,128)(2,1)} %convert_element_type.122.a, bf16[256,2048]{1,0:T(8,128)(2,1)} %bitcast.84), custom_call_target="tpu_custom_call" | custom-call | tf_op jit(solution)/shard_map/rows_and_expanded/pallas_call | solution.py:589
  292.9 14.5 %fusion.75 = f32[1024,2048]{1,0:T(8,128)} fusion(bf16[1024,2048]{1,0:T(8,128)(2,1)} %get-tuple-element.85, bf16[2048,2048]{1,0:T(8,128)(2,1)} %get-tuple-element.86), kind=kOutput, calls=%fused_computation.150 | convolution fusion | flops 8589934592 | bytes 20971520 | tf_op jit(solution)/shard_map/dot_general | solution.py:34
  307.3 15.5 %fusion.56 = f32[1024,2048]{1,0:T(8,128)S(1)} fusion(bf16[2048,2048]{1,0:T(8,128)(2,1)} %get-tuple-element.87, f32[1024,2048]{1,0:T(8,128)} %fusion.75, f32[2048]{0:T(1024)S(1)} %get-tuple-element.150), kind=kOutput, calls=%fused_computation.143 | convolution fusion | flops 8610906112 | bytes 25174016 | tf_op jit(solution)/shard_map/dot_general | solution.py:38
  323.3 2.7 convert_element_type.125
  326.0 19.1 %convert_reduce_fusion = (f32[2048]{0:T(1024)S(1)}, bf16[1024,2048]{1,0:T(8,128)(2,1)S(1)}) fusion(f32[1024,2048]{1,0:T(8,128)} %fusion.75, f32[2048]{0:T(1024)S(1)} %get-tuple-element.150, bf16[1024,2048]{1,0:T(8,128)(2,1)} %get-tuple-element.89, bf16[2048,2048]{1,0:T(8,128)(2,1)} %get-tuple-element.87), kind=kOutput, calls=%fused_computation.10 | convolution fusion | flops 8638167040 | bytes 25182208 | tf_op jit(solution)/shard_map/dot_general | solution.py:34
  345.2 12.8 %convolution_convert_fusion.4.x_ref = bf16[1024,2048]{1,0:T(8,128)(2,1)} fusion(bf16[1024,2048]{1,0:T(8,128)(2,1)S(1)} %get-tuple-element.140, bf16[2048,2048]{1,0:T(8,128)(2,1)} %get-tuple-element.86), kind=kOutput, calls=%fused_computation.30 | convolution fusion | flops 8592031744 | bytes 16777216 | tf_op jit(solution)/shard_map/dot_general | solution.py:38
  358.0 11.6 %convolution_convert_fusion.3.a = bf16[2048,2048]{1,0:T(8,128)(2,1)} fusion(bf16[1024,2048]{1,0:T(8,128)(2,1)S(1)} %copy-done.68, bf16[1024,2048]{1,0:T(8,128)(2,1)S(1)} %get-tuple-element.140), kind=kOutput, calls=%fused_computation.23 | convolution fusion | flops 8594128896 | bytes 16777216 | tf_op jit(solution)/shard_map/dot_general | solution.py:44
  369.6 11.9 %convolution_convert_fusion.2.b = bf16[2048,2048]{1,0:T(8,128)(2,1)} fusion(bf16[1024,2048]{1,0:T(8,128)(2,1)S(1)} %copy-done.22, f32[1024,2048]{1,0:T(8,128)S(1)} %bitcast.105, f32[2048]{0:T(1024)S(1)} %get-tuple-element.150), kind=kOutput, calls=%fused_computation.22 | convolution fusion | flops 8615100416 | bytes 20979712 | tf_op jit(solution)/shard_map/dot_general | solution.py:44
  381.5 90.1 %scatter_expanded.1 = (f32[256,2048]{1,0:T(8,128)}, f32[256,2048]{1,0:T(8,128)}, f32[256,2048]{1,0:T(8,128)}) custom-call(bf16[1024,2048]{1,0:T(8,128)(2,1)} %convolution_convert_fusion.4.x_ref, bf16[2048,2048]{1,0:T(8,128)(2,1)} %convolution_convert_fusion.3.a, bf16[2048,2048]{1,0:T(8,128)(2,1)} %convolution_convert_fusion.2.b), custom_call_target="tpu_custom_call" | custom-call | tf_op jit(solution)/shard_map/scatter_expanded/pallas_call | solution.py:589
  471.6 2.4 multiply_reduce_fusion.2
  477.7 5.2 fusion.24
  482.9 4.3 all-to-all-start.1
  487.3 5.8 convolution_convert_fusion.6.do
  493.2 16.9 %attend_back.1 = (bf16[256,2048]{1,0:T(8,128)(2,1)S(1)}, f32[768,128]{1,0:T(8,128)S(1)}, f32[768,128]{1,0:T(8,128)S(1)}) custom-call(bf16[256,2048]{1,0:T(8,128)(2,1)S(1)} %copy-done.1, bf16[256,2048]{1,0:T(8,128)(2,1)S(1)} %convolution_convert_fusion.6.do, f32[256,2048]{1,0:T(8,128)S(1)} %get-tuple-element.91.log_total, bf16[768,128]{1,0:T(8,128)(2,1)S(1)} %copy-done.5, ...), custom_call_target="tpu_custom_call" | custom-call | tf_op jit(solution)/shard_map/attend_back/pallas_call | solution.py:1020
  511.1 3.8 dynamic_update_slice.10.x_ref
  515.0 7.0 convolution_convert_fusion.b
  522.0 5.8 convolution_convert_fusion.1.a
  527.9 3.7 fusion.76
  531.6 5.4 fusion.41.y
  536.9 92.0 %scatter_shared.1 = (f32[256,256]{1,0:T(8,128)}, bf16[256,2048]{1,0:T(8,128)(2,1)}, bf16[256,2048]{1,0:T(8,128)(2,1)}, bf16[1024,2048]{1,0:T(8,128)(2,1)}) custom-call(bf16[1024,256]{1,0:T(8,128)(2,1)} %dynamic_update_slice.10.x_ref, bf16[1024,512]{1,0:T(8,128)(2,1)} %fusion.41.y, bf16[2048,2048]{1,0:T(8,128)(2,1)} %convolution_convert_fusion.1.a, ...), custom_call_target="tpu_custom_call" | custom-call | tf_op jit(solution)/shard_map/scatter_shared/pallas_call | solution.py:589
  634.6 3.3 convert_reduce_fusion.2
  637.9 24.9 %cols_and_shared.1 = (bf16[256,256]{1,0:T(8,128)(2,1)}, bf16[1024,512]{1,0:T(8,128)(2,1)}) custom-call(bf16[256,2048]{1,0:T(8,128)(2,1)} %get-tuple-element.146.x, bf16[2048,256]{1,0:T(8,128)(2,1)} %convolution_convert_fusion.5.c), custom_call_target="tpu_custom_call" | custom-call | tf_op jit(solution)/shard_map/cols_and_shared/pallas_call | solution.py:589
  662.9 4.8 fusion.25
  667.7 3.6 all-to-all-start.2
  671.3 56.7 %scatter_grads.1 = (f32[256,512]{1,0:T(8,128)}, f32[256,512]{1,0:T(8,128)}, f32[64,256]{1,0:T(8,128)}) custom-call(bf16[256,2048]{1,0:T(8,128)(2,1)} %get-tuple-element.103.a, bf16[256,2048]{1,0:T(8,128)(2,1)} %get-tuple-element.104.b, bf16[256,256]{1,0:T(8,128)(2,1)} %get-tuple-element.105.c), custom_call_target="tpu_custom_call" | custom-call | tf_op jit(solution)/shard_map/scatter_grads/pallas_call | solution.py:589
  728.1 3.8 fusion.42
  731.9 1.9 copy.65
  734.4 2.8 multiply_reduce_fusion.1
  740.4 3.6 multiply_reduce_fusion
  750.6 22.4 %sum_all.1 = f32[192,128]{1,0:T(8,128)} custom-call(f32[192,128]{1,0:T(8,128)} %bitcast.91), custom_call_target="tpu_custom_call" | custom-call | tf_op jit(solution)/shard_map/sum_all/pallas_call | solution.py:1111
  777.2 1.7 multiply_subtract_fusion.5
  778.9 2.7 multiply_subtract_fusion.2
  783.1 2.1 multiply_subtract_fusion.4
  785.3 3.8 multiply_subtract_fusion
  791.0 4.0 multiply_subtract_fusion.1
  795.0 23.9 %all-gather.2.cloned.1.call-done = bf16[1024,2048]{1,0:T(8,128)(2,1)} async-done(((bf16[1024,512]{1,0:T(8,128)(2,1)}), bf16[1024,2048]{1,0:T(8,128)(2,1)}) %all-gather.2.cloned.1.call-update) | async-done | bytes 4194320 | tf_op jit(solution)/shard_map/all_gather | solution.py:1305
  818.9 4.9 copy.74
  823.9 2.0 copy.75
  (234 shorter events, 42.3 us)
Async XLA Ops:
  18.0 6.4 copy-start.33
  18.0 7.1 copy-start.51
  18.0 7.7 copy-start.57
  18.0 8.0 copy-start.69
  18.1 9.0 %copy-start.24 = (f32[2048,256]{1,0:T(8,128)S(1)}, f32[2048,256]{1,0:T(8,128)}, u32[]{:S(2)}) copy-start(f32[2048,256]{1,0:T(8,128)} %param.38) | copy-start | bytes 6291460
  18.1 57.0 %all-to-all-start = ((bf16[8,256,1024]{2,1,0:T(8,128)(2,1)}), bf16[8,256,1024]{2,1,0:T(8,128)(2,1)}, u32[]{:S(2)}, u32[]{:S(2)}) async-start(bf16[8,256,1024]{2,1,0:T(8,128)(2,1)} %bitcast.85), calls=%async_computation | async-start | bytes 8388608 | tf_op jit(solution)/shard_map/all_to_all | solution.py:1174
  23.5 454.2 %reduce-scatter.2.cloned.1.call-start = ((), (), s32[]{:S(2)}) async-start(), calls=%async_computation.4 | async-start | bytes 5242880 | tf_op jit(solution)/shard_map/reduce_scatter | solution.py:1252
  26.1 49.0 %copy-start.66 = (s32[1,2,8,128]{3,1,2,0:T(2,128)}, s32[1,2,8,128]{3,1,2,0:T(2,128)S(1)}, u32[]{:S(2)}) copy-start(s32[1,2,8,128]{3,1,2,0:T(2,128)S(1)} %copy.66) | copy-start | bytes 24580
  26.6 171.1 %copy-start.6 = (s32[256,1]{1,0:T(8,128)}, s32[256,1]{1,0:T(8,128)S(1)}, u32[]{:S(2)}) copy-start(s32[256,1]{1,0:T(8,128)S(1)} %copy.59.seg_row) | copy-start | bytes 3076
  26.8 170.9 %copy-start.8 = (s32[256,1]{1,0:T(8,128)}, s32[256,1]{1,0:T(8,128)S(1)}, u32[]{:S(2)}) copy-start(s32[256,1]{1,0:T(8,128)S(1)} %copy.60.pos_row) | copy-start | bytes 3076
  26.9 170.8 %copy-start.12 = (s32[1,768]{1,0:T(1,128)}, s32[1,768]{1,0:T(1,128)S(1)}, u32[]{:S(2)}) copy-start(s32[1,768]{1,0:T(1,128)S(1)} %broadcast_in_dim.32.seg_col) | copy-start | bytes 9220
  27.0 170.7 %copy-start.14 = (s32[1,768]{1,0:T(1,128)}, s32[1,768]{1,0:T(1,128)S(1)}, u32[]{:S(2)}) copy-start(s32[1,768]{1,0:T(1,128)S(1)} %broadcast_in_dim.34.pos_col) | copy-start | bytes 9220
  28.4 46.5 %copy-start.49 = (f32[22656]{0:T(1024)S(1)}, f32[22656]{0:T(1024)}, u32[]{:S(2)}) copy-start(f32[22656]{0:T(1024)} %param.41) | copy-start | bytes 271876
  75.0 116.7 %copy-start.47 = (f32[2048]{0:T(1024)}, f32[2048]{0:T(1024)S(1)}, u32[]{:S(2)}) copy-start(f32[2048]{0:T(1024)S(1)} %get-tuple-element.156) | copy-start | bytes 24580
  75.0 116.7 %copy-start.54 = (f32[2048]{0:T(1024)}, f32[2048]{0:T(1024)S(1)}, u32[]{:S(2)}) copy-start(f32[2048]{0:T(1024)S(1)} %get-tuple-element.155) | copy-start | bytes 24580
  141.5 50.2 %copy-start.58 = (f32[256]{0:T(256)}, f32[256]{0:T(256)S(1)}, u32[]{:S(2)}) copy-start(f32[256]{0:T(256)S(1)} %broadcast_multiply_fusion.1) | copy-start | bytes 3076
  143.2 48.5 %copy-start.60 = (f32[256]{0:T(256)}, f32[256]{0:T(256)S(1)}, u32[]{:S(2)}) copy-start(f32[256]{0:T(256)S(1)} %fusion.50) | copy-start | bytes 3076
  190.3 21.4 %slice-start.3 = ((s8[8388608]{0:T(1024)(128)(4,1)}), s8[4194304]{0:T(1024)(128)(4,1)S(1)}, s32[]{:S(2)}) async-start(s8[8388608]{0:T(1024)(128)(4,1)} %bitcast.102), calls=%async_computation.9 | async-start | bytes 8388608
  191.7 6.1 copy-start.2
  191.7 6.1 copy-start.4
  191.7 20.0 %slice-start.4 = ((s8[8388608]{0:T(1024)(128)(4,1)}), s8[4194304]{0:T(1024)(128)(4,1)S(1)}, s32[]{:S(2)}) async-start(s8[8388608]{0:T(1024)(128)(4,1)} %bitcast.102), calls=%async_computation.10 | async-start | bytes 8388608
  214.3 108.5 %copy-start.16 = (f32[256,2048]{1,0:T(8,128)}, f32[256,2048]{1,0:T(8,128)S(1)}, u32[]{:S(2)}) copy-start(f32[256,2048]{1,0:T(8,128)S(1)} %get-tuple-element.160) | copy-start | bytes 6291460
  326.0 43.6 %slice-start.5 = ((s8[8388608]{0:T(1024)(128)(4,1)}), s8[4194304]{0:T(1024)(128)(4,1)S(1)}, s32[]{:S(2)}) async-start(s8[8388608]{0:T(1024)(128)(4,1)} %bitcast.104), calls=%async_computation.11 | async-start | bytes 8388608
  345.1 12.8 %copy-start.68 = (bf16[1024,2048]{1,0:T(8,128)(2,1)S(1)}, bf16[1024,2048]{1,0:T(8,128)(2,1)}, u32[]{:S(2)}) copy-start(bf16[1024,2048]{1,0:T(8,128)(2,1)} %get-tuple-element.85) | copy-start | bytes 12582916
  345.1 24.4 %slice-start.6 = ((s8[8388608]{0:T(1024)(128)(4,1)}), s8[4194304]{0:T(1024)(128)(4,1)S(1)}, s32[]{:S(2)}) async-start(s8[8388608]{0:T(1024)(128)(4,1)} %bitcast.104), calls=%async_computation.12 | async-start | bytes 8388608
  358.0 11.6 %copy-start.22 = (bf16[1024,2048]{1,0:T(8,128)(2,1)S(1)}, bf16[1024,2048]{1,0:T(8,128)(2,1)}, u32[]{:S(2)}) copy-start(bf16[1024,2048]{1,0:T(8,128)(2,1)} %get-tuple-element.89) | copy-start | bytes 12582916
  381.5 90.1 %copy-start.17 = (f32[256,2048]{1,0:T(8,128)S(1)}, f32[256,2048]{1,0:T(8,128)}, u32[]{:S(2)}) copy-start(f32[256,2048]{1,0:T(8,128)} %copy-done.16) | copy-start | bytes 6291460
  477.7 9.6 %copy-start.28 = (bf16[256,2048]{1,0:T(8,128)(2,1)}, bf16[256,2048]{1,0:T(8,128)(2,1)S(1)}, u32[]{:S(2)}) copy-start(bf16[256,2048]{1,0:T(8,128)(2,1)S(1)} %get-tuple-element.142) | copy-start | bytes 3145732
  482.9 48.7 %all-to-all-start.1 = ((bf16[8,256,512]{2,1,0:T(8,128)(2,1)}), bf16[8,256,512]{2,1,0:T(8,128)(2,1)}, u32[]{:S(2)}, u32[]{:S(2)}) async-start(bf16[8,256,512]{2,1,0:T(8,128)(2,1)} %bitcast.86), calls=%async_computation.2 | async-start | bytes 4194304 | tf_op jit(solution)/shard_map/all_to_all | solution.py:1174
  487.2 5.9 copy-start.1
  487.3 5.9 copy-start.3
  487.3 5.9 copy-start.5
  487.3 5.9 copy-start.7
  487.3 5.9 copy-start.9
  487.3 5.9 copy-start.13
  514.9 7.1 copy-start.19
  514.9 7.1 copy-start.48
  514.9 7.1 copy-start.55
  514.9 7.0 copy-start.59
  515.0 7.0 copy-start.61
  515.0 12.9 %slice-start.1 = ((s8[8388608]{0:T(1024)(128)(4,1)}), s8[4194304]{0:T(1024)(128)(4,1)S(1)}, s32[]{:S(2)}) async-start(s8[8388608]{0:T(1024)(128)(4,1)} %bitcast.100), calls=%async_computation.7 | async-start | bytes 8388608
  667.7 60.4 %all-to-all-start.2 = ((bf16[8,256,512]{2,1,0:T(8,128)(2,1)}), bf16[8,256,512]{2,1,0:T(8,128)(2,1)S(1)}, u32[]{:S(2)}, u32[]{:S(2)}) async-start(bf16[8,256,512]{2,1,0:T(8,128)(2,1)} %bitcast.88), calls=%async_computation.3 | async-start | bytes 4194304 | tf_op jit(solution)/shard_map/all_to_all | solution.py:1174
  671.3 147.6 %all-gather.2.cloned.1.call-start = ((), (), s32[]{:S(2)}) async-start(), calls=%async_computation.5 | async-start | bytes 5242880 | tf_op jit(solution)/shard_map/all_gather | solution.py:1305
  740.4 36.7 %copy-start.52 = (f32[64,256]{1,0:T(8,128)S(1)}, f32[64,256]{1,0:T(8,128)}, u32[]{:S(2)}) copy-start(f32[64,256]{1,0:T(8,128)} %param.29) | copy-start | bytes 196612
  740.4 38.5 %copy-start.32 = (f32[512,256]{1,0:T(8,128)S(1)}, f32[512,256]{1,0:T(8,128)}, u32[]{:S(2)}) copy-start(f32[512,256]{1,0:T(8,128)} %param.32) | copy-start | bytes 1572868
  744.6 38.5 %copy-start.50 = (f32[22656]{0:T(1024)S(1)}, f32[22656]{0:T(1024)}, u32[]{:S(2)}) copy-start(f32[22656]{0:T(1024)} %param.41) | copy-start | bytes 271876
  744.6 38.5 %copy-start.56 = (f32[22656]{0:T(1024)S(1)}, f32[22656]{0:T(1024)}, u32[]{:S(2)}) copy-start(f32[22656]{0:T(1024)} %param.42) | copy-start | bytes 271876
  778.9 6.3 copy-start.38
  (34 other events, 115.6 us)
Sparse Core Ops, SparseCore 0:
  326.1 86.1 reduce-scatter.1
  732.0 86.8 all-gather.1

commit v4 on v3

--- a/solution.py
+++ b/solution.py
@@ -43,6 +43,12 @@
 def mul_left_t(left, right):
     return lax.dot_general(
         left, right, (((0,), (0,)), ((), ())), preferred_element_type=jnp.float32
+    )
+
+
+def product(left, right, left_dim, right_dim):
+    return lax.dot_general(
+        left, right, (((left_dim,), (right_dim,)), ((), ())), preferred_element_type=jnp.float32
     )
 
 
@@ -528,6 +534,71 @@
             self.onward(e, c, way).wait_send()
 
 
+class ProductScatter(RingScatter):
+    @staticmethod
+    def scratch(chips, chunks, block, dtype):
+        return RingScatter.scratch(chips, chunks, block, dtype) + [pltpu.VMEM((2, *block), dtype)]
+
+    def __init__(self, at, chunks, left, right, out, scratch, unit, cost):
+        super().__init__(at, chunks, None, out, scratch[:-1], unit)
+        self.left, self.right, self.stage, self.cost = left, right, scratch[-1], cost
+
+    def across(self, place, c):
+        src = self.stage.at[self.places().index(place) % 2, self.span(c)]
+        dst = self.other.at[place, self.span(c)]
+        return remote(src, dst, self.s1.at[place, c], self.r1.at[place, c], self.at.sibling)
+
+    def product(self, place, core):
+        block = self.held.shape[2]
+        cols = lanes(self.target(place, core), block) if block % 128 == 0 else None
+        if cols is None:
+            left = self.left[pl.ds(pl.multiple_of(self.target(place, core) * block, block), block)]
+            total = product(left, self.right[...], 1, 0)
+        else:
+            total = product(self.left[:, cols], self.right[...], 0, 0)
+        return total.astype(self.mine.dtype)
+
+    def work(self, i, place, here):
+        if here:
+            self.mine[place] = self.product(place, self.at.core)
+            return
+        if i >= 2:
+            for c in range(self.chunks):
+                self.across(self.places()[i - 2], c).wait_send()
+        self.stage[i % 2] = self.product(place, 1 - self.at.core)
+        for c in range(self.chunks):
+            self.across(place, c).start()
+
+    def prepare(self):
+        pass
+
+    def prepared(self):
+        pass
+
+    def start(self):
+        pass
+
+    def steps(self):
+        when = 0.0
+        for i, place in enumerate(self.places()):
+            for here in (False, True):
+                yield when, functools.partial(self.work, i, place, here)
+                when += self.cost
+        for when, step in super().steps():
+            place = 0
+            if len(step.args) == 3:
+                e, _, way = step.args
+                place = self.at.chips - e if way else e
+            yield max(when, (2 * self.places().index(place) + 2) * self.cost), step
+
+    def finish(self):
+        for place in self.places()[-2:]:
+            for c in range(self.chunks):
+                self.across(place, c).wait_send()
+        for e, c, way in self.every():
+            self.onward(e, c, way).wait_send()
+
+
 class LineSwitch:
     @staticmethod
     def sems(n):
@@ -643,6 +714,14 @@
 
 def ring_scatter(at, x, out, axis, chunks, scratch, unit=1.0):
     return RingScatter(at, chunks, blocks_of(x, out, axis, chunks), out, scratch, unit)
+
+
+def product_scatter(at, left, right, out, chunks, scratch, unit, cost):
+    return ProductScatter(at, chunks, left, right, out, scratch, unit, cost)
+
+
+def by_lanes(left, n_dp):
+    return left if left.shape[1] // n_dp % 128 == 0 else left.T
 
 
 def like(x, rows, cols, dtype=None):
@@ -835,15 +914,15 @@
     )
 
 
-def scatter_shared(n_dp, n, x, result, query, project):
+def scatter_shared(n_dp, n, x, result, a, dq, dz, o):
     chips, chunks = n_dp // 2, 4
     block = (x.shape[0] // n, x.shape[1])
-    w_block = (project.shape[0] // n_dp, project.shape[1])
+    w_block = (a.shape[1] // n_dp, dq.shape[1])
     small = LineExchange.scratch(n, block, x.dtype)
     line = LineGather.sems(n, chunks)
-    ring = RingScatter.scratch(chips, chunks, w_block, x.dtype)
-
-    def kernel(x_ref, y, a, b, x_out, a_out, b_out, y_out, *refs):
+    ring = ProductScatter.scratch(chips, chunks, w_block, x.dtype)
+
+    def kernel(x_ref, y, a_ref, dq_ref, dz_ref, o_ref, x_out, a_out, b_out, y_out, *refs):
         parts = Parts(refs)
         at = Place(n_dp, n)
         run_jobs(
@@ -851,15 +930,15 @@
             [
                 line_exchange(at, x_ref, x_out, 0, parts.take(small)),
                 line_gather(at, y, y_out, 1, chunks, parts.take(line), 22.0),
-                ring_scatter(at, a, a_out, 0, chunks, parts.take(ring), 24.0),
-                ring_scatter(at, b, b_out, 0, chunks, parts.take(ring), 24.0),
+                product_scatter(at, dz_ref, o_ref, b_out, chunks, parts.take(ring), 24.0, 1.0),
+                product_scatter(at, a_ref, dq_ref, a_out, chunks, parts.take(ring), 24.0, 1.0),
             ],
         )
 
     return move(
         kernel,
-        (x, result, query, project),
-        2,
+        (x, result, by_lanes(a, n_dp), dq, by_lanes(dz, n_dp), o),
+        6,
         (
             jax.ShapeDtypeStruct(block, jnp.float32),
             jax.ShapeDtypeStruct(w_block, x.dtype),
@@ -942,12 +1021,6 @@
     )
 
 
-def product(left, right, left_dim, right_dim):
-    return lax.dot_general(
-        left, right, (((left_dim,), (right_dim,)), ((), ())), preferred_element_type=jnp.float32
-    )
-
-
 def fill_bias(bias, seg_row, seg_col, pos_row, pos_col):
     @pl.when(pl.program_id(0) == 0)
     def _():
@@ -967,7 +1040,7 @@
 
 
 def attend_back_kernel(
-    scale, q, do, log_total, k, v, seg_row, seg_col, pos_row, pos_col, dq, dk, dv, bias
+    scale, q, do, log_total, k, v, seg_row, seg_col, pos_row, pos_col, dq, dkv, bias, dk, dv
 ):
     fill_bias(bias, seg_row, seg_col, pos_row, pos_col)
 
@@ -984,6 +1057,15 @@
     dq[...] = (product(score_grad, k[...], 1, 0) * scale).astype(jnp.bfloat16)
     dk[...] += product(score_grad, q[...], 0, 0) * scale
     dv[...] += product(probs.astype(jnp.bfloat16), do[...], 0, 0)
+
+    @pl.when(pl.program_id(0) == pl.num_programs(0) - 1)
+    def _():
+        dkv[...] = jnp.zeros_like(dkv)
+        rows, (keys, size) = q.shape[0], k.shape
+        last = (lax.axis_index("tensor") + 1) * rows
+        window = pl.ds(pl.multiple_of(jnp.maximum(last - keys, 0), rows), keys)
+        dkv[window, pl.ds(0, size)] = dk[...].astype(dkv.dtype)
+        dkv[window, pl.ds(size, size)] = dv[...].astype(dkv.dtype)
 
 
 def attention_specs(rows, keys, size):
@@ -1007,24 +1089,30 @@
             jax.ShapeDtypeStruct(q.shape, jnp.float32),
         ),
         scratch_shapes=[pltpu.VMEM((rows, keys), jnp.float32)],
-        compiler_params=pltpu.CompilerParams(vmem_limit_bytes=32 * 2**20),
+        compiler_params=pltpu.CompilerParams(vmem_limit_bytes=32 * MIB),
         name="attend",
     )(q, k, v, *masks)
 
 
-def attend_back(q, do, log_total, k, v, masks):
+def attend_back(q, do, log_total, k, v, masks, total):
     rows, width = q.shape
     keys, size = k.shape
     head, shared, mask_specs = attention_specs(rows, keys, size)
-    grad = jax.ShapeDtypeStruct((keys, size), jnp.float32)
     return pl.pallas_call(
         functools.partial(attend_back_kernel, size**-0.5),
         grid=(width // size,),
         in_specs=[head, head, head, shared, shared, *mask_specs],
-        out_specs=(head, shared, shared),
-        out_shape=(jax.ShapeDtypeStruct(q.shape, jnp.bfloat16), grad, grad),
-        scratch_shapes=[pltpu.VMEM((rows, keys), jnp.float32)],
-        compiler_params=pltpu.CompilerParams(vmem_limit_bytes=32 * 2**20),
+        out_specs=(head, pl.BlockSpec((total, 2 * size), lambda h: (0, 0))),
+        out_shape=(
+            jax.ShapeDtypeStruct(q.shape, jnp.bfloat16),
+            jax.ShapeDtypeStruct((total, 2 * size), jnp.bfloat16),
+        ),
+        scratch_shapes=[
+            pltpu.VMEM((rows, keys), jnp.float32),
+            pltpu.VMEM((keys, size), jnp.float32),
+            pltpu.VMEM((keys, size), jnp.float32),
+        ],
+        compiler_params=pltpu.CompilerParams(vmem_limit_bytes=32 * MIB),
         name="attend_back",
     )(q, do, log_total, k, v, *masks)
 
@@ -1224,7 +1312,7 @@
         n_dp, n, owned, low(shared_out), project_line, owned_grad
     )
     window = min(row_count, part_rows + longest)
-    window_start = jnp.clip((t + 1) * part_rows - window, 0, row_count - window)
+    window_start = jnp.maximum((t + 1) * part_rows - window, 0)
     shared_window = lax.dynamic_slice_in_dim(shared_rows, window_start, window, 0)
     key_rows, value_rows = shared_window[:, :head_size], shared_window[:, head_size:]
     segment, position = segment_ids(lengths[0], row_count)
@@ -1244,10 +1332,11 @@
     expand_pre = mul_plain(normed_two_low, expand_cols) + expand_bias
     activated, gelu_back = jax.vjp(gelu_tanh, expand_pre)
     activated_low = activated.astype(jnp.bfloat16)
-    skipped = lax.dynamic_update_slice_in_dim(
-        jnp.zeros((row_count, width), jnp.float32), hidden_one + shrink_bias, t * part_rows, 0
-    )
-    result_part = low(mul_right_t(activated_low, shrink_rows_t) + skipped)
+    result_part = low(mul_right_t(activated_low, shrink_rows_t))
+    own_result = lax.dynamic_slice_in_dim(result_part, t * part_rows, part_rows, 0)
+    result_part = lax.dynamic_update_slice_in_dim(
+        result_part, low(own_result + (hidden_one + shrink_bias)), t * part_rows, 0
+    )
     result_part, owned_grad = lax.optimization_barrier((result_part, owned_grad))
     layer_cols = lax.psum_scatter(result_part, "tensor", scatter_dimension=1, tiled=True)
     shrink_grad_t = low(mul_left_t(owned_grad, activated_low))
@@ -1270,20 +1359,12 @@
     hidden_grad = output_float + hidden_from_norm
     branch_grad = hidden_grad.astype(jnp.bfloat16)
     project_bias_grad = jnp.sum(branch_grad.astype(jnp.float32), axis=0)
-    project_grad_t = low(mul_left_t(branch_grad, heads_out))
     heads_grad = low(mul_plain(branch_grad, project_all_t))
-    query_grad, key_grad, value_grad = attend_back(
-        queries, heads_grad, log_total, key_rows, value_rows, masks
-    )
-    query_weight_grad = low(mul_left_t(normed_low, query_grad))
-    shared_part = lax.dynamic_update_slice_in_dim(
-        jnp.zeros((row_count, 2 * head_size), jnp.bfloat16),
-        low(jnp.concatenate([key_grad, value_grad], axis=1)),
-        window_start,
-        0,
+    query_grad, shared_part = attend_back(
+        queries, heads_grad, log_total, key_rows, value_rows, masks, row_count
     )
     shared_grad, query_sum, project_sum, output_rows = scatter_shared(
-        n_dp, n, shared_part, output_cols, query_weight_grad, project_grad_t
+        n_dp, n, shared_part, output_cols, normed_low, query_grad, branch_grad, heads_out
     )
     shared_grad = low(shared_grad)
     query_bias_grad = jnp.sum(query_grad.astype(jnp.float32), axis=0)

time: 842 us -> 835 us (level)
    dot_general x8 -> x6, matrix products: 55.3 us -> 44.4 us  [mul_left_t(): lax.dot_general(left, right, (((0,), (0,)), ((), ())), preferred_element_...]
  transfers between devices with their start and end apart: 5 -> 5, of which waited for: 1 -> 1; matrix products, arithmetic and copies ran while one was open for 15% -> 14% of each run, Pallas kernels for 28% -> 28%
where the time goes in v4:
time: 835 us; the launch traced here: 826 us
  Pallas kernels  541 us (65%)
  matrix products  146 us (17%)
  other arithmetic  53.8 us (6%)
  local copies, waits for them, and re-layouts  25.2 us (3%)
  waiting for transfers between devices  24.7 us (3%)
  between operations  21.3 us (3%)
  starting transfers between devices  13.5 us (2%)
    pallas_call x8, Pallas kernels, move(): pl.pallas_call(kernel, out_shape=tuple(outs), in_specs=[IN_VMEM if i < in...  488 us
    dot_general x8, matrix products, mul_plain(): return jnp.dot(left, right, preferred_element_type=jnp.float32)  62.5 us
    dot_general x6, matrix products, mul_left_t(): lax.dot_general(left, right, (((0,), (0,)), ((), ())), preferred_element_...  44.4 us
    dot_general x5, matrix products, mul_right_t(): lax.dot_general(left, right, (((1,), (1,)), ((), ())), preferred_element_...  39.5 us
    all_gather x1, waiting for transfers between devices, local(): lax.all_gather(unpack(arrived, send_slots), 'tensor', axis=1, tiled=True)  24.6 us
    pallas_call x1, Pallas kernels, sum_all(): pl.pallas_call(functools.partial(sum_all_kernel, n_dp, n), out_shape=jax....  22.3 us
    pallas_call x1, Pallas kernels, attend_back(): pl.pallas_call(functools.partial(attend_back_kernel, size ** (-0.5)), gri...  17.5 us
  transfers between devices with their start and end apart: 5, of which 1 were waited for; matrix products, arithmetic and copies ran while one was open for 14% of the time, Pallas kernels for 28%

profile of v4, /device:TPU:0, one launch (start us, length us, event | category | flops | bytes accessed | tf_op | source)
XLA Modules:
  0.0 825.8 jit_solution(13505983888132184669)
XLA Ops:
  10.2 1.7 constant_dynamic-slice_fusion.1
  11.9 6.1 fusion.19
  18.1 5.5 all-to-all-start
  28.2 2.6 copy.61
  30.7 43.8 %gather_lines.1 = (bf16[256,2048]{1,0:T(8,128)(2,1)}, bf16[256,2048]{1,0:T(8,128)(2,1)}, bf16[256,256]{1,0:T(8,128)(2,1)}) custom-call(bf16[256,512]{1,0:T(8,128)(2,1)} %convert_element_type.111.a, bf16[256,512]{1,0:T(8,128)(2,1)} %bitcast.89, bf16[64,256]{1,0:T(8,128)(2,1)} %convert_element_type.113.c), custom_call_target="tpu_custom_call" | custom-call | tf_op jit(solution)/shard_map/gather_lines/pallas_call | solution.py:660
  74.6 8.1 fusion.40.x.y
  82.7 57.2 %rows_and_weights.1 = (bf16[256,2048]{1,0:T(8,128)(2,1)}, bf16[1024,2048]{1,0:T(8,128)(2,1)}, bf16[2048,2048]{1,0:T(8,128)(2,1)}, bf16[2048,256]{1,0:T(8,128)(2,1)}) custom-call(bf16[1024,1024]{1,0:T(8,128)(2,1)} %fusion.40.x.y, bf16[256,2048]{1,0:T(8,128)(2,1)} %get-tuple-element.74.a, bf16[256,256]{1,0:T(8,128)(2,1)} %get-tuple-element.75.b), custom_call_target="tpu_custom_call" | custom-call | tf_op jit(solution)/shard_map/rows_and_weights/pallas_call | solution.py:660
  143.7 6.1 fusion.26.q
  151.0 45.8 %shared_and_project.1 = (bf16[1024,256]{1,0:T(8,128)(2,1)}, bf16[2048,2048]{1,0:T(8,128)(2,1)}, bf16[1024,2048]{1,0:T(8,128)(2,1)}) custom-call(bf16[1024,1024]{1,0:T(8,128)(2,1)} %fusion.40.x.y, bf16[256,256]{1,0:T(8,128)(2,1)} %fusion.44.x, bf16[256,2048]{1,0:T(8,128)(2,1)} %get-tuple-element.79.a, ...), custom_call_target="tpu_custom_call", output_to_operand_aliasing={{2}: (3, {})} | custom-call | tf_op jit(solution)/shard_map/shared_and_project/pallas_call | solution.py:660
  198.2 13.0 %attend.1 = (bf16[256,2048]{1,0:T(8,128)(2,1)S(1)}, f32[256,2048]{1,0:T(8,128)S(1)}) custom-call(bf16[256,2048]{1,0:T(8,128)(2,1)S(1)} %fusion.26.q, bf16[768,128]{1,0:T(8,128)(2,1)S(1)} %get-tuple-element.146.k, bf16[768,128]{1,0:T(8,128)(2,1)S(1)} %get-tuple-element.145.v, s32[256,1]{1,0:T(8,128)S(1)} %copy.59.seg_row, ...), custom_call_target="tpu_custom_call" | custom-call | tf_op jit(solution)/shard_map/attend/pallas_call | solution.py:1082
  211.2 6.3 fusion.70
  219.3 76.1 %rows_and_expanded.1 = (bf16[1024,2048]{1,0:T(8,128)(2,1)}, bf16[2048,2048]{1,0:T(8,128)(2,1)}, bf16[2048,2048]{1,0:T(8,128)(2,1)}) custom-call(bf16[256,2048]{1,0:T(8,128)(2,1)} %add_convert_fusion.2.x_ref, bf16[256,2048]{1,0:T(8,128)(2,1)} %convert_element_type.121.a, bf16[256,2048]{1,0:T(8,128)(2,1)} %bitcast.84), custom_call_target="tpu_custom_call" | custom-call | tf_op jit(solution)/shard_map/rows_and_expanded/pallas_call | solution.py:660
  295.5 14.6 %fusion.71 = f32[1024,2048]{1,0:T(8,128)} fusion(bf16[1024,2048]{1,0:T(8,128)(2,1)} %get-tuple-element.84, bf16[2048,2048]{1,0:T(8,128)(2,1)} %get-tuple-element.85), kind=kOutput, calls=%fused_computation.148 | convolution fusion | flops 8589934592 | bytes 20971520 | tf_op jit(solution)/shard_map/dot_general | solution.py:34
  310.1 13.6 %convolution_convert_fusion.3 = bf16[1024,2048]{1,0:T(8,128)(2,1)} fusion(bf16[2048,2048]{1,0:T(8,128)(2,1)S(1)} %copy-done.68, f32[1024,2048]{1,0:T(8,128)} %fusion.71, f32[2048]{0:T(1024)S(1)} %get-tuple-element.148), kind=kOutput, calls=%fused_computation.29 | convolution fusion | flops 8613003264 | bytes 20979712 | tf_op jit(solution)/shard_map/dot_general | solution.py:38
  323.7 2.5 fusion.45
  326.3 18.8 %convert_reduce_fusion = (f32[2048]{0:T(1024)S(1)}, bf16[1024,2048]{1,0:T(8,128)(2,1)S(1)}) fusion(f32[1024,2048]{1,0:T(8,128)} %fusion.71, f32[2048]{0:T(1024)S(1)} %get-tuple-element.148, bf16[1024,2048]{1,0:T(8,128)(2,1)} %get-tuple-element.88, bf16[2048,2048]{1,0:T(8,128)(2,1)} %get-tuple-element.86), kind=kOutput, calls=%fused_computation.10 | convolution fusion | flops 8638167040 | bytes 25182208 | tf_op jit(solution)/shard_map/dot_general | solution.py:34
  345.1 2.0 copy-done.71
  347.1 12.7 %convolution_convert_fusion.2.x_ref = bf16[1024,2048]{1,0:T(8,128)(2,1)} fusion(bf16[1024,2048]{1,0:T(8,128)(2,1)S(1)} %get-tuple-element.138, bf16[2048,2048]{1,0:T(8,128)(2,1)} %get-tuple-element.85), kind=kOutput, calls=%fused_computation.28 | convolution fusion | flops 8592031744 | bytes 16777216 | tf_op jit(solution)/shard_map/dot_general | solution.py:38
  359.9 13.8 %convolution_convert_fusion.1.a = bf16[2048,2048]{1,0:T(8,128)(2,1)} fusion(bf16[1024,2048]{1,0:T(8,128)(2,1)S(1)} %copy-done.69, bf16[1024,2048]{1,0:T(8,128)(2,1)} %copy-done.71), kind=kOutput, calls=%fused_computation.21 | convolution fusion | flops 8594128896 | bytes 16777216 | tf_op jit(solution)/shard_map/dot_general | solution.py:44
  373.7 11.9 %convolution_convert_fusion.b = bf16[2048,2048]{1,0:T(8,128)(2,1)} fusion(bf16[1024,2048]{1,0:T(8,128)(2,1)S(1)} %copy-done.24, f32[1024,2048]{1,0:T(8,128)S(1)} %bitcast.101, f32[2048]{0:T(1024)S(1)} %get-tuple-element.148), kind=kOutput, calls=%fused_computation.20 | convolution fusion | flops 8615100416 | bytes 20979712 | tf_op jit(solution)/shard_map/dot_general | solution.py:44
  385.7 88.5 %scatter_expanded.1 = (f32[256,2048]{1,0:T(8,128)}, f32[256,2048]{1,0:T(8,128)}, f32[256,2048]{1,0:T(8,128)}) custom-call(bf16[1024,2048]{1,0:T(8,128)(2,1)} %convolution_convert_fusion.2.x_ref, bf16[2048,2048]{1,0:T(8,128)(2,1)} %convolution_convert_fusion.1.a, bf16[2048,2048]{1,0:T(8,128)(2,1)} %convolution_convert_fusion.b), custom_call_target="tpu_custom_call" | custom-call | tf_op jit(solution)/shard_map/scatter_expanded/pallas_call | solution.py:660
  474.1 2.5 multiply_reduce_fusion.2
  476.6 1.9 fusion.66
  478.5 4.8 fusion.24
  483.3 4.3 all-to-all-start.1
  487.7 2.2 convert_reduce_fusion.3
  490.0 6.2 convolution_convert_fusion.5.do
  496.3 17.5 %attend_back.1 = (bf16[256,2048]{1,0:T(8,128)(2,1)S(1)}, bf16[1024,256]{1,0:T(8,128)(2,1)S(1)}) custom-call(bf16[256,2048]{1,0:T(8,128)(2,1)S(1)} %copy-done.1, bf16[256,2048]{1,0:T(8,128)(2,1)S(1)} %convolution_convert_fusion.5.do, f32[256,2048]{1,0:T(8,128)S(1)} %get-tuple-element.90.log_total, bf16[768,128]{1,0:T(8,128)(2,1)S(1)} %copy-done.7, ...), custom_call_target="tpu_custom_call" | custom-call | tf_op jit(solution)/shard_map/attend_back/pallas_call | solution.py:1101
  514.5 6.1 fusion.72
  520.7 5.4 fusion.41.y
  526.1 96.7 %scatter_shared.1 = (f32[256,256]{1,0:T(8,128)}, bf16[256,2048]{1,0:T(8,128)(2,1)}, bf16[256,2048]{1,0:T(8,128)(2,1)}, bf16[1024,2048]{1,0:T(8,128)(2,1)}) custom-call(bf16[1024,256]{1,0:T(8,128)(2,1)} %copy-done.13, bf16[1024,512]{1,0:T(8,128)(2,1)} %fusion.41.y, bf16[256,2048]{1,0:T(8,128)(2,1)} %copy-done.25, bf16[256,2048]{1,0:T(8,128)(2,1)} %copy-done.2, ...), custom_call_target="tpu_custom_call" | custom-call | tf_op jit(solution)/shard_map/scatter_shared/pallas_call | solution.py:660
  627.8 3.3 convert_reduce_fusion.2
  631.1 23.7 %cols_and_shared.1 = (bf16[256,256]{1,0:T(8,128)(2,1)}, bf16[1024,512]{1,0:T(8,128)(2,1)}) custom-call(bf16[256,2048]{1,0:T(8,128)(2,1)} %get-tuple-element.144.x, bf16[2048,256]{1,0:T(8,128)(2,1)} %convolution_convert_fusion.4.c), custom_call_target="tpu_custom_call" | custom-call | tf_op jit(solution)/shard_map/cols_and_shared/pallas_call | solution.py:660
  654.9 4.8 fusion.25
  659.7 3.6 all-to-all-start.2
  663.3 56.2 %scatter_grads.1 = (f32[256,512]{1,0:T(8,128)}, f32[256,512]{1,0:T(8,128)}, f32[64,256]{1,0:T(8,128)}) custom-call(bf16[256,2048]{1,0:T(8,128)(2,1)} %get-tuple-element.101.a, bf16[256,2048]{1,0:T(8,128)(2,1)} %get-tuple-element.102.b, bf16[256,256]{1,0:T(8,128)(2,1)} %get-tuple-element.103.c), custom_call_target="tpu_custom_call" | custom-call | tf_op jit(solution)/shard_map/scatter_grads/pallas_call | solution.py:660
  719.6 3.8 fusion.42
  723.4 2.0 copy.65
  726.0 2.8 multiply_reduce_fusion.1
  732.0 3.6 multiply_reduce_fusion
  742.2 22.3 %sum_all.1 = f32[192,128]{1,0:T(8,128)} custom-call(f32[192,128]{1,0:T(8,128)} %bitcast.91), custom_call_target="tpu_custom_call" | custom-call | tf_op jit(solution)/shard_map/sum_all/pallas_call | solution.py:1199
  768.6 1.7 multiply_subtract_fusion.5
  770.4 2.9 multiply_subtract_fusion.3
  776.3 5.8 multiply_subtract_fusion.1
  782.1 3.7 multiply_subtract_fusion
  785.8 24.6 %all-gather.2.cloned.1.call-done = bf16[1024,2048]{1,0:T(8,128)(2,1)} async-done(((bf16[1024,512]{1,0:T(8,128)(2,1)}), bf16[1024,2048]{1,0:T(8,128)(2,1)}) %all-gather.2.cloned.1.call-update) | async-done | bytes 4194320 | tf_op jit(solution)/shard_map/all_gather | solution.py:1386
  810.4 4.9 copy.73
  815.4 2.0 copy.74
  (221 shorter events, 34.3 us)
Async XLA Ops:
  18.0 6.3 copy-start.36
  18.0 7.1 copy-start.50
  18.0 7.7 copy-start.57
  18.0 8.1 copy-start.70
  18.0 9.0 %copy-start.28 = (f32[256,2048]{1,0:T(8,128)S(1)}, f32[256,2048]{1,0:T(8,128)}, u32[]{:S(2)}) copy-start(f32[256,2048]{1,0:T(8,128)} %param.35) | copy-start | bytes 6291460
  18.1 56.6 %all-to-all-start = ((bf16[8,256,1024]{2,1,0:T(8,128)(2,1)}), bf16[8,256,1024]{2,1,0:T(8,128)(2,1)}, u32[]{:S(2)}, u32[]{:S(2)}) async-start(bf16[8,256,1024]{2,1,0:T(8,128)(2,1)} %bitcast.85), calls=%async_computation | async-start | bytes 8388608 | tf_op jit(solution)/shard_map/all_to_all | solution.py:1262
  23.5 455.0 %reduce-scatter.2.cloned.1.call-start = ((), (), s32[]{:S(2)}) async-start(), calls=%async_computation.4 | async-start | bytes 5242880 | tf_op jit(solution)/shard_map/reduce_scatter | solution.py:1341
  26.1 48.6 %copy-start.66 = (s32[1,2,8,128]{3,1,2,0:T(2,128)}, s32[1,2,8,128]{3,1,2,0:T(2,128)S(1)}, u32[]{:S(2)}) copy-start(s32[1,2,8,128]{3,1,2,0:T(2,128)S(1)} %copy.66) | copy-start | bytes 24580
  26.6 171.5 %copy-start.8 = (s32[256,1]{1,0:T(8,128)}, s32[256,1]{1,0:T(8,128)S(1)}, u32[]{:S(2)}) copy-start(s32[256,1]{1,0:T(8,128)S(1)} %copy.59.seg_row) | copy-start | bytes 3076
  26.7 171.4 %copy-start.14 = (s32[1,768]{1,0:T(1,128)}, s32[1,768]{1,0:T(1,128)S(1)}, u32[]{:S(2)}) copy-start(s32[1,768]{1,0:T(1,128)S(1)} %broadcast_in_dim.29.seg_col) | copy-start | bytes 9220
  26.9 171.2 %copy-start.10 = (s32[256,1]{1,0:T(8,128)}, s32[256,1]{1,0:T(8,128)S(1)}, u32[]{:S(2)}) copy-start(s32[256,1]{1,0:T(8,128)S(1)} %copy.60.pos_row) | copy-start | bytes 3076
  27.0 171.1 %copy-start.16 = (s32[1,768]{1,0:T(1,128)}, s32[1,768]{1,0:T(1,128)S(1)}, u32[]{:S(2)}) copy-start(s32[1,768]{1,0:T(1,128)S(1)} %broadcast_in_dim.31.pos_col) | copy-start | bytes 9220
  28.2 46.4 %copy-start.48 = (f32[22656]{0:T(1024)S(1)}, f32[22656]{0:T(1024)}, u32[]{:S(2)}) copy-start(f32[22656]{0:T(1024)} %param.41) | copy-start | bytes 271876
  74.6 68.6 %copy-start.53 = (f32[2048]{0:T(1024)}, f32[2048]{0:T(1024)S(1)}, u32[]{:S(2)}) copy-start(f32[2048]{0:T(1024)S(1)} %get-tuple-element.154) | copy-start | bytes 24580
  141.5 8.3 %copy-start.58 = (f32[256]{0:T(256)}, f32[256]{0:T(256)S(1)}, u32[]{:S(2)}) copy-start(f32[256]{0:T(256)S(1)} %broadcast_multiply_fusion.1) | copy-start | bytes 3076
  143.1 6.7 copy-start.62
  143.2 6.7 copy-start.60
  143.7 6.2 copy-start.25
  143.7 6.2 copy-start.42
  149.8 48.3 %copy-start = (bf16[256,2048]{1,0:T(8,128)(2,1)}, bf16[256,2048]{1,0:T(8,128)(2,1)S(1)}, u32[]{:S(2)}) copy-start(bf16[256,2048]{1,0:T(8,128)(2,1)S(1)} %fusion.26.q) | copy-start | bytes 3145732
  196.8 14.4 %copy-start.21 = (bf16[256,2048]{1,0:T(8,128)(2,1)S(1)}, bf16[256,2048]{1,0:T(8,128)(2,1)}, u32[]{:S(2)}) copy-start(bf16[256,2048]{1,0:T(8,128)(2,1)} %get-tuple-element.76) | copy-start | bytes 3145732
  198.1 13.1 %copy-start.4 = (bf16[768,128]{1,0:T(8,128)(2,1)}, bf16[768,128]{1,0:T(8,128)(2,1)S(1)}, u32[]{:S(2)}) copy-start(bf16[768,128]{1,0:T(8,128)(2,1)S(1)} %get-tuple-element.145.v) | copy-start | bytes 589828
  198.1 13.1 %copy-start.6 = (bf16[768,128]{1,0:T(8,128)(2,1)}, bf16[768,128]{1,0:T(8,128)(2,1)S(1)}, u32[]{:S(2)}) copy-start(bf16[768,128]{1,0:T(8,128)(2,1)S(1)} %get-tuple-element.146.k) | copy-start | bytes 589828
  211.2 6.3 copy-start.12
  217.5 106.2 %copy-start.18 = (f32[256,2048]{1,0:T(8,128)}, f32[256,2048]{1,0:T(8,128)S(1)}, u32[]{:S(2)}) copy-start(f32[256,2048]{1,0:T(8,128)S(1)} %get-tuple-element.158) | copy-start | bytes 6291460
  295.5 14.6 %copy-start.68 = (bf16[2048,2048]{1,0:T(8,128)(2,1)S(1)}, bf16[2048,2048]{1,0:T(8,128)(2,1)}, u32[]{:S(2)}) copy-start(bf16[2048,2048]{1,0:T(8,128)(2,1)} %get-tuple-element.86) | copy-start | bytes 25165828
  326.3 47.5 %slice-start.1 = ((s8[8388608]{0:T(1024)(128)(4,1)}), s8[4194304]{0:T(1024)(128)(4,1)S(1)}, s32[]{:S(2)}) async-start(s8[8388608]{0:T(1024)(128)(4,1)} %bitcast.100), calls=%async_computation.7 | async-start | bytes 8388608
  347.1 12.8 %copy-start.69 = (bf16[1024,2048]{1,0:T(8,128)(2,1)S(1)}, bf16[1024,2048]{1,0:T(8,128)(2,1)}, u32[]{:S(2)}) copy-start(bf16[1024,2048]{1,0:T(8,128)(2,1)} %get-tuple-element.84) | copy-start | bytes 12582916
  347.1 26.6 %slice-start.2 = ((s8[8388608]{0:T(1024)(128)(4,1)}), s8[4194304]{0:T(1024)(128)(4,1)S(1)}, s32[]{:S(2)}) async-start(s8[8388608]{0:T(1024)(128)(4,1)} %bitcast.100), calls=%async_computation.8 | async-start | bytes 8388608
  359.9 13.9 %copy-start.24 = (bf16[1024,2048]{1,0:T(8,128)(2,1)S(1)}, bf16[1024,2048]{1,0:T(8,128)(2,1)}, u32[]{:S(2)}) copy-start(bf16[1024,2048]{1,0:T(8,128)(2,1)} %get-tuple-element.88) | copy-start | bytes 12582916
  385.7 88.5 %copy-start.19 = (f32[256,2048]{1,0:T(8,128)S(1)}, f32[256,2048]{1,0:T(8,128)}, u32[]{:S(2)}) copy-start(f32[256,2048]{1,0:T(8,128)} %copy-done.18) | copy-start | bytes 6291460
  483.3 37.4 %all-to-all-start.1 = ((bf16[8,256,512]{2,1,0:T(8,128)(2,1)}), bf16[8,256,512]{2,1,0:T(8,128)(2,1)}, u32[]{:S(2)}, u32[]{:S(2)}) async-start(bf16[8,256,512]{2,1,0:T(8,128)(2,1)} %bitcast.86), calls=%async_computation.2 | async-start | bytes 4194304 | tf_op jit(solution)/shard_map/all_to_all | solution.py:1262
  489.9 6.3 copy-start.33
  490.0 6.3 copy-start.1
  490.0 6.3 copy-start.5
  490.0 6.3 copy-start.7
  490.0 6.3 copy-start.9
  490.0 6.3 copy-start.11
  490.0 6.2 copy-start.15
  490.0 6.2 copy-start.17
  514.5 6.2 copy-start.65
  526.1 97.9 %copy-start.26 = (bf16[256,2048]{1,0:T(8,128)(2,1)S(1)}, bf16[256,2048]{1,0:T(8,128)(2,1)}, u32[]{:S(2)}) copy-start(bf16[256,2048]{1,0:T(8,128)(2,1)} %copy-done.25) | copy-start | bytes 3145732
  659.7 59.9 %all-to-all-start.2 = ((bf16[8,256,512]{2,1,0:T(8,128)(2,1)}), bf16[8,256,512]{2,1,0:T(8,128)(2,1)S(1)}, u32[]{:S(2)}, u32[]{:S(2)}) async-start(bf16[8,256,512]{2,1,0:T(8,128)(2,1)} %bitcast.88), calls=%async_computation.3 | async-start | bytes 4194304 | tf_op jit(solution)/shard_map/all_to_all | solution.py:1262
  663.3 147.1 %all-gather.2.cloned.1.call-start = ((), (), s32[]{:S(2)}) async-start(), calls=%async_computation.5 | async-start | bytes 5242880 | tf_op jit(solution)/shard_map/all_gather | solution.py:1386
  732.0 36.6 %copy-start.51 = (f32[64,256]{1,0:T(8,128)S(1)}, f32[64,256]{1,0:T(8,128)}, u32[]{:S(2)}) copy-start(f32[64,256]{1,0:T(8,128)} %param.29) | copy-start | bytes 196612
  732.0 38.3 %copy-start.35 = (f32[256,512]{1,0:T(8,128)S(1)}, f32[256,512]{1,0:T(8,128)}, u32[]{:S(2)}) copy-start(f32[256,512]{1,0:T(8,128)} %param.26) | copy-start | bytes 1572868
  732.0 42.7 %copy-start.49 = (f32[22656]{0:T(1024)S(1)}, f32[22656]{0:T(1024)}, u32[]{:S(2)}) copy-start(f32[22656]{0:T(1024)} %param.41) | copy-start | bytes 271876
  732.0 42.7 %copy-start.55 = (f32[22656]{0:T(1024)S(1)}, f32[22656]{0:T(1024)}, u32[]{:S(2)}) copy-start(f32[22656]{0:T(1024)} %param.42) | copy-start | bytes 271876
  (32 other events, 107.3 us)
Sparse Core Ops, SparseCore 0:
  326.4 82.9 reduce-scatter.1
  723.5 86.8 all-gather.1

commit v5 on v4

--- a/solution.py
+++ b/solution.py
@@ -478,16 +478,21 @@
                 self.load(place, c).start()
 
     def prepared(self):
-        for place in self.places():
-            for c in range(self.chunks):
-                self.load(place, c).wait()
+        pass
 
     def start(self):
-        for place in self.places():
+        self.send_across(self.places()[:1])
+
+    def send_across(self, places):
+        for place in places:
             for c in range(self.chunks):
                 self.across(place, c).start()
 
+    def loaded(self, place, c):
+        self.load(place, c).wait()
+
     def base(self, place, c):
+        self.loaded(place, c)
         self.across(place, c).wait_recv()
         total = self.mine[place, self.span(c)].astype(jnp.float32)
         return total + self.other[place, self.span(c)].astype(jnp.float32)
@@ -519,6 +524,10 @@
                         yield e, c, way
 
     def steps(self):
+        yield 0.0, functools.partial(self.send_across, self.places()[1:])
+        yield from self.sum_steps()
+
+    def sum_steps(self):
         when = 0.0
         for e, c, way in self.every():
             yield when, functools.partial(self.step, e, c, way)
@@ -572,10 +581,10 @@
     def prepare(self):
         pass
 
-    def prepared(self):
+    def start(self):
         pass
 
-    def start(self):
+    def loaded(self, place, c):
         pass
 
     def steps(self):
@@ -584,7 +593,7 @@
             for here in (False, True):
                 yield when, functools.partial(self.work, i, place, here)
                 when += self.cost
-        for when, step in super().steps():
+        for when, step in self.sum_steps():
             place = 0
             if len(step.args) == 3:
                 e, _, way = step.args
@@ -629,6 +638,76 @@
     def finish(self):
         for copy in self.copies:
             copy.wait()
+
+
+class Pieces:
+    def __init__(self, ref, begin):
+        self.ref, self.begin, self.dtype = ref, begin, ref.dtype
+
+    def __setitem__(self, span, value):
+        pieces, _, cols = self.ref.shape
+        for k in range(pieces):
+            rows = pl.ds(self.begin + span.start, span.size)
+            self.ref[k, rows] = value[:, k * cols : (k + 1) * cols]
+
+
+class Later:
+    def __init__(self, job, when):
+        self.job, self.when = job, when
+
+    def prepare(self):
+        pass
+
+    def prepared(self):
+        pass
+
+    def start(self):
+        pass
+
+    def steps(self):
+        yield self.when, self.job.start
+
+    def finish(self):
+        self.job.finish()
+
+
+class RowProduct:
+    @staticmethod
+    def scratch(weight):
+        return [pltpu.VMEM(weight.shape, weight.dtype), DMA]
+
+    def __init__(self, left, weight, turn, bias, out, scratch, begin, cost):
+        self.left, self.turn, self.bias, self.out = left, turn, bias, out
+        self.held, self.begin, self.cost = scratch[0], begin, cost
+        self.copy = pltpu.make_async_copy(weight, scratch[0], scratch[1])
+        self.tile = 256
+
+    def prepare(self):
+        self.copy.start()
+
+    def prepared(self):
+        pass
+
+    def start(self):
+        pass
+
+    def work(self, j):
+        span = pl.ds(j * self.tile, self.tile)
+        if self.turn:
+            total = product(self.left[...], self.held[span], 1, 1)
+        else:
+            total = product(self.left[...], self.held[:, span], 1, 0)
+        if self.bias is not None:
+            total += self.bias[:, span]
+        self.out[:, span] = total.astype(self.out.dtype)
+
+    def steps(self):
+        yield self.begin, self.copy.wait
+        for j in range(self.out.shape[1] // self.tile):
+            yield self.begin + j * self.cost, functools.partial(self.work, j)
+
+    def finish(self):
+        pass
 
 
 def run_jobs(met, jobs):
@@ -738,17 +817,27 @@
 
 
 def gather_lines(n_dp, n, query, project, shared):
+    low = jnp.bfloat16
     sems = LineGather.sems(n, 1)
-
-    def kernel(a, b, c, a_out, b_out, c_out, *refs):
+    shapes = [
+        jax.ShapeDtypeStruct(query.shape, low),
+        jax.ShapeDtypeStruct(project.shape[::-1], low),
+        jax.ShapeDtypeStruct(shared.shape, low),
+    ]
+
+    def kernel(a, b, c, a_out, b_out, c_out, a_low, b_low, c_low, *refs):
         parts = Parts(refs)
         at = Place(n_dp, n)
+        met = at.greet(line=True)
+        a_low[...] = a[...].astype(low)
+        b_low[...] = b[...].T.astype(low)
+        c_low[...] = c[...].astype(low)
         run_jobs(
-            at.greet(line=True),
+            met,
             [
-                line_gather(at, a, a_out, 1, 1, parts.take(sems), 6.0),
-                line_gather(at, c, c_out, 0, 1, parts.take(sems), 6.5),
-                line_gather(at, b, b_out, 1, 1, parts.take(sems), 12.0),
+                line_gather(at, a_low, a_out, 1, 1, parts.take(sems), 6.0),
+                line_gather(at, c_low, c_out, 0, 1, parts.take(sems), 6.5),
+                line_gather(at, b_low, b_out, 1, 1, parts.take(sems), 12.0),
             ],
         )
 
@@ -756,9 +845,9 @@
         kernel,
         (query, project, shared),
         3,
-        (like(query, 1, n), like(project, 1, n), like(shared, n, 1)),
+        (like(shapes[0], 1, n), like(shapes[1], 1, n), like(shapes[2], n, 1)),
         0,
-        sems * 3,
+        [pltpu.VMEM(x.shape, low) for x in shapes] + sems * 3,
         1,
         "gather_lines",
     )
@@ -814,20 +903,23 @@
     )
 
 
-def shared_and_project(n_dp, n, owned, shared_rows, project, gathered):
+def shared_and_project(n_dp, n, owned, shared_rows, project, rows, bias, query, gathered):
     chips, chunks = n_dp // 2, 2
     total, cols = owned.shape[0], owned.shape[1] // 2
     half = total // 2
     small, line = LineGather.sems(n, 1), LineGather.sems(n, chunks)
     ring = RingGather.sems(chips, chunks)
 
-    def kernel(y, x, a, _, x_out, a_out, y_out, *refs):
+    made = RowProduct.scratch(query)
+
+    def kernel(y, x, a, r, b, w, _, q_out, x_out, a_out, y_out, *refs):
         parts = Parts(refs)
         at = Place(n_dp, n)
         lower = pl.ds(half, half)
         run_jobs(
             at.greet(line=True, ring=True),
             [
+                RowProduct(r, w, False, b, q_out, parts.take(made), 8.0, 3.0),
                 line_gather(at, x, x_out, 0, 1, parts.take(small), 4.0),
                 ring_gather(at, a, a_out, 0, chunks, parts.take(ring), 22.0),
                 line_gather(
@@ -844,30 +936,43 @@
 
     return move(
         kernel,
-        (owned, shared_rows, project, gathered),
-        3,
-        (like(shared_rows, n, 1), like(project, n_dp, 1), like(gathered, 1, 1)),
-        0,
-        small + ring + line,
+        (owned, shared_rows, project, rows, bias, query, gathered),
+        5,
+        (
+            jax.ShapeDtypeStruct((rows.shape[0], query.shape[1]), rows.dtype),
+            like(shared_rows, n, 1),
+            like(project, n_dp, 1),
+            like(gathered, 1, 1),
+        ),
+        1,
+        made + small + ring + line,
         3,
         "shared_and_project",
-        {3: 2},
+        {6: 3},
     )
 
 
 def rows_and_expanded(n_dp, n, x, expand, shrink):
+    low = jnp.bfloat16
+    shapes = [
+        jax.ShapeDtypeStruct(expand.shape, low),
+        jax.ShapeDtypeStruct(shrink.shape[::-1], low),
+    ]
     chips, chunks, halves = n_dp // 2, 4, 2
     line, ring = LineGather.sems(n, chunks), RingGather.sems(chips, halves)
 
-    def kernel(x_ref, a, b, x_out, a_out, b_out, *refs):
+    def kernel(x_ref, a, b, x_out, a_out, b_out, a_low, b_low, *refs):
         parts = Parts(refs)
         at = Place(n_dp, n)
+        met = at.greet(line=True, ring=True)
+        a_low[...] = a[...].astype(low)
+        b_low[...] = b[...].T.astype(low)
         run_jobs(
-            at.greet(line=True, ring=True),
+            met,
             [
                 line_gather(at, x_ref, x_out, 0, chunks, parts.take(line), 22.0),
-                ring_gather(at, a, a_out, 0, halves, parts.take(ring), 44.0),
-                ring_gather(at, b, b_out, 0, halves, parts.take(ring), 44.0),
+                ring_gather(at, a_low, a_out, 0, halves, parts.take(ring), 44.0),
+                ring_gather(at, b_low, b_out, 0, halves, parts.take(ring), 44.0),
             ],
         )
 
@@ -875,9 +980,9 @@
         kernel,
         (x, expand, shrink),
         3,
-        (like(x, n, 1), like(expand, n_dp, 1), like(shrink, n_dp, 1)),
+        (like(x, n, 1), like(shapes[0], n_dp, 1), like(shapes[1], n_dp, 1)),
         0,
-        line + ring * 2,
+        [pltpu.VMEM(x.shape, low) for x in shapes] + line + ring * 2,
         4,
         "rows_and_expanded",
     )
@@ -914,7 +1019,7 @@
     )
 
 
-def scatter_shared(n_dp, n, x, result, a, dq, dz, o):
+def scatter_shared(n_dp, n, x, result, a, dq, dz, o, query):
     chips, chunks = n_dp // 2, 4
     block = (x.shape[0] // n, x.shape[1])
     w_block = (a.shape[1] // n_dp, dq.shape[1])
@@ -922,13 +1027,19 @@
     line = LineGather.sems(n, chunks)
     ring = ProductScatter.scratch(chips, chunks, w_block, x.dtype)
 
-    def kernel(x_ref, y, a_ref, dq_ref, dz_ref, o_ref, x_out, a_out, b_out, y_out, *refs):
+    made = RowProduct.scratch(query)
+
+    def kernel(
+        x_ref, y, a_ref, dq_ref, dz_ref, o_ref, w, x_out, w_out, r_out, y_out, *refs
+    ):
         parts = Parts(refs)
         at = Place(n_dp, n)
+        a_out, b_out = Pieces(w_out, 0), Pieces(w_out, w_block[0])
         run_jobs(
             at.greet(line_all=True, ring=True),
             [
                 line_exchange(at, x_ref, x_out, 0, parts.take(small)),
+                RowProduct(dq_ref, w, True, None, r_out, parts.take(made), 30.0, 4.0),
                 line_gather(at, y, y_out, 1, chunks, parts.take(line), 22.0),
                 product_scatter(at, dz_ref, o_ref, b_out, chunks, parts.take(ring), 24.0, 1.0),
                 product_scatter(at, a_ref, dq_ref, a_out, chunks, parts.take(ring), 24.0, 1.0),
@@ -937,16 +1048,16 @@
 
     return move(
         kernel,
-        (x, result, by_lanes(a, n_dp), dq, by_lanes(dz, n_dp), o),
+        (x, result, by_lanes(a, n_dp), dq, by_lanes(dz, n_dp), o, query),
         6,
         (
             jax.ShapeDtypeStruct(block, jnp.float32),
-            jax.ShapeDtypeStruct(w_block, x.dtype),
-            jax.ShapeDtypeStruct(w_block, x.dtype),
+            jax.ShapeDtypeStruct((n, 2 * w_block[0], w_block[1] // n), x.dtype),
+            jax.ShapeDtypeStruct(dq.shape, jnp.float32),
             like(result, 1, n),
         ),
         3,
-        small + line + ring * 2,
+        small + made + line + ring * 2,
         6,
         "scatter_shared",
     )
@@ -957,10 +1068,12 @@
     count, width = rows.shape
     cols = width // n
     s_block = (shared.shape[0] // n_dp, shared.shape[1])
+    p_block = (s_block[0] // n, s_block[1])
     switch = LineSwitch.sems(n)
+    small = LineExchange.scratch(n, p_block, shared.dtype)
     ring = RingScatter.scratch(chips, 1, s_block, shared.dtype)
 
-    def kernel(x, c, c_out, x_out, *refs):
+    def kernel(x, c, c_out, x_out, c_sum, *refs):
         parts = Parts(refs)
         at = Place(n_dp, n)
         run_jobs(
@@ -972,7 +1085,8 @@
                     x_out.at[pl.ds(at.t * count, count)],
                     parts.take(switch),
                 ),
-                ring_scatter(at, c, c_out, 0, 1, parts.take(ring), 4.0),
+                ring_scatter(at, c, c_sum, 0, 1, parts.take(ring), 4.0),
+                Later(line_exchange(at, c_sum, c_out, 0, parts.take(small)), 15.0),
             ],
         )
 
@@ -981,43 +1095,13 @@
         (rows, shared),
         1,
         [
-            jax.ShapeDtypeStruct(s_block, shared.dtype),
+            jax.ShapeDtypeStruct(p_block, jnp.float32),
             jax.ShapeDtypeStruct((n * count, cols), rows.dtype),
         ],
         1,
-        switch + ring,
+        [pltpu.VMEM(s_block, shared.dtype)] + switch + ring + small,
         7,
         "cols_and_shared",
-    )
-
-
-def scatter_grads(n_dp, n, query, project, shared):
-    w_block = (query.shape[0], query.shape[1] // n)
-    s_block = (shared.shape[0] // n, shared.shape[1])
-    line = LineScatter.scratch(n, 1, w_block, query.dtype)
-    small = LineExchange.scratch(n, s_block, shared.dtype)
-
-    def kernel(a, b, c, a_out, b_out, c_out, *refs):
-        parts = Parts(refs)
-        at = Place(n_dp, n)
-        run_jobs(
-            at.greet(line_all=True),
-            [
-                line_scatter(at, a, a_out, 1, 1, parts.take(line), 12.0),
-                line_scatter(at, b, b_out, 1, 1, parts.take(line), 12.0),
-                line_exchange(at, c, c_out, 0, parts.take(small)),
-            ],
-        )
-
-    return move(
-        kernel,
-        (query, project, shared),
-        3,
-        [jax.ShapeDtypeStruct(block, jnp.float32) for block in (w_block, w_block, s_block)],
-        3,
-        line * 2 + small,
-        8,
-        "scatter_grads",
     )
 
 
@@ -1276,7 +1360,7 @@
         )
     )
     query_line, project_line, shared_line = gather_lines(
-        n_dp, n, low(query_here), low(project_here).T, low(shared_here)
+        n_dp, n, query_here, project_here, shared_here
     )
     arrived, query_line, shared_line = lax.optimization_barrier(
         (exchange(packed), query_line, shared_line)
@@ -1304,12 +1388,19 @@
     inputs_float = owned_rows.astype(jnp.float32)
     normed_one, norm_one_back = jax.vjp(layer_norm, inputs_float, gain_one, shift_one)
     normed_low = normed_one.astype(jnp.bfloat16)
-    queries = (mul_plain(normed_low, query_all) + query_bias).astype(jnp.bfloat16)
     shared_out = mul_plain(normed_low, shared_all) + jnp.concatenate(
         [jnp.zeros((head_size,), jnp.float32), value_bias]
     )
-    shared_rows, project_all_t, owned_grad = shared_and_project(
-        n_dp, n, owned, low(shared_out), project_line, owned_grad
+    queries, shared_rows, project_all_t, owned_grad = shared_and_project(
+        n_dp,
+        n,
+        owned,
+        low(shared_out),
+        project_line,
+        normed_low,
+        query_bias[None],
+        query_all,
+        owned_grad,
     )
     window = min(row_count, part_rows + longest)
     window_start = jnp.maximum((t + 1) * part_rows - window, 0)
@@ -1327,7 +1418,7 @@
     normed_two, norm_two_back = jax.vjp(layer_norm, hidden_one, gain_two, shift_two)
 
     normed_two_low, expand_cols, shrink_rows_t = rows_and_expanded(
-        n_dp, n, low(normed_two), low(expand_weight), low(shrink_weight).T
+        n_dp, n, low(normed_two), expand_weight, shrink_weight
     )
     expand_pre = mul_plain(normed_two_low, expand_cols) + expand_bias
     activated, gelu_back = jax.vjp(gelu_tanh, expand_pre)
@@ -1363,27 +1454,36 @@
     query_grad, shared_part = attend_back(
         queries, heads_grad, log_total, key_rows, value_rows, masks, row_count
     )
-    shared_grad, query_sum, project_sum, output_rows = scatter_shared(
-        n_dp, n, shared_part, output_cols, normed_low, query_grad, branch_grad, heads_out
+    shared_grad, weight_sums, normed_one_grad, output_rows = scatter_shared(
+        n_dp,
+        n,
+        shared_part,
+        output_cols,
+        normed_low,
+        query_grad,
+        branch_grad,
+        heads_out,
+        query_all,
     )
     shared_grad = low(shared_grad)
     query_bias_grad = jnp.sum(query_grad.astype(jnp.float32), axis=0)
-    normed_one_grad = mul_right_t(query_grad, query_all) + mul_right_t(shared_grad, shared_all)
+    normed_one_grad = normed_one_grad + mul_right_t(shared_grad, shared_all)
     inputs_from_norm, gain_one_grad, shift_one_grad = norm_one_back(normed_one_grad)
     input_result = (hidden_grad + inputs_from_norm).astype(jnp.bfloat16)
     shared_weight_grad = mul_left_t(normed_low, shared_grad)
     value_bias_grad = jnp.sum(shared_grad[:, head_size:].astype(jnp.float32), axis=0)
 
-    shared_sum, input_cols = cols_and_shared(n_dp, n, input_result, low(shared_weight_grad))
-    packed, query_sum, project_sum, shared_sum = lax.optimization_barrier(
-        (pack(input_cols, recv_slots), query_sum, project_sum, shared_sum)
-    )
-    query_part, project_part_t, shared_piece = scatter_grads(
-        n_dp, n, query_sum, project_sum, shared_sum
-    )
-    project_part = turned(project_part_t)
-    arrived, query_part = lax.optimization_barrier((exchange(packed), query_part))
-    grad_rows = lax.all_gather(unpack(arrived, send_slots), "tensor", axis=1, tiled=True)
+    shared_piece, input_cols = cols_and_shared(n_dp, n, input_result, low(shared_weight_grad))
+    input_cols, weight_sums = lax.optimization_barrier((input_cols, weight_sums))
+    grads = lax.psum_scatter(
+        weight_sums.reshape(-1, part_cols), "tensor", scatter_dimension=0, tiled=True
+    )
+    back = unpack(exchange(pack(input_cols, recv_slots)), send_slots)
+    back, grads = lax.optimization_barrier((back, grads))
+    grad_rows = lax.all_gather(back, "tensor", axis=1, tiled=True)
+    tall = grads.shape[0] // 2
+    query_part = grads[:tall].astype(jnp.float32)
+    project_part = turned(grads[tall:].astype(jnp.float32))
     output_back = output_rows.astype(jnp.float32)
     token_rms = jnp.sqrt(jnp.mean(output_back * output_back, axis=1))
 
@@ -1416,7 +1516,7 @@
     everything = jnp.concatenate(
         [vector_part, local_squares[None], jnp.zeros((padded - length - 1,), jnp.float32)]
     )
-    summed = sum_all(everything.reshape(padded // 128, 128), n_dp, n, 9).reshape(padded)
+    summed = sum_all(everything.reshape(padded // 128, 128), n_dp, n, 8).reshape(padded)
     vector_grad, weight_squares = summed[:length], summed[length]
     grad_size = jnp.sqrt(weight_squares + jnp.sum(vector_grad * vector_grad))
     clip_factor = jnp.minimum(1.0, clip_level / (grad_size + 1e-06))

time: 835 us -> 809 us (0.969)
  Pallas kernels: 541 us -> 492 us
  blocking collectives: 0 us -> 29.8 us
  matrix products: 146 us -> 134 us
  local copies, waits for them, and re-layouts: 25.2 us -> 34.9 us
    pallas_call x8 -> x7, Pallas kernels: 488 us -> 441 us  [move(): pl.pallas_call(kernel, out_shape=tuple(outs), in_specs=[IN_VMEM if i < in...]
    all_to_all x0 -> x1, blocking collectives: none -> 29.8 us  [exchange(): return lax.all_to_all(packed, 'dp', split_axis=0, concat_axis=0, tiled=True)]
    unnamed x153 -> x136, local copies, waits for them, and re-layouts: 14.1 us -> 23.3 us
    dot_general x8 -> x7, matrix products: 62.5 us -> 54.5 us  [mul_plain(): return jnp.dot(left, right, preferred_element_type=jnp.float32)]
    dot_general x5 -> x4, matrix products: 39.5 us -> 35 us  [mul_right_t(): lax.dot_general(left, right, (((1,), (1,)), ((), ())), preferred_element_...]
  transfers between devices with their start and end apart: 5 -> 5, of which waited for: 1 -> 3; matrix products, arithmetic and copies ran while one was open for 14% -> 15% of each run, Pallas kernels for 28% -> 21%
where the time goes in v5:
time: 809 us; the launch traced here: 801 us
  Pallas kernels  492 us (61%)
  matrix products  134 us (17%)
  other arithmetic  49.9 us (6%)
  local copies, waits for them, and re-layouts  34.9 us (4%)
  waiting for transfers between devices  30.2 us (4%)
  blocking collectives  29.8 us (4%)
  between operations  20.6 us (3%)
  starting transfers between devices  9.8 us (1%)
    pallas_call x7, Pallas kernels, move(): pl.pallas_call(kernel, out_shape=tuple(outs), in_specs=[IN_VMEM if i < in...  441 us
    dot_general x7, matrix products, mul_plain(): return jnp.dot(left, right, preferred_element_type=jnp.float32)  54.5 us
    dot_general x6, matrix products, mul_left_t(): lax.dot_general(left, right, (((0,), (0,)), ((), ())), preferred_element_...  44.3 us
    dot_general x4, matrix products, mul_right_t(): lax.dot_general(left, right, (((1,), (1,)), ((), ())), preferred_element_...  35 us
    all_to_all x1, blocking collectives, exchange(): return lax.all_to_all(packed, 'dp', split_axis=0, concat_axis=0, tiled=True)  29.8 us
    unnamed x136, local copies, waits for them, and re-layouts  23.3 us
    all_gather x1, waiting for transfers between devices, local(): grad_rows = lax.all_gather(back, 'tensor', axis=1, tiled=True)  21.3 us
    pallas_call x1, Pallas kernels, sum_all(): pl.pallas_call(functools.partial(sum_all_kernel, n_dp, n), out_shape=jax....  20.4 us
  transfers between devices with their start and end apart: 5, of which 3 were waited for; matrix products, arithmetic and copies ran while one was open for 15% of the time, Pallas kernels for 21%

profile of v5, /device:TPU:0, one launch (start us, length us, event | category | flops | bytes accessed | tf_op | source)
XLA Modules:
  0.0 801.4 jit_solution(14478557299891963550)
XLA Ops:
  11.9 6.1 fusion.19
  18.0 5.3 all-to-all-start
  24.6 43.9 %gather_lines.1 = (bf16[256,2048]{1,0:T(8,128)(2,1)}, bf16[256,2048]{1,0:T(8,128)(2,1)}, bf16[256,256]{1,0:T(8,128)(2,1)}) custom-call(f32[256,512]{1,0:T(8,128)} %a.1, f32[512,256]{1,0:T(8,128)} %b.1, f32[64,256]{1,0:T(8,128)} %c), custom_call_target="tpu_custom_call" | custom-call | tf_op jit(solution)/shard_map/gather_lines/pallas_call | solution.py:739
  69.2 3.4 all-to-all-done
  72.6 8.1 %fusion.39.x.y = bf16[1024,1024]{1,0:T(8,128)(2,1)} fusion(bf16[2048,1024]{1,0:T(8,128)(2,1)} %bitcast.3, s32[2048]{0:T(1024)S(1)} %bitcast.89), kind=kOutput, calls=%fused_computation.78 | convolution fusion | flops 4298113024 | bytes 6299648 | tf_op jit(solution)/shard_map/dot_general | solution.py:44
  80.6 59.1 %rows_and_weights.1 = (bf16[256,2048]{1,0:T(8,128)(2,1)}, bf16[1024,2048]{1,0:T(8,128)(2,1)}, bf16[2048,2048]{1,0:T(8,128)(2,1)}, bf16[2048,256]{1,0:T(8,128)(2,1)}) custom-call(bf16[1024,1024]{1,0:T(8,128)(2,1)} %fusion.39.x.y, bf16[256,2048]{1,0:T(8,128)(2,1)} %get-tuple-element.70.a, bf16[256,256]{1,0:T(8,128)(2,1)} %get-tuple-element.71.b), custom_call_target="tpu_custom_call" | custom-call | tf_op jit(solution)/shard_map/rows_and_weights/pallas_call | solution.py:739
  144.7 47.2 %shared_and_project.1 = (bf16[256,2048]{1,0:T(8,128)(2,1)}, bf16[1024,256]{1,0:T(8,128)(2,1)}, bf16[2048,2048]{1,0:T(8,128)(2,1)}, bf16[1024,2048]{1,0:T(8,128)(2,1)}) custom-call(bf16[1024,1024]{1,0:T(8,128)(2,1)} %fusion.39.x.y, bf16[256,256]{1,0:T(8,128)(2,1)} %fusion.43.x, ...), custom_call_target="tpu_custom_call", output_to_operand_aliasing={{3}: (6, {})} | custom-call | tf_op jit(solution)/shard_map/shared_and_project/pallas_call | solution.py:739
  194.5 13.0 %attend.1 = (bf16[256,2048]{1,0:T(8,128)(2,1)S(1)}, f32[256,2048]{1,0:T(8,128)S(1)}) custom-call(bf16[256,2048]{1,0:T(8,128)(2,1)S(1)} %copy-done.2, bf16[768,128]{1,0:T(8,128)(2,1)S(1)} %get-tuple-element.207.k, bf16[768,128]{1,0:T(8,128)(2,1)S(1)} %get-tuple-element.206.v, s32[256,1]{1,0:T(8,128)S(1)} %copy.68.seg_row, ...), custom_call_target="tpu_custom_call" | custom-call | tf_op jit(solution)/shard_map/attend/pallas_call | solution.py:1166
  207.5 6.3 fusion.76
  215.6 77.1 %rows_and_expanded.1 = (bf16[1024,2048]{1,0:T(8,128)(2,1)}, bf16[2048,2048]{1,0:T(8,128)(2,1)}, bf16[2048,2048]{1,0:T(8,128)(2,1)}) custom-call(bf16[256,2048]{1,0:T(8,128)(2,1)} %add_convert_fusion.2.x_ref, f32[256,2048]{1,0:T(8,128)} %a.2, f32[2048,256]{1,0:T(8,128)} %b.2), custom_call_target="tpu_custom_call" | custom-call | tf_op jit(solution)/shard_map/rows_and_expanded/pallas_call | solution.py:739
  292.7 14.6 %fusion.77 = f32[1024,2048]{1,0:T(8,128)} fusion(bf16[1024,2048]{1,0:T(8,128)(2,1)} %get-tuple-element.81, bf16[2048,2048]{1,0:T(8,128)(2,1)} %get-tuple-element.82), kind=kOutput, calls=%fused_computation.148 | convolution fusion | flops 8589934592 | bytes 20971520 | tf_op jit(solution)/shard_map/dot_general | solution.py:34
  307.2 13.6 %convolution_convert_fusion.3 = bf16[1024,2048]{1,0:T(8,128)(2,1)} fusion(bf16[2048,2048]{1,0:T(8,128)(2,1)S(1)} %copy-done.56, f32[1024,2048]{1,0:T(8,128)} %fusion.77, f32[2048]{0:T(1024)S(1)} %get-tuple-element.209), kind=kOutput, calls=%fused_computation.29 | convolution fusion | flops 8613003264 | bytes 20979712 | tf_op jit(solution)/shard_map/dot_general | solution.py:38
  320.9 2.5 fusion.44
  323.5 19.1 %convert_reduce_fusion = (f32[2048]{0:T(1024)S(1)}, bf16[1024,2048]{1,0:T(8,128)(2,1)S(1)}) fusion(f32[1024,2048]{1,0:T(8,128)} %fusion.77, f32[2048]{0:T(1024)S(1)} %get-tuple-element.209, bf16[1024,2048]{1,0:T(8,128)(2,1)} %get-tuple-element.85, bf16[2048,2048]{1,0:T(8,128)(2,1)} %get-tuple-element.83), kind=kOutput, calls=%fused_computation.10 | convolution fusion | flops 8638167040 | bytes 25182208 | tf_op jit(solution)/shard_map/dot_general | solution.py:34
  344.6 12.7 %convolution_convert_fusion.2.x_ref = bf16[1024,2048]{1,0:T(8,128)(2,1)} fusion(bf16[1024,2048]{1,0:T(8,128)(2,1)S(1)} %get-tuple-element.199, bf16[2048,2048]{1,0:T(8,128)(2,1)} %get-tuple-element.82), kind=kOutput, calls=%fused_computation.28 | convolution fusion | flops 8592031744 | bytes 16777216 | tf_op jit(solution)/shard_map/dot_general | solution.py:38
  357.3 13.8 %convolution_convert_fusion.1.a = bf16[2048,2048]{1,0:T(8,128)(2,1)} fusion(bf16[1024,2048]{1,0:T(8,128)(2,1)S(1)} %copy-done.57, bf16[1024,2048]{1,0:T(8,128)(2,1)} %copy-done.60), kind=kOutput, calls=%fused_computation.21 | convolution fusion | flops 8594128896 | bytes 16777216 | tf_op jit(solution)/shard_map/dot_general | solution.py:44
  371.1 11.9 %convolution_convert_fusion.b = bf16[2048,2048]{1,0:T(8,128)(2,1)} fusion(bf16[1024,2048]{1,0:T(8,128)(2,1)S(1)} %copy-done.19, f32[1024,2048]{1,0:T(8,128)S(1)} %bitcast.95, f32[2048]{0:T(1024)S(1)} %get-tuple-element.209), kind=kOutput, calls=%fused_computation.20 | convolution fusion | flops 8615100416 | bytes 20979712 | tf_op jit(solution)/shard_map/dot_general | solution.py:44
  383.0 86.3 %scatter_expanded.1 = (f32[256,2048]{1,0:T(8,128)}, f32[256,2048]{1,0:T(8,128)}, f32[256,2048]{1,0:T(8,128)}) custom-call(bf16[1024,2048]{1,0:T(8,128)(2,1)} %convolution_convert_fusion.2.x_ref, bf16[2048,2048]{1,0:T(8,128)(2,1)} %convolution_convert_fusion.1.a, bf16[2048,2048]{1,0:T(8,128)(2,1)} %convolution_convert_fusion.b), custom_call_target="tpu_custom_call" | custom-call | tf_op jit(solution)/shard_map/scatter_expanded/pallas_call | solution.py:739
  469.3 2.3 multiply_reduce_fusion.2
  471.6 4.8 fusion.24
  476.4 4.4 all-to-all-start.1
  480.9 2.8 fusion.72
  483.8 2.4 convert_reduce_fusion.3
  486.2 6.1 convolution_convert_fusion.5.do
  492.4 17.7 %attend_back.1 = (bf16[256,2048]{1,0:T(8,128)(2,1)S(1)}, bf16[1024,256]{1,0:T(8,128)(2,1)S(1)}) custom-call(bf16[256,2048]{1,0:T(8,128)(2,1)S(1)} %copy-done.3, bf16[256,2048]{1,0:T(8,128)(2,1)S(1)} %convolution_convert_fusion.5.do, f32[256,2048]{1,0:T(8,128)S(1)} %get-tuple-element.87.log_total, bf16[768,128]{1,0:T(8,128)(2,1)S(1)} %copy-done.7, ...), custom_call_target="tpu_custom_call" | custom-call | tf_op jit(solution)/shard_map/attend_back/pallas_call | solution.py:1185
  511.9 5.4 fusion.40.y
  517.2 96.5 %scatter_shared.1 = (f32[256,256]{1,0:T(8,128)}, bf16[4,512,512]{2,1,0:T(8,128)(2,1)}, f32[256,2048]{1,0:T(8,128)}, bf16[1024,2048]{1,0:T(8,128)(2,1)}) custom-call(bf16[1024,256]{1,0:T(8,128)(2,1)} %copy-done.9, bf16[1024,512]{1,0:T(8,128)(2,1)} %fusion.40.y, bf16[256,2048]{1,0:T(8,128)(2,1)} %copy-done.17, bf16[256,2048]{1,0:T(8,128)(2,1)} %copy-done, ...), custom_call_target="tpu_custom_call" | custom-call | tf_op jit(solution)/shard_map/scatter_shared/pallas_call | solution.py:739
  616.4 2.4 fusion.61
  620.4 3.3 convert_reduce_fusion.2
  623.7 31.1 %cols_and_shared.1 = (f32[64,256]{1,0:T(8,128)}, bf16[1024,512]{1,0:T(8,128)(2,1)}) custom-call(bf16[256,2048]{1,0:T(8,128)(2,1)} %get-tuple-element.205.x, bf16[2048,256]{1,0:T(8,128)(2,1)} %convolution_convert_fusion.4.c), custom_call_target="tpu_custom_call" | custom-call | tf_op jit(solution)/shard_map/cols_and_shared/pallas_call | solution.py:739
  654.9 2.4 copy.81
  658.5 2.6 fusion.25
  661.1 29.8 %all_to_all.15 = bf16[8,256,512]{2,1,0:T(8,128)(2,1)S(1)} all-to-all(bf16[8,256,512]{2,1,0:T(8,128)(2,1)S(1)} %bitcast.81), channel_id=1, replica_groups=mesh['dp'=8,'tensor'=4] {'dp'}, dimensions={0} | all-to-all | bytes 4194304 | tf_op jit(solution)/shard_map/all_to_all | solution.py:1346
  690.8 3.8 fusion.41
  694.6 5.5 reduce-scatter.5.cloned.1.call-done
  703.2 2.0 copy.73
  705.7 2.9 multiply_reduce_fusion.1
  717.4 20.4 %sum_all.1 = f32[192,128]{1,0:T(8,128)} custom-call(f32[192,128]{1,0:T(8,128)} %bitcast.84), custom_call_target="tpu_custom_call" | custom-call | tf_op jit(solution)/shard_map/sum_all/pallas_call | solution.py:1283
  741.9 2.6 multiply_subtract_fusion.3
  744.5 2.1 copy.78
  746.6 2.0 copy.79
  748.7 2.0 copy.80
  751.5 2.8 multiply_subtract_fusion.2
  755.1 6.4 multiply_subtract_fusion.1
  761.5 3.7 multiply_subtract_fusion
  765.2 21.3 %all-gather.2.cloned.1.call-done = bf16[1024,2048]{1,0:T(8,128)(2,1)} async-done(((bf16[1024,512]{1,0:T(8,128)(2,1)}), bf16[1024,2048]{1,0:T(8,128)(2,1)}) %all-gather.2.cloned.1.call-update) | async-done | bytes 4194320 | tf_op jit(solution)/shard_map/all_gather | solution.py:1483
  786.5 4.9 copy.89
  791.5 2.0 copy.90
  (199 shorter events, 38.3 us)
Async XLA Ops:
  18.0 5.4 copy-start.45
  18.0 5.7 copy-start.59
  18.0 6.6 slice-start
  18.0 50.5 %copy-start.37 = (f32[22656]{0:T(1024)S(1)}, f32[22656]{0:T(1024)}, u32[]{:S(2)}) copy-start(f32[22656]{0:T(1024)} %param.41) | copy-start | bytes 271876
  18.0 54.5 %all-to-all-start = ((bf16[8,256,1024]{2,1,0:T(8,128)(2,1)}), bf16[8,256,1024]{2,1,0:T(8,128)(2,1)}, u32[]{:S(2)}, u32[]{:S(2)}) async-start(bf16[8,256,1024]{2,1,0:T(8,128)(2,1)} %bitcast.78), calls=%async_computation | async-start | bytes 8388608 | tf_op jit(solution)/shard_map/all_to_all | solution.py:1346
  23.4 448.3 %reduce-scatter.3.cloned.1.call-start = ((), (), s32[]{:S(2)}) async-start(), calls=%async_computation.5 | async-start | bytes 5242880 | tf_op jit(solution)/shard_map/reduce_scatter | solution.py:1432
  69.2 73.9 %copy-start.41 = (f32[2048]{0:T(1024)}, f32[2048]{0:T(1024)S(1)}, u32[]{:S(2)}) copy-start(f32[2048]{0:T(1024)S(1)} %get-tuple-element.215) | copy-start | bytes 24580
  139.8 3.8 copy-start.32
  193.1 14.4 %copy-start.4 = (bf16[768,128]{1,0:T(8,128)(2,1)}, bf16[768,128]{1,0:T(8,128)(2,1)S(1)}, u32[]{:S(2)}) copy-start(bf16[768,128]{1,0:T(8,128)(2,1)S(1)} %get-tuple-element.206.v) | copy-start | bytes 589828
  193.1 14.4 %copy-start.6 = (bf16[768,128]{1,0:T(8,128)(2,1)}, bf16[768,128]{1,0:T(8,128)(2,1)S(1)}, u32[]{:S(2)}) copy-start(bf16[768,128]{1,0:T(8,128)(2,1)S(1)} %get-tuple-element.207.k) | copy-start | bytes 589828
  207.5 6.3 copy-start.8
  213.8 107.1 %copy-start.10 = (f32[256,2048]{1,0:T(8,128)}, f32[256,2048]{1,0:T(8,128)S(1)}, u32[]{:S(2)}) copy-start(f32[256,2048]{1,0:T(8,128)S(1)} %get-tuple-element.219) | copy-start | bytes 6291460
  292.7 14.6 %copy-start.56 = (bf16[2048,2048]{1,0:T(8,128)(2,1)S(1)}, bf16[2048,2048]{1,0:T(8,128)(2,1)}, u32[]{:S(2)}) copy-start(bf16[2048,2048]{1,0:T(8,128)(2,1)} %get-tuple-element.83) | copy-start | bytes 25165828
  323.4 47.6 %slice-start.1 = ((s8[8388608]{0:T(1024)(128)(4,1)}), s8[4194304]{0:T(1024)(128)(4,1)S(1)}, s32[]{:S(2)}) async-start(s8[8388608]{0:T(1024)(128)(4,1)} %bitcast.94), calls=%async_computation.9 | async-start | bytes 8388608
  344.6 12.7 %copy-start.57 = (bf16[1024,2048]{1,0:T(8,128)(2,1)S(1)}, bf16[1024,2048]{1,0:T(8,128)(2,1)}, u32[]{:S(2)}) copy-start(bf16[1024,2048]{1,0:T(8,128)(2,1)} %get-tuple-element.81) | copy-start | bytes 12582916
  344.6 26.5 %slice-start.2 = ((s8[8388608]{0:T(1024)(128)(4,1)}), s8[4194304]{0:T(1024)(128)(4,1)S(1)}, s32[]{:S(2)}) async-start(s8[8388608]{0:T(1024)(128)(4,1)} %bitcast.94), calls=%async_computation.10 | async-start | bytes 8388608
  357.3 13.8 %copy-start.19 = (bf16[1024,2048]{1,0:T(8,128)(2,1)S(1)}, bf16[1024,2048]{1,0:T(8,128)(2,1)}, u32[]{:S(2)}) copy-start(bf16[1024,2048]{1,0:T(8,128)(2,1)} %get-tuple-element.85) | copy-start | bytes 12582916
  383.0 86.3 %copy-start.11 = (f32[256,2048]{1,0:T(8,128)S(1)}, f32[256,2048]{1,0:T(8,128)}, u32[]{:S(2)}) copy-start(f32[256,2048]{1,0:T(8,128)} %copy-done.10) | copy-start | bytes 6291460
  476.4 35.4 %all-to-all-start.1 = ((bf16[8,256,512]{2,1,0:T(8,128)(2,1)}), bf16[8,256,512]{2,1,0:T(8,128)(2,1)}, u32[]{:S(2)}, u32[]{:S(2)}) async-start(bf16[8,256,512]{2,1,0:T(8,128)(2,1)} %bitcast.80), calls=%async_computation.2 | async-start | bytes 4194304 | tf_op jit(solution)/shard_map/all_to_all | solution.py:1346
  480.8 219.3 %reduce-scatter.5.cloned.1.call-start = ((), (), s32[]{:S(2)}) async-start(), calls=%async_computation.6 | async-start | bytes 2621440 | tf_op jit(solution)/shard_map/reduce_scatter | solution.py:1478
  486.2 6.2 copy-start.23
  486.2 6.2 copy-start.3
  486.2 6.2 copy-start.5
  486.2 6.2 copy-start.7
  492.4 19.5 %copy-start.55 = (s32[1,2,8,128]{3,1,2,0:T(2,128)S(1)}, s32[1,2,8,128]{3,1,2,0:T(2,128)}, u32[]{:S(2)}) copy-start(s32[1,2,8,128]{3,1,2,0:T(2,128)} %copy-done.54) | copy-start | bytes 24580
  517.2 97.7 %copy-start.18 = (bf16[256,2048]{1,0:T(8,128)(2,1)S(1)}, bf16[256,2048]{1,0:T(8,128)(2,1)}, u32[]{:S(2)}) copy-start(bf16[256,2048]{1,0:T(8,128)(2,1)} %copy-done.17) | copy-start | bytes 3145732
  623.7 31.1 %copy-start.26 = (bf16[4,512,512]{2,1,0:T(8,128)(2,1)S(1)}, bf16[4,512,512]{2,1,0:T(8,128)(2,1)}, u32[]{:S(2)}) copy-start(bf16[4,512,512]{2,1,0:T(8,128)(2,1)} %get-tuple-element.97) | copy-start | bytes 6291460
  657.3 129.2 %all-gather.2.cloned.1.call-start = ((), (), s32[]{:S(2)}) async-start(), calls=%async_computation.7 | async-start | bytes 5242880 | tf_op jit(solution)/shard_map/all_gather | solution.py:1483
  690.8 9.3 %copy-start.27 = (f32[256,512]{1,0:T(8,128)S(1)}, f32[256,512]{1,0:T(8,128)}, u32[]{:S(2)}) copy-start(f32[256,512]{1,0:T(8,128)} %a.1) | copy-start | bytes 1572868
  694.6 6.5 copy-start.35
  694.6 7.5 copy-start.36
  705.7 4.0 copy-start.40
  705.7 4.7 copy-start.16
  710.4 31.5 %copy-start.29 = (f32[256,512]{0,1:T(8,128)S(1)}, f32[256,512]{0,1:T(8,128)}, u32[]{:S(2)}) copy-start(f32[256,512]{0,1:T(8,128)} %copy.77) | copy-start | bytes 1572868
  744.5 6.2 copy-start.39
  744.5 6.2 copy-start.46
  744.5 6.2 copy-start.47
  744.5 7.0 copy-start.28
  750.7 3.5 copy-start.34
  750.7 3.5 copy-start.38
  750.7 3.5 copy-start.43
  750.7 3.5 copy-start.44
  750.8 4.3 copy-start.22
  751.5 3.6 copy-start.20
  755.0 6.5 copy-start.21
  755.0 6.5 copy-start.30
  755.0 6.5 copy-start.31
  786.5 4.9 copy-start.24
  (21 other events, 42.3 us)
Sparse Core Ops, SparseCore 0:
  323.6 84.7 reduce-scatter.2
  657.4 42.6 reduce-scatter.4
  702.3 84.1 all-gather.1

commit v6 on v5

--- a/solution.py
+++ b/solution.py
@@ -669,6 +669,101 @@
 
     def finish(self):
         self.job.finish()
+
+
+class Begun:
+    def __init__(self, job, when):
+        self.job, self.when = job, when
+        self.prepare, self.prepared, self.finish = job.prepare, job.prepared, job.finish
+
+    def start(self):
+        pass
+
+    def steps(self):
+        yield self.when, self.job.start
+        for when, step in self.job.steps():
+            yield self.when + when, step
+
+
+class Ended:
+    def __init__(self, job, when):
+        self.job, self.when = job, when
+        self.prepare, self.prepared, self.start = job.prepare, job.prepared, job.start
+
+    def steps(self):
+        yield from self.job.steps()
+        yield self.when, self.job.finish
+
+    def finish(self):
+        pass
+
+
+class GatheredProduct:
+    @staticmethod
+    def scratch(n, block, weight):
+        held = pltpu.VMEM((n - 1, 2, *block.shape), block.dtype)
+        return [pltpu.VMEM(weight.shape, weight.dtype), DMA, held, DMA((n - 1, 2))]
+
+    def __init__(self, line, own, gathered, weight, bias, out, scratch, begin, cost):
+        self.line, self.own, self.gathered, self.bias, self.out = line, own, gathered, bias, out
+        self.weight, self.held, self.sems = scratch[0], scratch[2], scratch[3]
+        self.copy = pltpu.make_async_copy(weight, scratch[0], scratch[1])
+        self.begin, self.cost, self.tile = begin, cost, 512
+
+    def prepare(self):
+        pass
+
+    def prepared(self):
+        pass
+
+    def start(self):
+        pass
+
+    def place(self, h, right):
+        rows, t = self.own.shape[0], self.line.at.t
+        return pl.ds(pl.multiple_of((t - 1 - h if right else t + 1 + h) * rows, rows), rows)
+
+    def load(self, h, right):
+        side = 0 if right else 1
+        return pltpu.make_async_copy(
+            self.gathered.at[self.place(h, right)], self.held.at[h, side], self.sems.at[h, side]
+        )
+
+    def multiply(self, block, rows):
+        for j in range(self.out.shape[1] // self.tile):
+            span = pl.ds(j * self.tile, self.tile)
+            total = product(block[...], self.weight[:, span], 1, 0) + self.bias[:, span]
+            self.out[rows, span] = total
+
+    def arrived(self, h, right):
+        pl.when(self.line.gets(h, right))(lambda: self.load(h, right).start())
+
+    def work(self, h, right):
+        @pl.when(self.line.gets(h, right))
+        def _():
+            self.load(h, right).wait()
+            self.multiply(self.held.at[h, 0 if right else 1], self.place(h, right))
+
+    def mine(self):
+        rows = self.own.shape[0]
+        self.multiply(self.own, pl.ds(pl.multiple_of(self.line.at.t * rows, rows), rows))
+
+    def steps(self):
+        yield self.begin - 4.0, self.copy.start
+        yield self.begin, self.copy.wait
+        yield self.begin, self.mine
+        when = self.begin + self.cost
+        for h in range(self.line.at.n - 1):
+            come = self.line.unit * (h + 1) + 0.5
+            for right in (True, False):
+                yield come, functools.partial(self.arrived, h, right)
+            when = max(when, come + 1.0)
+            for right in (True, False):
+                yield when, functools.partial(self.work, h, right)
+                when += self.cost
+
+    def finish(self):
+        pass
 
 
 class RowProduct:
@@ -952,7 +1047,7 @@
     )
 
 
-def rows_and_expanded(n_dp, n, x, expand, shrink):
+def rows_and_expanded(n_dp, n, x, expand, shrink, bias):
     low = jnp.bfloat16
     shapes = [
         jax.ShapeDtypeStruct(expand.shape, low),
@@ -961,28 +1056,44 @@
     chips, chunks, halves = n_dp // 2, 4, 2
     line, ring = LineGather.sems(n, chunks), RingGather.sems(chips, halves)
 
-    def kernel(x_ref, a, b, x_out, a_out, b_out, a_low, b_low, *refs):
+    full = like(shapes[0], n_dp, 1)
+    made = GatheredProduct.scratch(n, x, full)
+
+    def kernel(x_ref, a, b, c, u, x_out, a_out, b_out, a_low, b_low, *refs):
         parts = Parts(refs)
         at = Place(n_dp, n)
         met = at.greet(line=True, ring=True)
         a_low[...] = a[...].astype(low)
         b_low[...] = b[...].T.astype(low)
+        line_job = line_gather(at, x_ref, x_out, 0, chunks, parts.take(line), 22.0)
         run_jobs(
             met,
             [
-                line_gather(at, x_ref, x_out, 0, chunks, parts.take(line), 22.0),
-                ring_gather(at, a_low, a_out, 0, halves, parts.take(ring), 44.0),
-                ring_gather(at, b_low, b_out, 0, halves, parts.take(ring), 44.0),
+                line_job,
+                Ended(
+                    ring_gather(at, a_low, a_out, 0, halves, parts.take(ring), 22.0), 35.0
+                ),
+                Begun(
+                    ring_gather(at, b_low, b_out, 0, halves, parts.take(ring), 30.0), 22.5
+                ),
+                GatheredProduct(
+                    line_job, x_ref, x_out, a_out, c, u, parts.take(made), 39.5, 6.0
+                ),
             ],
         )
 
     return move(
         kernel,
-        (x, expand, shrink),
-        3,
-        (like(x, n, 1), like(shapes[0], n_dp, 1), like(shapes[1], n_dp, 1)),
-        0,
-        [pltpu.VMEM(x.shape, low) for x in shapes] + line + ring * 2,
+        (x, expand, shrink, bias),
+        4,
+        (
+            jax.ShapeDtypeStruct((n * x.shape[0], full.shape[1]), jnp.float32),
+            like(x, n, 1),
+            full,
+            like(shapes[1], n_dp, 1),
+        ),
+        1,
+        [pltpu.VMEM(x.shape, low) for x in shapes] + line + ring * 2 + made,
         4,
         "rows_and_expanded",
     )
@@ -1417,10 +1528,9 @@
     hidden_one = inputs_float + (mul_right_t(heads_out, project_all_t) + project_bias)
     normed_two, norm_two_back = jax.vjp(layer_norm, hidden_one, gain_two, shift_two)
 
-    normed_two_low, expand_cols, shrink_rows_t = rows_and_expanded(
-        n_dp, n, low(normed_two), expand_weight, shrink_weight
-    )
-    expand_pre = mul_plain(normed_two_low, expand_cols) + expand_bias
+    expand_pre, normed_two_low, expand_cols, shrink_rows_t = rows_and_expanded(
+        n_dp, n, low(normed_two), expand_weight, shrink_weight, expand_bias[None]
+    )
     activated, gelu_back = jax.vjp(gelu_tanh, expand_pre)
     activated_low = activated.astype(jnp.bfloat16)
     result_part = low(mul_right_t(activated_low, shrink_rows_t))

time: 809 us -> 800 us (0.989)
  matrix products: 134 us -> 122 us
    dot_general x7 -> x6, matrix products: 54.5 us -> 39.1 us  [mul_plain(): return jnp.dot(left, right, preferred_element_type=jnp.float32)]
    unnamed x136 -> x120, local copies, waits for them, and re-layouts: 23.3 us -> 21.1 us
where the time goes in v6:
time: 800 us; the launch traced here: 793 us
  Pallas kernels  497 us (62%)
  matrix products  122 us (15%)
  other arithmetic  49.9 us (6%)
  local copies, waits for them, and re-layouts  32.8 us (4%)
  waiting for transfers between devices  30.1 us (4%)
  blocking collectives  29.8 us (4%)
  between operations  20.7 us (3%)
  starting transfers between devices  9.79 us (1%)
    pallas_call x7, Pallas kernels, move(): pl.pallas_call(kernel, out_shape=tuple(outs), in_specs=[IN_VMEM if i < in...  446 us
    dot_general x6, matrix products, mul_left_t(): lax.dot_general(left, right, (((0,), (0,)), ((), ())), preferred_element_...  45.2 us
    dot_general x6, matrix products, mul_plain(): return jnp.dot(left, right, preferred_element_type=jnp.float32)  39.1 us
    dot_general x4, matrix products, mul_right_t(): lax.dot_general(left, right, (((1,), (1,)), ((), ())), preferred_element_...  37.8 us
    all_to_all x1, blocking collectives, exchange(): return lax.all_to_all(packed, 'dp', split_axis=0, concat_axis=0, tiled=True)  29.8 us
    all_gather x1, waiting for transfers between devices, local(): grad_rows = lax.all_gather(back, 'tensor', axis=1, tiled=True)  21.2 us
    unnamed x120, local copies, waits for them, and re-layouts  21.1 us
    pallas_call x1, Pallas kernels, sum_all(): pl.pallas_call(functools.partial(sum_all_kernel, n_dp, n), out_shape=jax....  20.5 us
  transfers between devices with their start and end apart: 5, of which 3 were waited for; matrix products, arithmetic and copies ran while one was open for 15% of the time, Pallas kernels for 21%

profile of v6, /device:TPU:0, one launch (start us, length us, event | category | flops | bytes accessed | tf_op | source)
XLA Modules:
  0.0 792.6 jit_solution(2984572573484366202)
XLA Ops:
  10.2 1.7 constant_dynamic-slice_fusion.1
  11.9 6.1 fusion.19
  18.0 5.3 all-to-all-start
  24.6 43.9 %gather_lines.1 = (bf16[256,2048]{1,0:T(8,128)(2,1)}, bf16[256,2048]{1,0:T(8,128)(2,1)}, bf16[256,256]{1,0:T(8,128)(2,1)}) custom-call(f32[256,512]{1,0:T(8,128)} %a.1, f32[512,256]{1,0:T(8,128)} %b.1, f32[64,256]{1,0:T(8,128)} %c), custom_call_target="tpu_custom_call" | custom-call | tf_op jit(solution)/shard_map/gather_lines/pallas_call | solution.py:834
  69.3 3.3 all-to-all-done
  72.6 8.1 %fusion.39.x.y = bf16[1024,1024]{1,0:T(8,128)(2,1)} fusion(bf16[2048,1024]{1,0:T(8,128)(2,1)} %bitcast.3, s32[2048]{0:T(1024)S(1)} %bitcast.89), kind=kOutput, calls=%fused_computation.78 | convolution fusion | flops 4298113024 | bytes 6299648 | tf_op jit(solution)/shard_map/dot_general | solution.py:44
  80.6 59.1 %rows_and_weights.1 = (bf16[256,2048]{1,0:T(8,128)(2,1)}, bf16[1024,2048]{1,0:T(8,128)(2,1)}, bf16[2048,2048]{1,0:T(8,128)(2,1)}, bf16[2048,256]{1,0:T(8,128)(2,1)}) custom-call(bf16[1024,1024]{1,0:T(8,128)(2,1)} %fusion.39.x.y, bf16[256,2048]{1,0:T(8,128)(2,1)} %get-tuple-element.71.a, bf16[256,256]{1,0:T(8,128)(2,1)} %get-tuple-element.72.b), custom_call_target="tpu_custom_call" | custom-call | tf_op jit(solution)/shard_map/rows_and_weights/pallas_call | solution.py:834
  144.7 47.2 %shared_and_project.1 = (bf16[256,2048]{1,0:T(8,128)(2,1)}, bf16[1024,256]{1,0:T(8,128)(2,1)}, bf16[2048,2048]{1,0:T(8,128)(2,1)}, bf16[1024,2048]{1,0:T(8,128)(2,1)}) custom-call(bf16[1024,1024]{1,0:T(8,128)(2,1)} %fusion.39.x.y, bf16[256,256]{1,0:T(8,128)(2,1)} %fusion.43.x, ...), custom_call_target="tpu_custom_call", output_to_operand_aliasing={{3}: (6, {})} | custom-call | tf_op jit(solution)/shard_map/shared_and_project/pallas_call | solution.py:834
  194.3 13.1 %attend.1 = (bf16[256,2048]{1,0:T(8,128)(2,1)S(1)}, f32[256,2048]{1,0:T(8,128)S(1)}) custom-call(bf16[256,2048]{1,0:T(8,128)(2,1)S(1)} %copy-done.2, bf16[768,128]{1,0:T(8,128)(2,1)S(1)} %get-tuple-element.209.k, bf16[768,128]{1,0:T(8,128)(2,1)S(1)} %get-tuple-element.208.v, s32[256,1]{1,0:T(8,128)S(1)} %copy.68.seg_row, ...), custom_call_target="tpu_custom_call" | custom-call | tf_op jit(solution)/shard_map/attend/pallas_call | solution.py:1277
  207.4 6.3 fusion.76
  215.5 83.9 %rows_and_expanded.1 = (f32[1024,2048]{1,0:T(8,128)}, bf16[1024,2048]{1,0:T(8,128)(2,1)}, bf16[2048,2048]{1,0:T(8,128)(2,1)}, bf16[2048,2048]{1,0:T(8,128)(2,1)}) custom-call(bf16[256,2048]{1,0:T(8,128)(2,1)} %add_convert_fusion.2.x_ref, f32[256,2048]{1,0:T(8,128)} %a.2, f32[2048,256]{1,0:T(8,128)} %b.2, f32[1,2048]{1,0:T(1,128)} %bitcast.84), custom_call_target="tpu_custom_call" | custom-call | tf_op jit(solution)/shard_map/rows_and_expanded/pallas_call | solution.py:834
  299.4 16.3 %convolution_convert_fusion.3 = bf16[1024,2048]{1,0:T(8,128)(2,1)} fusion(bf16[2048,2048]{1,0:T(8,128)(2,1)} %get-tuple-element.83, f32[1024,2048]{1,0:T(8,128)} %get-tuple-element.82), kind=kOutput, calls=%fused_computation.29 | convolution fusion | flops 8610906112 | bytes 20971520 | tf_op jit(solution)/shard_map/dot_general | solution.py:38
  315.6 2.5 fusion.44
  318.2 18.3 %convert_reduce_fusion = (f32[2048]{0:T(1024)S(1)}, bf16[1024,2048]{1,0:T(8,128)(2,1)S(1)}) fusion(f32[1024,2048]{1,0:T(8,128)} %get-tuple-element.82, bf16[1024,2048]{1,0:T(8,128)(2,1)} %get-tuple-element.85, bf16[2048,2048]{1,0:T(8,128)(2,1)} %get-tuple-element.83), kind=kOutput, calls=%fused_computation.10 | convolution fusion | flops 8636069888 | bytes 25174016 | tf_op jit(solution)/shard_map/dot_general | solution.py:34
  336.5 12.9 %convolution_convert_fusion.2.x_ref = bf16[1024,2048]{1,0:T(8,128)(2,1)} fusion(bf16[1024,2048]{1,0:T(8,128)(2,1)S(1)} %get-tuple-element.201, bf16[2048,2048]{1,0:T(8,128)(2,1)} %get-tuple-element.86), kind=kOutput, calls=%fused_computation.28 | convolution fusion | flops 8592031744 | bytes 16777216 | tf_op jit(solution)/shard_map/dot_general | solution.py:38
  349.4 11.4 %convolution_convert_fusion.1.a = bf16[2048,2048]{1,0:T(8,128)(2,1)} fusion(bf16[1024,2048]{1,0:T(8,128)(2,1)S(1)} %copy-done.52, bf16[1024,2048]{1,0:T(8,128)(2,1)S(1)} %get-tuple-element.201), kind=kOutput, calls=%fused_computation.21 | convolution fusion | flops 8594128896 | bytes 16777216 | tf_op jit(solution)/shard_map/dot_general | solution.py:44
  360.8 15.1 %convolution_convert_fusion.b = bf16[2048,2048]{1,0:T(8,128)(2,1)} fusion(bf16[1024,2048]{1,0:T(8,128)(2,1)S(1)} %copy-done.15, f32[1024,2048]{1,0:T(8,128)} %get-tuple-element.82), kind=kOutput, calls=%fused_computation.20 | convolution fusion | flops 8613003264 | bytes 20971520 | tf_op jit(solution)/shard_map/dot_general | solution.py:44
  376.0 87.5 %scatter_expanded.1 = (f32[256,2048]{1,0:T(8,128)}, f32[256,2048]{1,0:T(8,128)}, f32[256,2048]{1,0:T(8,128)}) custom-call(bf16[1024,2048]{1,0:T(8,128)(2,1)} %convolution_convert_fusion.2.x_ref, bf16[2048,2048]{1,0:T(8,128)(2,1)} %convolution_convert_fusion.1.a, bf16[2048,2048]{1,0:T(8,128)(2,1)} %convolution_convert_fusion.b), custom_call_target="tpu_custom_call" | custom-call | tf_op jit(solution)/shard_map/scatter_expanded/pallas_call | solution.py:834
  463.5 2.3 multiply_reduce_fusion.2
  465.8 4.8 fusion.24
  470.6 4.4 all-to-all-start.1
  475.1 2.8 fusion.72
  477.9 2.4 convert_reduce_fusion.3
  480.4 6.1 convolution_convert_fusion.5.do
  486.5 17.5 %attend_back.1 = (bf16[256,2048]{1,0:T(8,128)(2,1)S(1)}, bf16[1024,256]{1,0:T(8,128)(2,1)S(1)}) custom-call(bf16[256,2048]{1,0:T(8,128)(2,1)S(1)} %copy-done.3, bf16[256,2048]{1,0:T(8,128)(2,1)S(1)} %convolution_convert_fusion.5.do, f32[256,2048]{1,0:T(8,128)S(1)} %get-tuple-element.89.log_total, bf16[768,128]{1,0:T(8,128)(2,1)S(1)} %get-tuple-element.209.k, ...), custom_call_target="tpu_custom_call" | custom-call | tf_op jit(solution)/shard_map/attend_back/pallas_call | solution.py:1296
  505.8 5.4 fusion.40.y
  511.2 93.5 %scatter_shared.1 = (f32[256,256]{1,0:T(8,128)}, bf16[4,512,512]{2,1,0:T(8,128)(2,1)}, f32[256,2048]{1,0:T(8,128)}, bf16[1024,2048]{1,0:T(8,128)(2,1)}) custom-call(bf16[1024,256]{1,0:T(8,128)(2,1)} %copy-done.5, bf16[1024,512]{1,0:T(8,128)(2,1)} %fusion.40.y, bf16[256,2048]{1,0:T(8,128)(2,1)} %copy-done.13, bf16[256,2048]{1,0:T(8,128)(2,1)} %copy-done, ...), custom_call_target="tpu_custom_call" | custom-call | tf_op jit(solution)/shard_map/scatter_shared/pallas_call | solution.py:834
  607.4 2.4 fusion.61
  611.4 3.3 convert_reduce_fusion.2
  614.7 31.2 %cols_and_shared.1 = (f32[64,256]{1,0:T(8,128)}, bf16[1024,512]{1,0:T(8,128)(2,1)}) custom-call(bf16[256,2048]{1,0:T(8,128)(2,1)} %get-tuple-element.207.x, bf16[2048,256]{1,0:T(8,128)(2,1)} %convolution_convert_fusion.4.c), custom_call_target="tpu_custom_call" | custom-call | tf_op jit(solution)/shard_map/cols_and_shared/pallas_call | solution.py:834
  645.9 2.4 copy.81
  649.5 2.6 fusion.25
  652.2 29.8 %all_to_all.15 = bf16[8,256,512]{2,1,0:T(8,128)(2,1)S(1)} all-to-all(bf16[8,256,512]{2,1,0:T(8,128)(2,1)S(1)} %bitcast.80), channel_id=1, replica_groups=mesh['dp'=8,'tensor'=4] {'dp'}, dimensions={0} | all-to-all | bytes 4194304 | tf_op jit(solution)/shard_map/all_to_all | solution.py:1457
  681.9 3.8 fusion.41
  685.7 5.5 reduce-scatter.5.cloned.1.call-done
  694.2 2.0 copy.73
  696.8 2.9 multiply_reduce_fusion.1
  708.4 20.5 %sum_all.1 = f32[192,128]{1,0:T(8,128)} custom-call(f32[192,128]{1,0:T(8,128)} %bitcast.83), custom_call_target="tpu_custom_call" | custom-call | tf_op jit(solution)/shard_map/sum_all/pallas_call | solution.py:1394
  733.0 2.6 multiply_subtract_fusion.3
  735.6 2.1 copy.78
  737.7 2.0 copy.79
  739.8 2.0 copy.80
  742.6 2.8 multiply_subtract_fusion.2
  746.1 6.4 multiply_subtract_fusion.1
  752.6 3.7 multiply_subtract_fusion
  756.3 21.2 %all-gather.2.cloned.1.call-done = bf16[1024,2048]{1,0:T(8,128)(2,1)} async-done(((bf16[1024,512]{1,0:T(8,128)(2,1)}), bf16[1024,2048]{1,0:T(8,128)(2,1)}) %all-gather.2.cloned.1.call-update) | async-done | bytes 4194320 | tf_op jit(solution)/shard_map/all_gather | solution.py:1593
  777.5 4.9 copy.89
  782.5 2.0 copy.90
  (181 shorter events, 34.5 us)
Async XLA Ops:
  18.0 5.4 copy-start.41
  18.0 5.7 copy-start.54
  18.0 6.6 slice-start
  18.0 50.5 %copy-start.33 = (f32[22656]{0:T(1024)S(1)}, f32[22656]{0:T(1024)}, u32[]{:S(2)}) copy-start(f32[22656]{0:T(1024)} %param.41) | copy-start | bytes 271876
  18.0 54.5 %all-to-all-start = ((bf16[8,256,1024]{2,1,0:T(8,128)(2,1)}), bf16[8,256,1024]{2,1,0:T(8,128)(2,1)}, u32[]{:S(2)}, u32[]{:S(2)}) async-start(bf16[8,256,1024]{2,1,0:T(8,128)(2,1)} %bitcast.77), calls=%async_computation | async-start | bytes 8388608 | tf_op jit(solution)/shard_map/all_to_all | solution.py:1457
  23.4 442.5 %reduce-scatter.3.cloned.1.call-start = ((), (), s32[]{:S(2)}) async-start(), calls=%async_computation.5 | async-start | bytes 5242880 | tf_op jit(solution)/shard_map/reduce_scatter | solution.py:1542
  69.3 73.8 %copy-start.37 = (f32[2048]{0:T(1024)}, f32[2048]{0:T(1024)S(1)}, u32[]{:S(2)}) copy-start(f32[2048]{0:T(1024)S(1)} %get-tuple-element.217) | copy-start | bytes 24580
  139.8 3.3 copy-start.8
  139.8 3.8 copy-start.28
  141.4 3.3 copy-start.44
  207.4 6.3 copy-start.4
  213.7 102.0 %copy-start.6 = (f32[256,2048]{1,0:T(8,128)}, f32[256,2048]{1,0:T(8,128)S(1)}, u32[]{:S(2)}) copy-start(f32[256,2048]{1,0:T(8,128)S(1)} %get-tuple-element.221) | copy-start | bytes 6291460
  336.5 12.9 %copy-start.52 = (bf16[1024,2048]{1,0:T(8,128)(2,1)S(1)}, bf16[1024,2048]{1,0:T(8,128)(2,1)}, u32[]{:S(2)}) copy-start(bf16[1024,2048]{1,0:T(8,128)(2,1)} %get-tuple-element.87) | copy-start | bytes 12582916
  349.4 11.4 %copy-start.15 = (bf16[1024,2048]{1,0:T(8,128)(2,1)S(1)}, bf16[1024,2048]{1,0:T(8,128)(2,1)}, u32[]{:S(2)}) copy-start(bf16[1024,2048]{1,0:T(8,128)(2,1)} %get-tuple-element.85) | copy-start | bytes 12582916
  376.0 87.5 %copy-start.7 = (f32[256,2048]{1,0:T(8,128)S(1)}, f32[256,2048]{1,0:T(8,128)}, u32[]{:S(2)}) copy-start(f32[256,2048]{1,0:T(8,128)} %copy-done.6) | copy-start | bytes 6291460
  470.6 35.2 %all-to-all-start.1 = ((bf16[8,256,512]{2,1,0:T(8,128)(2,1)}), bf16[8,256,512]{2,1,0:T(8,128)(2,1)}, u32[]{:S(2)}, u32[]{:S(2)}) async-start(bf16[8,256,512]{2,1,0:T(8,128)(2,1)} %bitcast.79), calls=%async_computation.2 | async-start | bytes 4194304 | tf_op jit(solution)/shard_map/all_to_all | solution.py:1457
  475.0 216.2 %reduce-scatter.5.cloned.1.call-start = ((), (), s32[]{:S(2)}) async-start(), calls=%async_computation.6 | async-start | bytes 2621440 | tf_op jit(solution)/shard_map/reduce_scatter | solution.py:1588
  480.3 6.2 copy-start.19
  480.4 6.2 copy-start.3
  486.5 19.3 %copy-start.51 = (s32[1,2,8,128]{3,1,2,0:T(2,128)S(1)}, s32[1,2,8,128]{3,1,2,0:T(2,128)}, u32[]{:S(2)}) copy-start(s32[1,2,8,128]{3,1,2,0:T(2,128)} %copy-done.50) | copy-start | bytes 24580
  511.2 94.7 %copy-start.14 = (bf16[256,2048]{1,0:T(8,128)(2,1)S(1)}, bf16[256,2048]{1,0:T(8,128)(2,1)}, u32[]{:S(2)}) copy-start(bf16[256,2048]{1,0:T(8,128)(2,1)} %copy-done.13) | copy-start | bytes 3145732
  604.8 2.6 copy-start.9
  604.8 2.6 copy-start.29
  604.8 2.6 copy-start.38
  604.8 2.6 copy-start.45
  607.4 2.4 copy-start.47
  614.7 31.2 %copy-start.22 = (bf16[4,512,512]{2,1,0:T(8,128)(2,1)S(1)}, bf16[4,512,512]{2,1,0:T(8,128)(2,1)}, u32[]{:S(2)}) copy-start(bf16[4,512,512]{2,1,0:T(8,128)(2,1)} %get-tuple-element.99) | copy-start | bytes 6291460
  648.3 129.2 %all-gather.2.cloned.1.call-start = ((), (), s32[]{:S(2)}) async-start(), calls=%async_computation.7 | async-start | bytes 5242880 | tf_op jit(solution)/shard_map/all_gather | solution.py:1593
  681.9 9.3 %copy-start.23 = (f32[256,512]{1,0:T(8,128)S(1)}, f32[256,512]{1,0:T(8,128)}, u32[]{:S(2)}) copy-start(f32[256,512]{1,0:T(8,128)} %a.1) | copy-start | bytes 1572868
  685.7 6.5 copy-start.31
  685.7 7.5 copy-start.32
  696.7 4.0 copy-start.36
  696.7 4.7 copy-start.12
  701.5 31.5 %copy-start.25 = (f32[256,512]{0,1:T(8,128)S(1)}, f32[256,512]{0,1:T(8,128)}, u32[]{:S(2)}) copy-start(f32[256,512]{0,1:T(8,128)} %copy.77) | copy-start | bytes 1572868
  735.6 6.2 copy-start.35
  735.6 6.2 copy-start.42
  735.6 6.2 copy-start.43
  735.6 7.0 copy-start.24
  741.8 3.5 copy-start.30
  741.8 3.5 copy-start.34
  741.8 3.5 copy-start.39
  741.8 3.5 copy-start.40
  741.8 4.3 copy-start.18
  742.6 3.6 copy-start.16
  746.1 6.5 copy-start.17
  746.1 6.5 copy-start.26
  746.1 6.5 copy-start.27
  777.5 4.9 copy-start.20
  (13 other events, 20.6 us)
Sparse Core Ops, SparseCore 0:
  318.3 85.2 reduce-scatter.2
  648.5 42.6 reduce-scatter.4
  693.3 84.1 all-gather.1

commit v7 on v6

--- a/solution.py
+++ b/solution.py
@@ -1533,13 +1533,16 @@
     )
     activated, gelu_back = jax.vjp(gelu_tanh, expand_pre)
     activated_low = activated.astype(jnp.bfloat16)
-    result_part = low(mul_right_t(activated_low, shrink_rows_t))
-    own_result = lax.dynamic_slice_in_dim(result_part, t * part_rows, part_rows, 0)
-    result_part = lax.dynamic_update_slice_in_dim(
-        result_part, low(own_result + (hidden_one + shrink_bias)), t * part_rows, 0
-    )
+    pieces = []
+    for k in range(n):
+        span = slice(k * part_cols, (k + 1) * part_cols)
+        piece = low(mul_right_t(activated_low, shrink_rows_t[span]))
+        own_piece = lax.dynamic_slice_in_dim(piece, t * part_rows, part_rows, 0)
+        own_piece = low(own_piece + (hidden_one[:, span] + shrink_bias[span]))
+        pieces.append(lax.dynamic_update_slice_in_dim(piece, own_piece, t * part_rows, 0))
+    result_part = jnp.concatenate(pieces)
     result_part, owned_grad = lax.optimization_barrier((result_part, owned_grad))
-    layer_cols = lax.psum_scatter(result_part, "tensor", scatter_dimension=1, tiled=True)
+    layer_cols = lax.psum_scatter(result_part, "tensor", scatter_dimension=0, tiled=True)
     shrink_grad_t = low(mul_left_t(owned_grad, activated_low))
     activated_grad = mul_plain(owned_grad, shrink_rows_t)
     expand_pre_grad = gelu_back(activated_grad)[0].astype(jnp.bfloat16)

time: 800 us -> 802 us (level)
  matrix products: 122 us -> 112 us
    dot_general x4 -> x7, matrix products: 37.8 us -> 30.8 us  [mul_right_t(): lax.dot_general(left, right, (((1,), (1,)), ((), ())), preferred_element_...]
    unnamed x120 -> x126, local copies, waits for them, and re-layouts: 21.1 us -> 22 us
  transfers between devices with their start and end apart: 5 -> 5, of which waited for: 3 -> 3; matrix products, arithmetic and copies ran while one was open for 15% -> 15% of each run, Pallas kernels for 21% -> 22%
where the time goes in v7:
time: 802 us; the launch traced here: 795 us
  Pallas kernels  504 us (63%)
  matrix products  112 us (14%)
  other arithmetic  54.9 us (7%)
  local copies, waits for them, and re-layouts  33.7 us (4%)
  waiting for transfers between devices  30 us (4%)
  blocking collectives  29.8 us (4%)
  between operations  20.8 us (3%)
  starting transfers between devices  9.8 us (1%)
    pallas_call x7, Pallas kernels, move(): pl.pallas_call(kernel, out_shape=tuple(outs), in_specs=[IN_VMEM if i < in...  453 us
    dot_general x6, matrix products, mul_left_t(): lax.dot_general(left, right, (((0,), (0,)), ((), ())), preferred_element_...  41.5 us
    dot_general x6, matrix products, mul_plain(): return jnp.dot(left, right, preferred_element_type=jnp.float32)  39.3 us
    dot_general x7, matrix products, mul_right_t(): lax.dot_general(left, right, (((1,), (1,)), ((), ())), preferred_element_...  30.8 us
    all_to_all x1, blocking collectives, exchange(): return lax.all_to_all(packed, 'dp', split_axis=0, concat_axis=0, tiled=True)  29.8 us
    unnamed x126, local copies, waits for them, and re-layouts  22 us
    all_gather x1, waiting for transfers between devices, local(): grad_rows = lax.all_gather(back, 'tensor', axis=1, tiled=True)  21.2 us
    pallas_call x1, Pallas kernels, sum_all(): pl.pallas_call(functools.partial(sum_all_kernel, n_dp, n), out_shape=jax....  20.5 us
  transfers between devices with their start and end apart: 5, of which 3 were waited for; matrix products, arithmetic and copies ran while one was open for 15% of the time, Pallas kernels for 22%

profile of v7, /device:TPU:0, one launch (start us, length us, event | category | flops | bytes accessed | tf_op | source)
XLA Modules:
  0.0 794.8 jit_solution(259557970769131886)
XLA Ops:
  11.9 6.1 fusion.19
  18.0 5.3 all-to-all-start
  24.6 43.9 %gather_lines.1 = (bf16[256,2048]{1,0:T(8,128)(2,1)}, bf16[256,2048]{1,0:T(8,128)(2,1)}, bf16[256,256]{1,0:T(8,128)(2,1)}) custom-call(f32[256,512]{1,0:T(8,128)} %a.1, f32[512,256]{1,0:T(8,128)} %b.1, f32[64,256]{1,0:T(8,128)} %c), custom_call_target="tpu_custom_call" | custom-call | tf_op jit(solution)/shard_map/gather_lines/pallas_call | solution.py:834
  69.3 3.3 all-to-all-done
  72.6 8.1 %fusion.47.x.y = bf16[1024,1024]{1,0:T(8,128)(2,1)} fusion(bf16[2048,1024]{1,0:T(8,128)(2,1)} %bitcast.3, s32[2048]{0:T(1024)S(1)} %bitcast.93), kind=kOutput, calls=%fused_computation.85 | convolution fusion | flops 4298113024 | bytes 6299648 | tf_op jit(solution)/shard_map/dot_general | solution.py:44
  80.6 59.1 %rows_and_weights.1 = (bf16[256,2048]{1,0:T(8,128)(2,1)}, bf16[1024,2048]{1,0:T(8,128)(2,1)}, bf16[2048,2048]{1,0:T(8,128)(2,1)}, bf16[2048,256]{1,0:T(8,128)(2,1)}) custom-call(bf16[1024,1024]{1,0:T(8,128)(2,1)} %fusion.47.x.y, bf16[256,2048]{1,0:T(8,128)(2,1)} %get-tuple-element.71.a, bf16[256,256]{1,0:T(8,128)(2,1)} %get-tuple-element.72.b), custom_call_target="tpu_custom_call" | custom-call | tf_op jit(solution)/shard_map/rows_and_weights/pallas_call | solution.py:834
  144.7 47.2 %shared_and_project.1 = (bf16[256,2048]{1,0:T(8,128)(2,1)}, bf16[1024,256]{1,0:T(8,128)(2,1)}, bf16[2048,2048]{1,0:T(8,128)(2,1)}, bf16[1024,2048]{1,0:T(8,128)(2,1)}) custom-call(bf16[1024,1024]{1,0:T(8,128)(2,1)} %fusion.47.x.y, bf16[256,256]{1,0:T(8,128)(2,1)} %fusion.63.x, ...), custom_call_target="tpu_custom_call", output_to_operand_aliasing={{3}: (6, {})} | custom-call | tf_op jit(solution)/shard_map/shared_and_project/pallas_call | solution.py:834
  194.3 13.1 %attend.1 = (bf16[256,2048]{1,0:T(8,128)(2,1)S(1)}, f32[256,2048]{1,0:T(8,128)S(1)}) custom-call(bf16[256,2048]{1,0:T(8,128)(2,1)S(1)} %copy-done, bf16[768,128]{1,0:T(8,128)(2,1)S(1)} %get-tuple-element.213.k, bf16[768,128]{1,0:T(8,128)(2,1)S(1)} %get-tuple-element.212.v, s32[256,1]{1,0:T(8,128)S(1)} %copy.68.seg_row, ...), custom_call_target="tpu_custom_call" | custom-call | tf_op jit(solution)/shard_map/attend/pallas_call | solution.py:1277
  207.5 6.3 fusion.108
  215.6 83.9 %rows_and_expanded.1 = (f32[1024,2048]{1,0:T(8,128)}, bf16[1024,2048]{1,0:T(8,128)(2,1)}, bf16[2048,2048]{1,0:T(8,128)(2,1)}, bf16[2048,2048]{1,0:T(8,128)(2,1)}) custom-call(bf16[256,2048]{1,0:T(8,128)(2,1)} %add_convert_fusion.1.x_ref, f32[256,2048]{1,0:T(8,128)} %a.2, f32[2048,256]{1,0:T(8,128)} %b.2, f32[1,2048]{1,0:T(1,128)} %bitcast.88), custom_call_target="tpu_custom_call" | custom-call | tf_op jit(solution)/shard_map/rows_and_expanded/pallas_call | solution.py:834
  299.5 5.0 multiply_convert_fusion
  305.3 2.4 fusion.48
  307.7 2.4 fusion.54
  310.0 2.4 fusion.51
  312.4 2.4 fusion.57
  315.2 2.2 pad_maximum_fusion
  317.4 18.5 %convert_reduce_fusion = (f32[2048]{0:T(1024)S(1)}, bf16[1024,2048]{1,0:T(8,128)(2,1)S(1)}) fusion(f32[1024,2048]{1,0:T(8,128)} %get-tuple-element.82, bf16[1024,2048]{1,0:T(8,128)(2,1)} %get-tuple-element.85, bf16[2048,2048]{1,0:T(8,128)(2,1)} %get-tuple-element.83), kind=kOutput, calls=%fused_computation.10 | convolution fusion | flops 8636069888 | bytes 25174016 | tf_op jit(solution)/shard_map/dot_general | solution.py:34
  335.9 12.8 %convolution_convert_fusion.2.x_ref = bf16[1024,2048]{1,0:T(8,128)(2,1)} fusion(bf16[1024,2048]{1,0:T(8,128)(2,1)S(1)} %get-tuple-element.201, bf16[2048,2048]{1,0:T(8,128)(2,1)} %get-tuple-element.86), kind=kOutput, calls=%fused_computation.29 | convolution fusion | flops 8592031744 | bytes 16777216 | tf_op jit(solution)/shard_map/dot_general | solution.py:38
  348.7 11.4 %convolution_convert_fusion.b = bf16[2048,2048]{1,0:T(8,128)(2,1)} fusion(bf16[1024,2048]{1,0:T(8,128)(2,1)S(1)} %copy-done.15, bf16[1024,2048]{1,0:T(8,128)(2,1)S(1)} %copy-done.20), kind=kOutput, calls=%fused_computation.20 | convolution fusion | flops 8594128896 | bytes 16777216 | tf_op jit(solution)/shard_map/dot_general | solution.py:44
  360.1 11.4 %convolution_convert_fusion.1.a = bf16[2048,2048]{1,0:T(8,128)(2,1)} fusion(bf16[1024,2048]{1,0:T(8,128)(2,1)S(1)} %copy-done.55, bf16[1024,2048]{1,0:T(8,128)(2,1)S(1)} %get-tuple-element.201), kind=kOutput, calls=%fused_computation.21 | convolution fusion | flops 8594128896 | bytes 16777216 | tf_op jit(solution)/shard_map/dot_general | solution.py:44
  371.5 91.2 %scatter_expanded.1 = (f32[256,2048]{1,0:T(8,128)}, f32[256,2048]{1,0:T(8,128)}, f32[256,2048]{1,0:T(8,128)}) custom-call(bf16[1024,2048]{1,0:T(8,128)(2,1)} %convolution_convert_fusion.2.x_ref, bf16[2048,2048]{1,0:T(8,128)(2,1)} %convolution_convert_fusion.1.a, bf16[2048,2048]{1,0:T(8,128)(2,1)} %convolution_convert_fusion.b), custom_call_target="tpu_custom_call" | custom-call | tf_op jit(solution)/shard_map/scatter_expanded/pallas_call | solution.py:834
  462.7 2.3 multiply_reduce_fusion.2
  465.0 4.8 fusion.24
  469.8 4.4 all-to-all-start.1
  474.3 2.8 fusion.103
  477.1 2.4 convert_reduce_fusion.3
  479.6 6.1 convolution_convert_fusion.4.do
  485.7 17.5 %attend_back.1 = (bf16[256,2048]{1,0:T(8,128)(2,1)S(1)}, bf16[1024,256]{1,0:T(8,128)(2,1)S(1)}) custom-call(bf16[256,2048]{1,0:T(8,128)(2,1)S(1)} %copy-done.1, bf16[256,2048]{1,0:T(8,128)(2,1)S(1)} %convolution_convert_fusion.4.do, f32[256,2048]{1,0:T(8,128)S(1)} %get-tuple-element.89.log_total, bf16[768,128]{1,0:T(8,128)(2,1)S(1)} %get-tuple-element.213.k, ...), custom_call_target="tpu_custom_call" | custom-call | tf_op jit(solution)/shard_map/attend_back/pallas_call | solution.py:1296
  505.1 5.4 fusion.60.y
  510.4 96.5 %scatter_shared.1 = (f32[256,256]{1,0:T(8,128)}, bf16[4,512,512]{2,1,0:T(8,128)(2,1)}, f32[256,2048]{1,0:T(8,128)}, bf16[1024,2048]{1,0:T(8,128)(2,1)}) custom-call(bf16[1024,256]{1,0:T(8,128)(2,1)} %copy-done.5, bf16[1024,512]{1,0:T(8,128)(2,1)} %fusion.60.y, bf16[256,2048]{1,0:T(8,128)(2,1)} %copy-done.13, bf16[256,2048]{1,0:T(8,128)(2,1)} %copy-done.2, ...), custom_call_target="tpu_custom_call" | custom-call | tf_op jit(solution)/shard_map/scatter_shared/pallas_call | solution.py:834
  609.6 2.4 fusion.92
  613.6 3.3 convert_reduce_fusion.2
  616.9 31.3 %cols_and_shared.1 = (f32[64,256]{1,0:T(8,128)}, bf16[1024,512]{1,0:T(8,128)(2,1)}) custom-call(bf16[256,2048]{1,0:T(8,128)(2,1)} %get-tuple-element.207.x, bf16[2048,256]{1,0:T(8,128)(2,1)} %convolution_convert_fusion.3.c), custom_call_target="tpu_custom_call" | custom-call | tf_op jit(solution)/shard_map/cols_and_shared/pallas_call | solution.py:834
  648.2 2.4 copy.81
  651.8 2.6 fusion.25
  654.4 29.8 %all_to_all.15 = bf16[8,256,512]{2,1,0:T(8,128)(2,1)S(1)} all-to-all(bf16[8,256,512]{2,1,0:T(8,128)(2,1)S(1)} %bitcast.84), channel_id=1, replica_groups=mesh['dp'=8,'tensor'=4] {'dp'}, dimensions={0} | all-to-all | bytes 4194304 | tf_op jit(solution)/shard_map/all_to_all | solution.py:1457
  684.1 3.8 fusion.61
  687.9 5.4 reduce-scatter.5.cloned.1.call-done
  698.9 2.9 multiply_reduce_fusion.1
  710.6 20.5 %sum_all.1 = f32[192,128]{1,0:T(8,128)} custom-call(f32[192,128]{1,0:T(8,128)} %bitcast.87), custom_call_target="tpu_custom_call" | custom-call | tf_op jit(solution)/shard_map/sum_all/pallas_call | solution.py:1394
  735.2 2.6 multiply_subtract_fusion.3
  737.8 2.1 copy.78
  739.9 2.0 copy.79
  744.8 2.8 multiply_subtract_fusion.2
  748.4 6.4 multiply_subtract_fusion.1
  754.8 3.7 multiply_subtract_fusion
  758.5 21.2 %all-gather.2.cloned.1.call-done = bf16[1024,2048]{1,0:T(8,128)(2,1)} async-done(((bf16[1024,512]{1,0:T(8,128)(2,1)}), bf16[1024,2048]{1,0:T(8,128)(2,1)}) %all-gather.2.cloned.1.call-update) | async-done | bytes 4194320 | tf_op jit(solution)/shard_map/all_gather | solution.py:1596
  779.8 4.9 copy.92
  (193 shorter events, 43.5 us)
Async XLA Ops:
  18.0 5.4 copy-start.43
  18.0 5.7 copy-start.57
  18.0 6.6 slice-start
  18.0 50.6 %copy-start.35 = (f32[22656]{0:T(1024)S(1)}, f32[22656]{0:T(1024)}, u32[]{:S(2)}) copy-start(f32[22656]{0:T(1024)} %param.41) | copy-start | bytes 271876
  18.0 54.5 %all-to-all-start = ((bf16[8,256,1024]{2,1,0:T(8,128)(2,1)}), bf16[8,256,1024]{2,1,0:T(8,128)(2,1)}, u32[]{:S(2)}, u32[]{:S(2)}) async-start(bf16[8,256,1024]{2,1,0:T(8,128)(2,1)} %bitcast.81), calls=%async_computation | async-start | bytes 8388608 | tf_op jit(solution)/shard_map/all_to_all | solution.py:1457
  23.4 441.6 %reduce-scatter.3.cloned.1.call-start = ((), (), s32[]{:S(2)}) async-start(), calls=%async_computation.5 | async-start | bytes 5242880 | tf_op jit(solution)/shard_map/reduce_scatter | solution.py:1545
  69.3 73.8 %copy-start.39 = (f32[2048]{0:T(1024)}, f32[2048]{0:T(1024)S(1)}, u32[]{:S(2)}) copy-start(f32[2048]{0:T(1024)S(1)} %get-tuple-element.224) | copy-start | bytes 24580
  139.8 3.3 copy-start.8
  139.8 3.8 copy-start.30
  141.4 3.3 copy-start.46
  207.5 6.3 copy-start.4
  213.8 101.0 %copy-start.6 = (f32[256,2048]{1,0:T(8,128)}, f32[256,2048]{1,0:T(8,128)S(1)}, u32[]{:S(2)}) copy-start(f32[256,2048]{1,0:T(8,128)S(1)} %get-tuple-element.228) | copy-start | bytes 6291460
  299.5 5.8 copy-start.54
  304.5 8.0 %copy-start.19 = (bf16[1024,2048]{1,0:T(8,128)(2,1)}, bf16[1024,2048]{1,0:T(8,128)(2,1)S(1)}, u32[]{:S(2)}) copy-start(bf16[1024,2048]{1,0:T(8,128)(2,1)S(1)} %multiply_convert_fusion) | copy-start | bytes 12582916
  335.9 12.8 %copy-start.15 = (bf16[1024,2048]{1,0:T(8,128)(2,1)S(1)}, bf16[1024,2048]{1,0:T(8,128)(2,1)}, u32[]{:S(2)}) copy-start(bf16[1024,2048]{1,0:T(8,128)(2,1)} %get-tuple-element.85) | copy-start | bytes 12582916
  335.9 12.8 %copy-start.20 = (bf16[1024,2048]{1,0:T(8,128)(2,1)S(1)}, bf16[1024,2048]{1,0:T(8,128)(2,1)}, u32[]{:S(2)}) copy-start(bf16[1024,2048]{1,0:T(8,128)(2,1)} %copy-done.19) | copy-start | bytes 12582916
  348.7 11.4 %copy-start.55 = (bf16[1024,2048]{1,0:T(8,128)(2,1)S(1)}, bf16[1024,2048]{1,0:T(8,128)(2,1)}, u32[]{:S(2)}) copy-start(bf16[1024,2048]{1,0:T(8,128)(2,1)} %get-tuple-element.87) | copy-start | bytes 12582916
  371.5 91.2 %copy-start.7 = (f32[256,2048]{1,0:T(8,128)S(1)}, f32[256,2048]{1,0:T(8,128)}, u32[]{:S(2)}) copy-start(f32[256,2048]{1,0:T(8,128)} %copy-done.6) | copy-start | bytes 6291460
  469.8 35.2 %all-to-all-start.1 = ((bf16[8,256,512]{2,1,0:T(8,128)(2,1)}), bf16[8,256,512]{2,1,0:T(8,128)(2,1)}, u32[]{:S(2)}, u32[]{:S(2)}) async-start(bf16[8,256,512]{2,1,0:T(8,128)(2,1)} %bitcast.83), calls=%async_computation.2 | async-start | bytes 4194304 | tf_op jit(solution)/shard_map/all_to_all | solution.py:1457
  474.2 219.2 %reduce-scatter.5.cloned.1.call-start = ((), (), s32[]{:S(2)}) async-start(), calls=%async_computation.6 | async-start | bytes 2621440 | tf_op jit(solution)/shard_map/reduce_scatter | solution.py:1591
  479.6 6.2 copy-start.21
  479.6 6.2 copy-start.1
  485.7 19.3 %copy-start.53 = (s32[1,2,8,128]{3,1,2,0:T(2,128)S(1)}, s32[1,2,8,128]{3,1,2,0:T(2,128)}, u32[]{:S(2)}) copy-start(s32[1,2,8,128]{3,1,2,0:T(2,128)} %copy-done.52) | copy-start | bytes 24580
  510.4 97.7 %copy-start.14 = (bf16[256,2048]{1,0:T(8,128)(2,1)S(1)}, bf16[256,2048]{1,0:T(8,128)(2,1)}, u32[]{:S(2)}) copy-start(bf16[256,2048]{1,0:T(8,128)(2,1)} %copy-done.13) | copy-start | bytes 3145732
  606.9 2.6 copy-start.9
  607.0 2.6 copy-start.31
  616.9 31.3 %copy-start.24 = (bf16[4,512,512]{2,1,0:T(8,128)(2,1)S(1)}, bf16[4,512,512]{2,1,0:T(8,128)(2,1)}, u32[]{:S(2)}) copy-start(bf16[4,512,512]{2,1,0:T(8,128)(2,1)} %get-tuple-element.99) | copy-start | bytes 6291460
  650.6 129.2 %all-gather.2.cloned.1.call-start = ((), (), s32[]{:S(2)}) async-start(), calls=%async_computation.7 | async-start | bytes 5242880 | tf_op jit(solution)/shard_map/all_gather | solution.py:1596
  684.1 9.3 %copy-start.25 = (f32[256,512]{1,0:T(8,128)S(1)}, f32[256,512]{1,0:T(8,128)}, u32[]{:S(2)}) copy-start(f32[256,512]{1,0:T(8,128)} %a.1) | copy-start | bytes 1572868
  687.9 6.5 copy-start.33
  687.9 7.5 copy-start.34
  698.9 4.0 copy-start.38
  698.9 4.7 copy-start.12
  703.6 31.5 %copy-start.27 = (f32[256,512]{0,1:T(8,128)S(1)}, f32[256,512]{0,1:T(8,128)}, u32[]{:S(2)}) copy-start(f32[256,512]{0,1:T(8,128)} %copy.77) | copy-start | bytes 1572868
  737.8 6.2 copy-start.37
  737.8 6.2 copy-start.44
  737.8 6.2 copy-start.45
  737.8 7.0 copy-start.26
  744.0 3.5 copy-start.32
  744.0 3.5 copy-start.36
  744.0 3.5 copy-start.41
  744.0 3.5 copy-start.42
  744.1 4.3 copy-start.18
  744.8 3.6 copy-start.16
  748.3 6.5 copy-start.17
  748.3 6.5 copy-start.28
  748.3 6.5 copy-start.29
  779.8 4.9 copy-start.22
  (16 other events, 28.3 us)
Sparse Core Ops, SparseCore 0:
  317.5 88.9 reduce-scatter.2
  650.7 42.6 reduce-scatter.4
  695.5 84.1 all-gather.1
